TPU v7x, 128 devices: a whole 4x4x4 slice. The times are simulated.
128 devices in a mesh: side: 2 (over core), dev: 64 (over x, y, z).
Axes of the slice: x: 4, y: 4, z: 4, core: 2. Of those that a mesh axis runs over, the one named last changes fastest.
Arguments:
- query: bfloat16 [128, 6144], P('dev'), may hold values from -120 to 120
- new_key: bfloat16 [128, 1024], P('dev'), may hold values from -4 to 4
- new_value: bfloat16 [128, 1024], P('dev'), may hold values from -4 to 4
- key_cache: bfloat16 [128, 128, 1024], P('dev'), may hold values from -4 to 4
- value_cache: bfloat16 [128, 128, 1024], P('dev'), may hold values from -4 to 4
- cached: int32 [128], P('dev'), may hold values from 2 to 128, as said below
- residual: bfloat16 [128, 6144], P('dev'), may hold values from -36 to 36
- out_weight: bfloat16 [6144, 6144], P(None, 'dev'), may hold values from -0.078125 to 0.078125
- norm_gain: bfloat16 [6144], replicated, may hold values from 0.25 to 1.75
- expert_ids: int32 [128, 2], P('dev'), may hold values from 0 to 3, all different within a row; in each aligned block of 2 rows (0 to 1, 2 to 3, ...) at most 2 rows name the same one
- gate_weights: float32 [128, 2], P('dev'), may hold values from 0.1 to 0.9
- w_gate: bfloat16 [6144, 32768], P(None, 'dev'), may hold values from -0.078125 to 0.078125
- w_up: bfloat16 [6144, 32768], P(None, 'dev'), may hold values from -0.078125 to 0.078125
- w_down: bfloat16 [32768, 6144], P('dev'), may hold values from -0.0625 to 0.0625
Outputs:
- mixed: bfloat16 [128, 6144], P('dev', 'side')
Inputs may be any that keep to these rules, and one draw needn't show every extreme that they name: `expert_ids`: each row names 2 different experts; in each aligned block of 2 rows (the rows of one device) no expert is named by more than 2 rows, a bound that some block reaches. `cached`: some sequence uses all 128 positions.
All inputs are finite; a program needn't handle non-finite values.
Results may differ from a plain program's by a relative error of at most 0.012.
Values may be sent and summed in bfloat16 or wider, within the bound.
No kernel may reach another device: no remote copies, remote signals or barrier semaphores. Data moves between devices by JAX's collectives and lax.ppermute only.
A program may use at most 128 MiB of HBM per device.

v0:
```python
import math

import jax
import jax.numpy as jnp
from jax import lax
from jax.sharding import PartitionSpec as P

D = 6144
HEADS = 48
KV_HEADS = 8
HEAD_DIM = 128
EXPERTS = 4
TOP = 2
CACHE_LEN = 128
CAP = 2


epsilon = 1e-05


def shifted(value, axis, steps):
    count = lax.axis_size(axis)
    leading, last = (max(0, -steps), min(count, count - steps))
    return lax.ppermute(value, axis, [(source, source + steps) for source in range(leading, last)])


def attend(query, new_key, new_value, key_cache, value_cache, cached):
    seq_count = query.shape[0]
    group_size = HEADS // KV_HEADS
    score_scale = 1.0 / math.sqrt(HEAD_DIM)
    queries = query.reshape(seq_count, KV_HEADS, group_size, HEAD_DIM)
    cache_keys = key_cache.reshape(seq_count, CACHE_LEN, KV_HEADS, HEAD_DIM)
    cache_values = value_cache.reshape(seq_count, CACHE_LEN, KV_HEADS, HEAD_DIM)
    scores = (
        jnp.einsum("bgrd,blgd->bgrl", queries, cache_keys, preferred_element_type=jnp.float32)
        * score_scale
    )
    own_score = (
        jnp.einsum(
            "bgrd,bgd->bgr",
            queries,
            new_key.reshape(seq_count, KV_HEADS, HEAD_DIM),
            preferred_element_type=jnp.float32,
        )
        * score_scale
    )
    visible = jnp.arange(CACHE_LEN)[None, :] < cached[:, None]
    scores = jnp.where(visible[:, None, None, :], scores, -jnp.inf)
    highest = jnp.maximum(jnp.max(scores, axis=3), own_score)
    exponents = jnp.exp(scores - highest[..., None])
    own_exp = jnp.exp(own_score - highest)
    denominator = jnp.sum(exponents, axis=3) + own_exp
    weights = (exponents / denominator[..., None]).astype(jnp.bfloat16)
    own_weight = (own_exp / denominator).astype(jnp.bfloat16)
    context = jnp.einsum(
        "bgrl,blgd->bgrd", weights, cache_values, preferred_element_type=jnp.float32
    )
    context = context + own_weight.astype(jnp.float32)[..., None] * new_value.reshape(
        seq_count, KV_HEADS, 1, HEAD_DIM
    ).astype(jnp.float32)
    return context.reshape(seq_count, HEADS * HEAD_DIM).astype(jnp.bfloat16)


def skip_attend(query, new_key, new_value, key_cache, value_cache, cached):
    return jnp.zeros_like(query)


def normalize(hidden, norm_gain):
    widened = hidden.astype(jnp.float32)
    factor = lax.rsqrt(jnp.mean(widened * widened, axis=1, keepdims=True) + epsilon)
    return (widened * factor * norm_gain.astype(jnp.float32)[None, :]).astype(jnp.bfloat16)


def expert_block(expert_rows, w_gate, w_up, w_down):
    gate_part = jnp.dot(expert_rows, w_gate, preferred_element_type=jnp.float32)
    up_part = jnp.dot(expert_rows, w_up, preferred_element_type=jnp.float32)
    act = (jax.nn.silu(gate_part) * up_part).astype(jnp.bfloat16)
    return jnp.dot(act, w_down, preferred_element_type=jnp.float32).astype(jnp.bfloat16)


def skip_block(expert_rows, w_gate, w_up, w_down):
    return jnp.zeros((expert_rows.shape[0], w_down.shape[1]), jnp.bfloat16)


def slot_table(expert_ids):
    picked = expert_ids.reshape(-1)
    onehot = (picked[:, None] == jnp.arange(EXPERTS)[None, :]).astype(jnp.int32)
    slot_rank = jnp.sum((jnp.cumsum(onehot, axis=0) - onehot) * onehot, axis=1)
    target = picked * CAP + slot_rank
    table = target[None, :] == jnp.arange(EXPERTS * CAP)[:, None]
    return table.reshape(EXPERTS * CAP, expert_ids.shape[0], TOP)


def send_slots(normed, table, group_size):
    placing = jnp.any(table, axis=2).astype(jnp.bfloat16)
    slots = jnp.dot(placing, normed, preferred_element_type=jnp.float32).astype(jnp.bfloat16)
    width = slots.shape[1]
    slots = slots.reshape(EXPERTS, 1, CAP, width)
    return jnp.broadcast_to(slots, (EXPERTS, group_size, CAP, width)).reshape(
        EXPERTS * group_size, CAP, width
    )


def combine(table, gate_weights, returned):
    mix_table = jnp.sum(table.astype(jnp.float32) * gate_weights[None, :, :], axis=2)
    return jnp.dot(
        mix_table.T, returned, precision=lax.Precision.HIGHEST, preferred_element_type=jnp.float32
    )


def local(
    query,
    new_key,
    new_value,
    key_cache,
    value_cache,
    cached,
    residual,
    out_weight,
    norm_gain,
    expert_ids,
    gate_weights,
    w_gate,
    w_up,
    w_down,
):
    role_index = lax.axis_index("side")
    devices = lax.axis_size("dev")
    group_size = devices // EXPERTS
    half_width = D // 2
    attention = lax.cond(
        role_index == 0,
        attend,
        skip_attend,
        query,
        new_key,
        new_value,
        key_cache,
        value_cache,
        cached,
    )
    columns = jnp.dot(
        lax.all_gather(attention, "dev", axis=0, tiled=True),
        out_weight,
        preferred_element_type=jnp.float32,
    )
    projected = lax.all_to_all(
        columns.astype(jnp.bfloat16), "dev", split_axis=0, concat_axis=1, tiled=True
    ).astype(columns.dtype)
    hidden = (residual.astype(jnp.float32) + projected).astype(jnp.bfloat16)
    table = slot_table(expert_ids)
    upper_rows = shifted(hidden[:, half_width:], "side", 1)
    outgoing = send_slots(normalize(hidden, norm_gain), table, group_size)
    padded_rows = jnp.concatenate([jnp.zeros_like(outgoing), outgoing], axis=0)
    received = lax.all_to_all(padded_rows, ("side", "dev"), split_axis=0, concat_axis=0, tiled=True)
    expert_rows = received[:devices].reshape(devices * CAP, D)
    partial_value = lax.cond(
        role_index == 1, expert_block, skip_block, expert_rows, w_gate, w_up, w_down
    )
    halves = (
        partial_value.reshape(devices, CAP, 2, half_width)
        .transpose(2, 0, 1, 3)
        .reshape(2 * devices, CAP, half_width)
    )
    returned_rows = lax.all_to_all(halves, ("side", "dev"), split_axis=0, concat_axis=0, tiled=True)
    summed = jnp.sum(
        returned_rows[devices:].reshape(EXPERTS, group_size, CAP, half_width).astype(jnp.float32),
        axis=1,
    )
    expert_sum = combine(table, gate_weights, summed.reshape(EXPERTS * CAP, half_width))
    own_half = jnp.where(role_index == 0, hidden[:, :half_width], upper_rows)
    mixed = own_half.astype(jnp.float32) + expert_sum
    return mixed.astype(jnp.bfloat16)


def solution(mesh):
    in_specs = (
        P("dev", None),
        P("dev", None),
        P("dev", None),
        P("dev", None, None),
        P("dev", None, None),
        P("dev"),
        P("dev", None),
        P(None, "dev"),
        P(),
        P("dev", None),
        P("dev", None),
        P(None, "dev"),
        P(None, "dev"),
        P("dev", None),
    )
    out_specs = P("dev", "side")
    return jax.shard_map(local, mesh=mesh, in_specs=in_specs, out_specs=out_specs, check_vma=False)
```

profile of v0, /device:TPU:1, one launch (start us, length us, event | category | flops | bytes accessed | tf_op | source)
XLA Modules:
  0.0 219.5 jit_solution(17281379304689095894)
XLA Ops:
  6.5 0.0 copy-start
  6.5 0.0 copy-start.4
  6.5 0.0 all-gather.3.cloned.1.call-start
  6.6 0.0 copy-start.1
  6.6 0.6 copy-done.1
  7.2 0.1 all-gather.3.cloned.1.call-update
  7.3 0.1 copy-done.4
  7.3 0.1 eq.37
  7.4 0.1 fusion.25
  7.5 0.2 select_reduce_fusion.1
  7.7 0.1 reduce_sum.48
  7.8 72.2 %all-gather.3.cloned.1.call-done = bf16[64,2,6144]{2,1,0:T(2,128)(2,1)} async-done(((bf16[1,2,6144]{2,1,0:T(2,128)(2,1)}), bf16[64,2,6144]{2,1,0:T(2,128)(2,1)}) %all-gather.3.cloned.1.call-update) | async-done | bytes 1572880 | tf_op jit(solution)/shard_map/all_gather | solution.py:143
  80.0 3.6 %reshape.107 = bf16[128,6144]{1,0:T(8,128)(2,1)S(1)} reshape(bf16[64,2,6144]{2,1,0:T(2,128)(2,1)} %all-gather.3.cloned.1.call-done) | data formatting | bytes 3145728
  83.6 0.0 copy-done
  83.6 0.0 copy-start.3
  83.6 0.0 copy-start.2
  83.6 0.6 convolution_convert_fusion.2
  84.2 0.7 copy.53
  85.0 6.4 %all-to-all-start = ((bf16[64,2,96]{2,1,0:T(2,128)(2,1)}), bf16[64,2,96]{2,1,0:T(2,128)(2,1)S(1)}, u32[]{:S(2)}, u32[]{:S(2)}) async-start(bf16[64,2,96]{2,1,0:T(2,128)(2,1)} %bitcast.3), calls=%async_computation | async-start | bytes 65536 | tf_op jit(solution)/shard_map/all_to_all | solution.py:147
  91.4 0.1 fusion.24
  91.5 0.0 copy-done.3
  91.5 8.3 %all-to-all-done = bf16[64,2,96]{2,1,0:T(2,128)(2,1)S(1)} async-done(((bf16[64,2,96]{2,1,0:T(2,128)(2,1)}), bf16[64,2,96]{2,1,0:T(2,128)(2,1)S(1)}, u32[]{:S(2)}, u32[]{:S(2)}) %all-to-all-start) | async-done | bytes 24608 | tf_op jit(solution)/shard_map/all_to_all | solution.py:147
  99.8 0.1 reshape.104
  100.0 0.0 copy-done.2
  100.0 0.2 fusion.19
  100.1 0.2 convolution_convert_fusion.1
  100.4 0.1 broadcast_in_dim.22
  100.5 0.9 broadcast_in_dim.23
  101.4 3.7 %concatenate.3 = bf16[128,2,6144]{2,1,0:T(2,128)(2,1)} pad(bf16[64,2,6144]{2,1,0:T(2,128)(2,1)S(1)} %bitcast.46, bf16[]{:T(256)} %constant.41.clone.1), padding=64_0x0_0x0_0 | pad | bytes 4718594 | tf_op jit(solution)/shard_map/concatenate | solution.py:154
  105.1 7.7 %all-to-all-start.1 = ((bf16[128,2,6144]{2,1,0:T(2,128)(2,1)}), bf16[128,2,6144]{2,1,0:T(2,128)(2,1)}, u32[]{:S(2)}, u32[]{:S(2)}) async-start(bf16[128,2,6144]{2,1,0:T(2,128)(2,1)} %concatenate.3), calls=%async_computation.1 | async-start | bytes 6291456 | tf_op jit(solution)/shard_map/all_to_all | solution.py:155
  112.8 40.1 %all-to-all-done.1 = bf16[128,2,6144]{2,1,0:T(2,128)(2,1)} async-done(((bf16[128,2,6144]{2,1,0:T(2,128)(2,1)}), bf16[128,2,6144]{2,1,0:T(2,128)(2,1)}, u32[]{:S(2)}, u32[]{:S(2)}) %all-to-all-start.1) | async-done | bytes 3145760 | tf_op jit(solution)/shard_map/all_to_all | solution.py:155
  152.9 18.7 %conditional.3 = (bf16[128,6144]{1,0:T(8,128)(2,1)}) conditional(s32[]{:T(128)} %convert_element_type.94, () %tuple.19, (bf16[128,2,6144]{2,1,0:T(2,128)(2,1)}, bf16[6144,512]{1,0:T(8,128)(2,1)}, bf16[6144,512]{1,0:T(8,128)(2,1)}, bf16[512,6144]{1,0:T(8,128)(2,1)}) %tuple.20), branch_computations={%region_9.10_spmd, %region_10.11_spmd} | conditional | flops 2417098752 | bytes 30408712 | solution.py:157
  152.9 3.6 %slice.9 = bf16[64,2,6144]{2,1,0:T(2,128)(2,1)} slice(bf16[128,2,6144]{2,1,0:T(2,128)(2,1)} %get-tuple-element.39), slice={[0:64], [0:2], [0:6144]} | slice | bytes 3145728 | tf_op jit(solution)/shard_map/slice | solution.py:156
  156.5 3.6 %reshape.94 = bf16[128,6144]{1,0:T(8,128)(2,1)S(1)} reshape(bf16[64,2,6144]{2,1,0:T(2,128)(2,1)} %slice.9) | data formatting | bytes 3145728 | tf_op jit(solution)/shard_map/reshape | solution.py:156
  160.1 3.8 %fusion.27 = f32[128,512]{1,0:T(8,128)S(1)} fusion(bf16[128,6144]{1,0:T(8,128)(2,1)S(1)} %reshape.94, bf16[6144,512]{1,0:T(8,128)(2,1)} %get-tuple-element.58), kind=kOutput, calls=%fused_computation.53 | convolution fusion | flops 805306368 | bytes 8126464 | tf_op jit(solution)/shard_map/cond/branch_1_fun/dot_general | solution.py:75
  163.9 7.7 %convolution_convert_fusion = bf16[128,6144]{1,0:T(8,128)(2,1)} fusion(bf16[512,6144]{1,0:T(8,128)(2,1)} %get-tuple-element.60, bf16[128,6144]{1,0:T(8,128)(2,1)S(1)} %reshape.94, bf16[6144,512]{1,0:T(8,128)(2,1)} %get-tuple-element.59, f32[128,512]{1,0:T(8,128)S(1)} %fusion.27), kind=kOutput, calls=%fused_computation.21 | convolution fusion | flops 1611792384 | bytes 15990784 | tf_op jit(solution)/shard_map/cond/branch_1_fun/dot_general | solution.py:78
  171.6 4.1 %reshape.100 = bf16[64,2,2,3072]{3,2,1,0:T(2,128)(2,1)S(1)} reshape(bf16[128,6144]{1,0:T(8,128)(2,1)} %get-tuple-element.68) | data formatting | bytes 3145728 | tf_op jit(solution)/shard_map/reshape | solution.py:161
  175.6 0.5 copy.55
  176.1 2.8 %copy.56 = bf16[128,2,3072]{2,1,0:T(2,128)(2,1)} copy(bf16[128,2,3072]{2,0,1:T(8,128)(2,1)S(1)} %bitcast.48) | data formatting | bytes 3145728 | tf_op jit(solution)/shard_map/reshape | solution.py:163
  178.9 0.0 copy-start.5
  178.9 9.3 %all-to-all-start.2 = ((bf16[128,2,3072]{2,1,0:T(2,128)(2,1)}), bf16[128,2,3072]{2,1,0:T(2,128)(2,1)S(1)}, u32[]{:S(2)}, u32[]{:S(2)}) async-start(bf16[128,2,3072]{2,1,0:T(2,128)(2,1)} %copy.56), calls=%async_computation.2 | async-start | bytes 3145728 | tf_op jit(solution)/shard_map/all_to_all | solution.py:165
  188.2 0.0 copy-done.5
  188.2 0.1 select_reduce_fusion
  188.3 1.3 collective-permute-start
  189.6 21.5 %all-to-all-done.2 = bf16[128,2,3072]{2,1,0:T(2,128)(2,1)S(1)} async-done(((bf16[128,2,3072]{2,1,0:T(2,128)(2,1)}), bf16[128,2,3072]{2,1,0:T(2,128)(2,1)S(1)}, u32[]{:S(2)}, u32[]{:S(2)}) %all-to-all-start.2) | async-done | bytes 1572896 | tf_op jit(solution)/shard_map/all_to_all | solution.py:165
  211.1 0.7 convert_reduce_fusion
  211.8 0.1 reshape.102
  211.8 0.0 collective-permute-done
  211.8 0.8 add_convert_fusion.1
  (9 shorter events, 0.1 us)
Async XLA Ops:
  6.5 77.0 %copy-start = (bf16[6144,96]{0,1:T(8,128)(2,1)S(1)}, bf16[6144,96]{0,1:T(8,128)(2,1)}, u32[]{:S(2)}) copy-start(bf16[6144,96]{0,1:T(8,128)(2,1)} %param.25) | copy-start | bytes 3538948
  6.5 0.8 copy-start.4
  6.5 73.5 %all-gather.3.cloned.1.call-start = ((), (), s32[]{:S(2)}) async-start(), calls=%async_computation.3 | async-start | bytes 1597440 | tf_op jit(solution)/shard_map/all_gather | solution.py:143
  6.6 0.6 copy-start.1
  83.6 7.9 %copy-start.3 = (bf16[6144]{0:T(1024)(128)(2,1)S(1)}, bf16[6144]{0:T(1024)(128)(2,1)}, u32[]{:S(2)}) copy-start(bf16[6144]{0:T(1024)(128)(2,1)} %param.26) | copy-start | bytes 36868
  83.6 16.4 %copy-start.2 = (bf16[2,6144]{1,0:T(2,128)(2,1)S(1)}, bf16[2,6144]{1,0:T(2,128)(2,1)}, u32[]{:S(2)}) copy-start(bf16[2,6144]{1,0:T(2,128)(2,1)} %param.24) | copy-start | bytes 73732
  85.0 14.8 %all-to-all-start = ((bf16[64,2,96]{2,1,0:T(2,128)(2,1)}), bf16[64,2,96]{2,1,0:T(2,128)(2,1)S(1)}, u32[]{:S(2)}, u32[]{:S(2)}) async-start(bf16[64,2,96]{2,1,0:T(2,128)(2,1)} %bitcast.3), calls=%async_computation | async-start | bytes 65536 | tf_op jit(solution)/shard_map/all_to_all | solution.py:147
  105.1 47.8 %all-to-all-start.1 = ((bf16[128,2,6144]{2,1,0:T(2,128)(2,1)}), bf16[128,2,6144]{2,1,0:T(2,128)(2,1)}, u32[]{:S(2)}, u32[]{:S(2)}) async-start(bf16[128,2,6144]{2,1,0:T(2,128)(2,1)} %concatenate.3), calls=%async_computation.1 | async-start | bytes 6291456 | tf_op jit(solution)/shard_map/all_to_all | solution.py:155
  178.9 9.3 %copy-start.5 = (f32[2,2]{1,0:T(2,128)S(1)}, f32[2,2]{1,0:T(2,128)}, u32[]{:S(2)}) copy-start(f32[2,2]{1,0:T(2,128)} %param.28) | copy-start | bytes 52
  178.9 32.2 %all-to-all-start.2 = ((bf16[128,2,3072]{2,1,0:T(2,128)(2,1)}), bf16[128,2,3072]{2,1,0:T(2,128)(2,1)S(1)}, u32[]{:S(2)}, u32[]{:S(2)}) async-start(bf16[128,2,3072]{2,1,0:T(2,128)(2,1)} %copy.56), calls=%async_computation.2 | async-start | bytes 3145728 | tf_op jit(solution)/shard_map/all_to_all | solution.py:165
  188.3 23.5 %collective-permute-start = (bf16[2,3072]{1,0:T(2,128)(2,1)S(1)}, bf16[2,3072]{1,0:T(2,128)(2,1)S(1)}, u32[]{:S(2)}, u32[]{:S(2)}) collective-permute-start(bf16[2,3072]{1,0:T(2,128)(2,1)S(1)} %slice.17), channel_id=1, source_target_pairs={{0,64},{1,65},{2,66},{3,67},{4,68},{5,69},{6,70},{7,71},{8,72},{9,... | collective-permute-start | bytes 36872 | tf_op jit(solution)/shard_map/ppermute | solution.py:24
Sparse Core Ops, SparseCore 0:
  10.2 69.7 all-gather.2
where the time goes:
time: 220 us
  waiting for transfers between devices  142 us (65%)
  starting transfers between devices  24.7 us (11%)
  local copies, waits for them, and re-layouts  24.5 us (11%)
  between operations  13.6 us (6%)
  matrix products  13.2 us (6%)
    all_gather x1, waiting for transfers between devices, local(): lax.all_gather(attention, 'dev', axis=0, tiled=True)  72.2 us
    all_to_all x1, waiting for transfers between devices, local(): lax.all_to_all(padded_rows, ('side', 'dev'), split_axis=0, concat_axis=0,...  40.1 us
    all_to_all x1, waiting for transfers between devices, local(): lax.all_to_all(halves, ('side', 'dev'), split_axis=0, concat_axis=0, tile...  21.5 us
    all_to_all x1, starting transfers between devices, local(): lax.all_to_all(halves, ('side', 'dev'), split_axis=0, concat_axis=0, tile...  9.34 us
    all_to_all x1, waiting for transfers between devices, local(): lax.all_to_all(columns.astype(jnp.bfloat16), 'dev', split_axis=0, concat_...  8.3 us
    all_to_all x1, starting transfers between devices, local(): lax.all_to_all(padded_rows, ('side', 'dev'), split_axis=0, concat_axis=0,...  7.69 us
    dot_general x1, matrix products, expert_block(): jnp.dot(act, w_down, preferred_element_type=jnp.float32)  7.68 us
    all_to_all x1, starting transfers between devices, local(): lax.all_to_all(columns.astype(jnp.bfloat16), 'dev', split_axis=0, concat_...  6.42 us
  transfers between devices with their start and end apart: 5, of which 4 were waited for; matrix products, arithmetic and copies ran while one was open for 1% of the time, Pallas kernels for 0%

commit v1 on v0

v1 whole, which is shorter than its diff:
```python
import math

import jax
import jax.numpy as jnp
import numpy as np
from jax import lax
from jax.sharding import PartitionSpec as P

D = 6144
HEADS = 48
KV_HEADS = 8
HEAD_DIM = 128
EXPERTS = 4
CACHE_LEN = 128
DEVS = 64
COLS = D // DEVS
HALF = COLS // 2
ROWS = D // 128

epsilon = 1e-05


def attend(query, new_key, new_value, key_cache, value_cache, cached):
    group_size = HEADS // KV_HEADS
    score_scale = 1.0 / math.sqrt(HEAD_DIM)
    queries = query.reshape(KV_HEADS, group_size, HEAD_DIM)
    cache_keys = key_cache.reshape(CACHE_LEN, KV_HEADS, HEAD_DIM)
    cache_values = value_cache.reshape(CACHE_LEN, KV_HEADS, HEAD_DIM)
    scores = (
        jnp.einsum("grd,lgd->grl", queries, cache_keys, preferred_element_type=jnp.float32)
        * score_scale
    )
    own_score = (
        jnp.einsum(
            "grd,gd->gr",
            queries,
            new_key.reshape(KV_HEADS, HEAD_DIM),
            preferred_element_type=jnp.float32,
        )
        * score_scale
    )
    visible = jnp.arange(CACHE_LEN) < cached
    scores = jnp.where(visible[None, None, :], scores, -jnp.inf)
    highest = jnp.maximum(jnp.max(scores, axis=2), own_score)
    exponents = jnp.exp(scores - highest[..., None])
    own_exp = jnp.exp(own_score - highest)
    denominator = jnp.sum(exponents, axis=2) + own_exp
    weights = (exponents / denominator[..., None]).astype(jnp.bfloat16)
    own_weight = (own_exp / denominator).astype(jnp.bfloat16)
    context = jnp.einsum(
        "grl,lgd->grd", weights, cache_values, preferred_element_type=jnp.float32
    )
    context = context + own_weight.astype(jnp.float32)[..., None] * new_value.reshape(
        KV_HEADS, 1, HEAD_DIM
    ).astype(jnp.float32)
    return context.reshape(HEADS, HEAD_DIM).astype(jnp.bfloat16)


def exchange(parts):
    return lax.all_to_all(parts, "dev", split_axis=0, concat_axis=0, tiled=True)


def local(
    query,
    new_key,
    new_value,
    key_cache,
    value_cache,
    cached,
    residual,
    out_weight,
    norm_gain,
    expert_ids,
    gate_weights,
    w_gate,
    w_up,
    w_down,
):
    core = lax.axis_index("side")
    chip = lax.axis_index("dev")

    def own(value):
        return lax.dynamic_index_in_dim(value, core, 0, keepdims=False)

    context = attend(
        own(query), own(new_key), own(new_value), own(key_cache), own(value_cache), own(cached)
    )
    first_row = (COLS * np.arange(DEVS)) // 128
    wanted = np.minimum(first_row[:, None] + np.arange(8)[None, :], ROWS - 1)
    residual_rows = own(residual).reshape(ROWS, 128)[wanted]
    outgoing = jnp.concatenate(
        [jnp.broadcast_to(context[None], (DEVS, ROWS, 128)), residual_rows], axis=1
    )
    arrived = exchange(outgoing)
    projected = jnp.dot(
        arrived[:, :ROWS].reshape(DEVS, D), out_weight, preferred_element_type=jnp.float32
    )
    residual_part = lax.dynamic_slice_in_dim(
        arrived[:, ROWS : ROWS + 2].reshape(DEVS, 256), (COLS * chip) % 128, COLS, 1
    )
    hidden_part = (residual_part.astype(jnp.float32) + projected).astype(jnp.bfloat16)
    flipped = hidden_part.T
    packed = jnp.concatenate([flipped[:HALF], flipped[HALF:]], axis=1)
    hidden_all = exchange(jnp.broadcast_to(packed[None], (DEVS, HALF, 128)))
    hidden = (
        hidden_all.reshape(DEVS, HALF, 2, DEVS).transpose(3, 0, 2, 1).reshape(DEVS, D)
    )
    widened = hidden.astype(jnp.float32)
    factor = lax.rsqrt(jnp.mean(widened * widened, axis=1, keepdims=True) + epsilon)
    normed = (widened * factor * norm_gain.astype(jnp.float32)[None, :]).astype(jnp.bfloat16)
    gate_part = jnp.dot(normed, w_gate, preferred_element_type=jnp.float32)
    up_part = jnp.dot(normed, w_up, preferred_element_type=jnp.float32)
    act = (jax.nn.silu(gate_part) * up_part).astype(jnp.bfloat16)
    partial_value = jnp.dot(act, w_down, preferred_element_type=jnp.float32).astype(jnp.bfloat16)
    returned = exchange(partial_value.reshape(DEVS, ROWS, 128))
    share = jnp.sum(
        jnp.where(
            own(expert_ids)[None, :] == jnp.arange(EXPERTS)[:, None], own(gate_weights)[None, :], 0.0
        ),
        axis=1,
    )
    per_expert = jnp.sum(
        returned.reshape(EXPERTS, DEVS // EXPERTS, ROWS, 128).astype(jnp.float32), axis=1
    )
    moe = jnp.sum(per_expert * share[:, None, None], axis=0)
    own_hidden = lax.dynamic_index_in_dim(hidden, chip, 0, keepdims=False).reshape(ROWS, 128)
    mixed = (own_hidden.astype(jnp.float32) + moe).astype(jnp.bfloat16)
    halves = mixed.reshape(2, ROWS // 2, 128)
    kept = own(halves)
    given = lax.dynamic_index_in_dim(halves, 1 - core, 0, keepdims=False)
    taken = lax.ppermute(given, "side", [(0, 1), (1, 0)])
    first = jnp.where(core == 0, kept, taken)
    second = jnp.where(core == 0, taken, kept)
    return jnp.stack([first.reshape(D // 2), second.reshape(D // 2)])


def solution(mesh):
    in_specs = (
        P("dev", None),
        P("dev", None),
        P("dev", None),
        P("dev", None, None),
        P("dev", None, None),
        P("dev"),
        P("dev", None),
        P(None, "dev"),
        P(),
        P("dev", None),
        P("dev", None),
        P(None, "dev"),
        P(None, "dev"),
        P("dev", None),
    )
    out_specs = P("dev", "side")
    return jax.shard_map(local, mesh=mesh, in_specs=in_specs, out_specs=out_specs, check_vma=False)
```

time: 220 us -> 112 us (0.51)
  waiting for transfers between devices: 142 us -> 41.8 us
  between operations: 13.6 us -> 0.27 us
  other arithmetic: 1.35 us -> 8.14 us
  local copies, waits for them, and re-layouts: 24.5 us -> 21.6 us
  starting transfers between devices: 24.7 us -> 27.5 us
    all_gather x1 -> x0, waiting for transfers between devices: 72.2 us -> none  [local(): lax.all_gather(attention, 'dev', axis=0, tiled=True)]
    all_to_all x3, waiting for transfers between devices: 69.9 us -> 41 us  [exchange(): return lax.all_to_all(parts, 'dev', split_axis=0, concat_axis=0, tiled=True)]
    transpose x1, local copies, waits for them, and re-layouts: 0.47 us -> 6.18 us  [local(): hidden_all.reshape(DEVS, HALF, 2, DEVS).transpose(3, 0, 2, 1)]
    concatenate x1 -> x0, local copies, waits for them, and re-layouts: 3.72 us -> none  [local(): padded_rows = jnp.concatenate([jnp.zeros_like(outgoing), outgoing], axis=0)]
    dynamic_slice x0 -> x3, local copies, waits for them, and re-layouts: none -> 3.33 us  [own(): return lax.dynamic_index_in_dim(value, core, 0, keepdims=False)]
    slice x2 -> x5, local copies, waits for them, and re-layouts: 3.63 us -> 0.32 us  [the longest x3 0.24 us: local(): packed = jnp.concatenate([flipped[:HALF], flipped[HALF:]], axis=1)]
    unnamed x13 -> x18, local copies, waits for them, and re-layouts: 4.22 us -> 1.41 us
    reshape x4 -> x3, local copies, waits for them, and re-layouts: 10.5 us -> 7.83 us  [the longest x2 7.82 us: local(): hidden_all.reshape(DEVS, HALF, 2, DEVS).transpose(3, 0, 2, 1)]
  transfers between devices with their start and end apart: 5 -> 4, of which waited for: 4 -> 4; matrix products, arithmetic and copies ran while one was open for 1% -> 1% of each run, Pallas kernels for 0% -> 0%
where the time goes in v1:
time: 112 us
  waiting for transfers between devices  41.8 us (37%)
  starting transfers between devices  27.5 us (25%)
  local copies, waits for them, and re-layouts  21.6 us (19%)
  matrix products  12.3 us (11%)
  other arithmetic  8.14 us (7%)
    all_to_all x3, waiting for transfers between devices, exchange(): return lax.all_to_all(parts, 'dev', split_axis=0, concat_axis=0, tiled=True)  41 us
    all_to_all x3, starting transfers between devices, exchange(): return lax.all_to_all(parts, 'dev', split_axis=0, concat_axis=0, tiled=True)  23.7 us
    reshape x2, local copies, waits for them, and re-layouts, local(): hidden_all.reshape(DEVS, HALF, 2, DEVS).transpose(3, 0, 2, 1)  7.82 us
    dot_general x1, matrix products, local(): jnp.dot(act, w_down, preferred_element_type=jnp.float32)  7.03 us
    transpose x1, local copies, waits for them, and re-layouts, local(): hidden_all.reshape(DEVS, HALF, 2, DEVS).transpose(3, 0, 2, 1)  6.18 us
    dot_general x1, matrix products, local(): gate_part = jnp.dot(normed, w_gate, preferred_element_type=jnp.float32)  4.04 us
    ppermute x1, starting transfers between devices, local(): taken = lax.ppermute(given, 'side', [(0, 1), (1, 0)])  3.82 us
    dynamic_slice x3, local copies, waits for them, and re-layouts, own(): return lax.dynamic_index_in_dim(value, core, 0, keepdims=False)  3.33 us
  transfers between devices with their start and end apart: 4, of which 4 were waited for; matrix products, arithmetic and copies ran while one was open for 1% of the time, Pallas kernels for 0%

profile of v1, /device:TPU:1, one launch (start us, length us, event | category | flops | bytes accessed | tf_op | source)
XLA Modules:
  0.0 111.5 jit_solution(9298415530537617362)
XLA Ops:
  0.0 0.0 copy-start
  0.0 0.0 copy-start.3
  0.0 1.3 %dynamic_slice.47 = s32[1]{0:T(128)} dynamic-slice(s32[2]{0:T(128)} %param.21, s32[]{:T(128)S(6)} %select_n.60), dynamic_slice_sizes={1} | dynamic-slice | bytes 12 | tf_op jit(solution)/shard_map/jit(dynamic_index_in_dim)/dynamic_slice | solution.py:83
  1.4 0.6 iota_compare_fusion
  2.0 0.7 dynamic-slice_convert_fusion.1
  2.7 0.7 pad_clamp_fusion
  3.4 0.9 dynamic-slice_reduce_fusion
  4.3 1.1 constant_dynamic-slice_fusion.2
  5.4 0.2 copy.43
  5.6 0.2 copy.42
  5.8 0.0 copy-done.3
  5.8 0.1 fusion.20
  5.9 0.3 fusion.31
  6.2 0.2 fusion.15
  6.3 0.3 fusion.3
  6.7 1.3 %gather_fusion = bf16[512,128]{1,0:T(8,128)(2,1)S(1)} fusion(bf16[48,128]{1,0:T(8,128)(2,1)S(1)} %bitcast.64, s32[1024]{0:T(1024)S(1)} %pad_clamp_fusion), kind=kCustom, calls=%fused_computation | custom fusion | bytes 264192 | tf_op jit(solution)/shard_map/gather | solution.py:90
  8.0 0.1 broadcast_in_dim.34
  8.1 1.0 pad_maximum_fusion
  9.1 12.0 %all-to-all-start = ((bf16[64,56,128]{2,1,0:T(8,128)(2,1)}), bf16[64,56,128]{2,1,0:T(8,128)(2,1)S(1)}, u32[]{:S(2)}, u32[]{:S(2)}) async-start(bf16[64,56,128]{2,1,0:T(8,128)(2,1)} %pad_maximum_fusion), calls=%async_computation | async-start | bytes 1835008 | tf_op jit(solution)/shard_map/all_to_all | solution.py:60
  21.1 15.3 %all-to-all-done = bf16[64,56,128]{2,1,0:T(8,128)(2,1)S(1)} async-done(((bf16[64,56,128]{2,1,0:T(8,128)(2,1)}), bf16[64,56,128]{2,1,0:T(8,128)(2,1)S(1)}, u32[]{:S(2)}, u32[]{:S(2)}) %all-to-all-start) | async-done | bytes 917536 | tf_op jit(solution)/shard_map/all_to_all | solution.py:60
  36.5 0.1 slice.19
  36.5 0.0 copy-done
  36.5 0.0 copy-start.2
  36.6 0.0 copy-start.4
  36.6 0.0 copy-start.5
  36.6 0.6 fusion.5
  37.1 0.1 fusion.30
  37.2 0.1 copy.35
  37.3 0.1 copy.36
  37.4 0.1 pad_maximum_fusion.1
  37.5 1.0 broadcast_in_dim.55
  38.5 5.8 %all-to-all-start.1 = ((bf16[64,48,128]{2,1,0:T(8,128)(2,1)}), bf16[64,48,128]{2,1,0:T(8,128)(2,1)S(1)}, u32[]{:S(2)}, u32[]{:S(2)}) async-start(bf16[64,48,128]{2,1,0:T(8,128)(2,1)} %broadcast_in_dim.55), calls=%async_computation.1 | async-start | bytes 1572864 | tf_op jit(solution)/shard_map/all_to_all | solution.py:60
  44.3 0.0 copy-done.2
  44.3 0.6 convert_element_type.84
  44.9 0.0 copy-done.4
  44.9 0.0 copy-done.5
  44.9 12.7 %all-to-all-done.1 = bf16[64,48,128]{2,1,0:T(8,128)(2,1)S(1)} async-done(((bf16[64,48,128]{2,1,0:T(8,128)(2,1)}), bf16[64,48,128]{2,1,0:T(8,128)(2,1)S(1)}, u32[]{:S(2)}, u32[]{:S(2)}) %all-to-all-start.1) | async-done | bytes 786464 | tf_op jit(solution)/shard_map/all_to_all | solution.py:60
  57.6 0.7 reshape.88
  58.3 3.3 %multiply_reduce_fusion = f32[64]{0:T(128)S(1)} fusion(bf16[64,48,2,64]{3,2,1,0:T(2,128)(2,1)S(1)} %reshape.88), kind=kLoop, calls=%fused_computation.2 | loop fusion | flops 1179584 | bytes 786688 | tf_op jit(solution)/shard_map/reduce_sum | solution.py:109
  61.6 6.2 %copy.37 = bf16[64,64,2,48]{3,2,1,0:T(2,128)(2,1)} copy(bf16[64,64,2,48]{0,2,3,1:T(2,128)(2,1)S(1)} %bitcast.65) | data formatting | bytes 1572864 | tf_op jit(solution)/shard_map/transpose | solution.py:106
  67.7 0.0 copy-start.1
  67.7 7.1 %reshape.89 = bf16[64,6144]{1,0:T(8,128)(2,1)S(1)} reshape(bf16[64,64,2,48]{3,2,1,0:T(2,128)(2,1)} %copy.37) | data formatting | bytes 1572864 | tf_op jit(solution)/shard_map/reshape | solution.py:106
  74.9 0.0 copy-done.1
  74.9 4.0 %fusion.8 = f32[64,512]{1,0:T(8,128)S(1)} fusion(bf16[6144,512]{1,0:T(8,128)(2,1)} %param.27, bf16[64,6144]{1,0:T(8,128)(2,1)S(1)} %reshape.89, f32[6144]{0:T(1024)S(1)} %copy-done.1, f32[64]{0:T(128)S(1)} %add_rsqrt_fusion), kind=kOutput, calls=%fused_computation.18 | convolution fusion | flops 404226048 | bytes 7233792 | tf_op jit(solution)/shard_map/dot_general | solution.py:111
  78.9 7.0 %fusion = bf16[8,8,48,128]{3,1,2,0:T(8,128)(2,1)S(1)} fusion(bf16[512,6144]{1,0:T(8,128)(2,1)} %param.29, bf16[6144,512]{1,0:T(8,128)(2,1)} %param.28, bf16[64,6144]{1,0:T(8,128)(2,1)S(1)} %reshape.89, f32[6144]{0:T(1024)S(1)} %copy-done.1, f32[64]{0:T(128)S(1)} %add_rsqrt_fusion, f32[64,512]{1,0:T(8,128)S(1)} %fusion.8), kind=kOutput, calls=%fused_computation.5 | convolution fusion | flops 807469056 | bytes 14311680 | tf_op jit(solution)/shard_map/dot_general | solution.py:114
  86.0 1.0 copy.46
  87.0 5.9 %all-to-all-start.2 = ((bf16[64,48,128]{2,1,0:T(8,128)(2,1)}), bf16[64,48,128]{2,1,0:T(8,128)(2,1)S(1)}, u32[]{:S(2)}, u32[]{:S(2)}) async-start(bf16[64,48,128]{2,1,0:T(8,128)(2,1)} %bitcast.24), calls=%async_computation.2 | async-start | bytes 1572864 | tf_op jit(solution)/shard_map/all_to_all | solution.py:60
  92.9 0.1 fusion.26
  93.0 13.0 %all-to-all-done.2 = bf16[64,48,128]{2,1,0:T(8,128)(2,1)S(1)} async-done(((bf16[64,48,128]{2,1,0:T(8,128)(2,1)}), bf16[64,48,128]{2,1,0:T(8,128)(2,1)S(1)}, u32[]{:S(2)}, u32[]{:S(2)}) %all-to-all-start.2) | async-done | bytes 786464 | tf_op jit(solution)/shard_map/all_to_all | solution.py:60
  106.0 0.1 convert_reduce_fusion
  106.1 0.1 multiply_reduce_fusion.1
  106.2 3.8 %collective-permute-start = (bf16[24,128]{1,0:T(8,128)(2,1)S(1)}, bf16[24,128]{1,0:T(8,128)(2,1)S(1)}, u32[]{:S(2)}, u32[]{:S(2)}) collective-permute-start(bf16[24,128]{1,0:T(8,128)(2,1)S(1)} %dynamic-slice_bitcast_fusion), channel_id=1, source_target_pairs={{0,64},{64,0},{1,65},{65,1},{2,66},{66,2},{3,67},{67,3},{4,68},{68... | collective-permute-start | bytes 18440 | tf_op jit(solution)/shard_map/ppermute | solution.py:131
  110.0 0.8 collective-permute-done
  110.9 0.6 pad_maximum_fusion.2
  (15 shorter events, 0.2 us)
Async XLA Ops:
  0.0 36.5 %copy-start = (bf16[6144,96]{0,1:T(8,128)(2,1)S(1)}, bf16[6144,96]{0,1:T(8,128)(2,1)}, u32[]{:S(2)}) copy-start(bf16[6144,96]{0,1:T(8,128)(2,1)} %param.23) | copy-start | bytes 3538948
  0.0 5.8 %copy-start.3 = (bf16[2,1024]{1,0:T(2,128)(2,1)S(1)}, bf16[2,1024]{1,0:T(2,128)(2,1)}, u32[]{:S(2)}) copy-start(bf16[2,1024]{1,0:T(2,128)(2,1)} %param.17) | copy-start | bytes 12292
  9.1 27.3 %all-to-all-start = ((bf16[64,56,128]{2,1,0:T(8,128)(2,1)}), bf16[64,56,128]{2,1,0:T(8,128)(2,1)S(1)}, u32[]{:S(2)}, u32[]{:S(2)}) async-start(bf16[64,56,128]{2,1,0:T(8,128)(2,1)} %pad_maximum_fusion), calls=%async_computation | async-start | bytes 1835008 | tf_op jit(solution)/shard_map/all_to_all | solution.py:60
  36.5 7.7 %copy-start.2 = (bf16[6144]{0:T(1024)(128)(2,1)S(1)}, bf16[6144]{0:T(1024)(128)(2,1)}, u32[]{:S(2)}) copy-start(bf16[6144]{0:T(1024)(128)(2,1)} %param.24) | copy-start | bytes 36868
  36.6 8.3 %copy-start.4 = (s32[2,2]{1,0:T(2,128)S(1)}, s32[2,2]{1,0:T(2,128)}, u32[]{:S(2)}) copy-start(s32[2,2]{1,0:T(2,128)} %param.25) | copy-start | bytes 52
  36.6 8.3 %copy-start.5 = (f32[2,2]{1,0:T(2,128)S(1)}, f32[2,2]{1,0:T(2,128)}, u32[]{:S(2)}) copy-start(f32[2,2]{1,0:T(2,128)} %param.26) | copy-start | bytes 52
  38.5 19.1 %all-to-all-start.1 = ((bf16[64,48,128]{2,1,0:T(8,128)(2,1)}), bf16[64,48,128]{2,1,0:T(8,128)(2,1)S(1)}, u32[]{:S(2)}, u32[]{:S(2)}) async-start(bf16[64,48,128]{2,1,0:T(8,128)(2,1)} %broadcast_in_dim.55), calls=%async_computation.1 | async-start | bytes 1572864 | tf_op jit(solution)/shard_map/all_to_all | solution.py:60
  67.7 7.1 %copy-start.1 = (f32[6144]{0:T(1024)S(1)}, f32[6144]{0:T(1024)}, u32[]{:S(2)}) copy-start(f32[6144]{0:T(1024)} %convert_element_type.84) | copy-start | bytes 73732
  87.0 19.0 %all-to-all-start.2 = ((bf16[64,48,128]{2,1,0:T(8,128)(2,1)}), bf16[64,48,128]{2,1,0:T(8,128)(2,1)S(1)}, u32[]{:S(2)}, u32[]{:S(2)}) async-start(bf16[64,48,128]{2,1,0:T(8,128)(2,1)} %bitcast.24), calls=%async_computation.2 | async-start | bytes 1572864 | tf_op jit(solution)/shard_map/all_to_all | solution.py:60
  106.2 4.6 %collective-permute-start = (bf16[24,128]{1,0:T(8,128)(2,1)S(1)}, bf16[24,128]{1,0:T(8,128)(2,1)S(1)}, u32[]{:S(2)}, u32[]{:S(2)}) collective-permute-start(bf16[24,128]{1,0:T(8,128)(2,1)S(1)} %dynamic-slice_bitcast_fusion), channel_id=1, source_target_pairs={{0,64},{64,0},{1,65},{65,1},{2,66},{66,2},{3,67},{67,3},{4,68},{68... | collective-permute-start | bytes 18440 | tf_op jit(solution)/shard_map/ppermute | solution.py:131

commit v2 on v1

v2 whole, which is shorter than its diff:
```python
import math

import jax
import jax.numpy as jnp
from jax import lax
from jax.experimental import pallas as pl
from jax.experimental.pallas import tpu as pltpu
from jax.sharding import PartitionSpec as P

D = 6144
HEADS = 48
KV_HEADS = 8
HEAD_DIM = 128
GROUP = HEADS // KV_HEADS
EXPERTS = 4
CACHE_LEN = 128
DEVS = 64
COLS = D // DEVS
HALF = COLS // 2
ROWS = D // 128
SENT = ROWS + 8
UNITS = 512
HALF_D = D // 2
CHUNK = 768
PART = CHUNK // HALF

epsilon = 1e-05

VMEM_BLOCK = pl.BlockSpec(memory_space=pltpu.VMEM)
SMEM_BLOCK = pl.BlockSpec(memory_space=pltpu.SMEM)
ANY_BLOCK = pl.BlockSpec(memory_space=pl.ANY)


def last_dims(left, right):
    return lax.dot_general(
        left, right, (((1,), (1,)), ((), ())), preferred_element_type=jnp.float32
    )


def attend_kernel(
    core_ref,
    cached_ref,
    query_ref,
    new_key_ref,
    new_value_ref,
    residual_ref,
    key_ref,
    value_ref,
    out_ref,
    query_rows,
    context_rows,
    residual_rows,
):
    core = core_ref[0]

    def own(ref):
        both = ref[...].astype(jnp.float32)
        return jnp.where(core == 0, both[0:1], both[1:2])

    query = own(query_ref)
    new_key = own(new_key_ref)
    new_value = own(new_value_ref)
    residual = own(residual_ref)
    query_rows[...] = jnp.zeros_like(query_rows)
    for head in range(HEADS):
        row = head // GROUP * 8 + head % GROUP
        query_rows[row : row + 1, :] = query[:, head * 128 : head * 128 + 128]
    for row in range(ROWS):
        residual_rows[row : row + 1, :] = residual[:, row * 128 : row * 128 + 128]
    residual_rows[ROWS:SENT, :] = jnp.zeros((SENT - ROWS, 128), jnp.float32)
    queries = query_rows[...]
    narrow = queries.astype(jnp.bfloat16)
    scale = 1.0 / math.sqrt(HEAD_DIM)
    scores = []
    own_keys = []
    for kv in range(KV_HEADS):
        lanes = slice(kv * 128, kv * 128 + 128)
        scores.append(last_dims(narrow[kv * 8 : kv * 8 + 8], key_ref[0, :, lanes]))
        own_keys.append(jnp.broadcast_to(new_key[:, lanes], (8, 128)))
    scores = jnp.concatenate(scores, axis=0) * scale
    own_score = jnp.sum(queries * jnp.concatenate(own_keys, axis=0), axis=1, keepdims=True) * scale
    visible = lax.broadcasted_iota(jnp.int32, scores.shape, 1) < cached_ref[core]
    scores = jnp.where(visible, scores, -jnp.inf)
    highest = jnp.maximum(jnp.max(scores, axis=1, keepdims=True), own_score)
    exponents = jnp.exp(scores - highest)
    own_exp = jnp.exp(own_score - highest)
    denominator = jnp.sum(exponents, axis=1, keepdims=True) + own_exp
    weights = (exponents / denominator).astype(jnp.bfloat16)
    own_weight = (own_exp / denominator).astype(jnp.bfloat16).astype(jnp.float32)
    for kv in range(KV_HEADS):
        lanes = slice(kv * 128, kv * 128 + 128)
        context = jnp.dot(
            weights[kv * 8 : kv * 8 + 8], value_ref[0, :, lanes], preferred_element_type=jnp.float32
        )
        context = context + own_weight[kv * 8 : kv * 8 + 8] * new_value[:, lanes]
        context_rows[kv * GROUP : kv * GROUP + 8, :] = context
    context = context_rows[0:HEADS, :].astype(jnp.bfloat16)
    for chip in range(DEVS):
        first = COLS * chip // 128
        out_ref[chip, 0:ROWS, :] = context
        out_ref[chip, ROWS:SENT, :] = residual_rows[first : first + 8, :].astype(jnp.bfloat16)


def attend(core, cached, query, new_key, new_value, residual, key_cache, value_cache):
    def whole(shape):
        return pl.BlockSpec(shape, lambda step, core, cached: (0,) * len(shape))

    cache = pl.BlockSpec((1, CACHE_LEN, 1024), lambda step, core, cached: (core[0], 0, 0))
    return pl.pallas_call(
        attend_kernel,
        out_shape=jax.ShapeDtypeStruct((DEVS, SENT, 128), jnp.bfloat16),
        grid_spec=pltpu.PrefetchScalarGridSpec(
            num_scalar_prefetch=2,
            grid=(1,),
            in_specs=[
                whole((2, D)),
                whole((2, 1024)),
                whole((2, 1024)),
                whole((2, D)),
                cache,
                cache,
            ],
            out_specs=whole((DEVS, SENT, 128)),
            scratch_shapes=[
                pltpu.VMEM((64, 128), jnp.float32),
                pltpu.VMEM((SENT, 128), jnp.float32),
                pltpu.VMEM((SENT, 128), jnp.float32),
            ],
        ),
        compiler_params=pltpu.CompilerParams(vmem_limit_bytes=8 << 20),
        name="attend",
    )(core, cached, query, new_key, new_value, residual, key_cache, value_cache)


def project_kernel(chip_ref, arrived_ref, weight_ref, out_ref, rows, context):
    for source in range(DEVS):
        rows[source * SENT : source * SENT + SENT, :] = arrived_ref[source].astype(jnp.float32)
    for head in range(HEADS):
        context[:, head * 128 : head * 128 + 128] = rows[pl.ds(head, DEVS, stride=SENT), :].astype(
            jnp.bfloat16
        )
    tokens = context[...]
    projected = last_dims(weight_ref[...], jnp.concatenate([tokens, tokens], axis=0))
    flipped = []
    for row in (ROWS, ROWS + 1):
        part = rows[pl.ds(row, DEVS, stride=SENT), :]
        flipped.append(jnp.concatenate([part, part], axis=0).T)
    rows[0:256, :] = jnp.concatenate(flipped, axis=0)
    first = pl.multiple_of(lax.rem(chip_ref[0] * COLS, 128), 32)
    hidden = rows[pl.ds(first, COLS), :] + projected
    lane = lax.broadcasted_iota(jnp.int32, (HALF, 128), 1)
    packed = jnp.where(lane < DEVS, hidden[0:HALF], hidden[HALF:COLS]).astype(jnp.bfloat16)
    for target in range(DEVS):
        out_ref[target] = packed


def project(chip, arrived, weight):
    return pl.pallas_call(
        project_kernel,
        out_shape=jax.ShapeDtypeStruct((DEVS, HALF, 128), jnp.bfloat16),
        in_specs=[SMEM_BLOCK, VMEM_BLOCK, VMEM_BLOCK],
        out_specs=VMEM_BLOCK,
        scratch_shapes=[
            pltpu.VMEM((DEVS * SENT, 128), jnp.float32),
            pltpu.VMEM((DEVS, D), jnp.bfloat16),
        ],
        compiler_params=pltpu.CompilerParams(vmem_limit_bytes=16 << 20),
        name="project",
    )(chip, arrived, weight)


def expert_kernel(
    chip_ref,
    hidden_ref,
    gain_ref,
    gate_hbm,
    up_hbm,
    down_hbm,
    out_ref,
    own_ref,
    gate_vmem,
    up_vmem,
    down_vmem,
    flipped,
    scaled,
    result,
    sems,
):
    copies = []
    for half in range(2):
        for step in range(HALF_D // CHUNK):
            part = pl.ds(step * PART, PART)
            pair = []
            for source, target, which in ((gate_hbm, gate_vmem, 0), (up_hbm, up_vmem, 1)):
                copy = pltpu.make_async_copy(
                    source.at[part, half], target.at[part, half], sems.at[which, half, step]
                )
                copy.start()
                pair.append(copy)
            copies.append(pair)
    down_copies = []
    for step in range(4):
        part = pl.ds(step * (D // 4), D // 4)
        copy = pltpu.make_async_copy(
            down_hbm.at[:, part], down_vmem.at[:, part], sems.at[2, 0, step]
        )
        copy.start()
        down_copies.append(copy)

    squares = jnp.zeros((128, 128), jnp.float32)
    for block in range(HALF_D // 128):
        lanes = slice(block * 128, block * 128 + 128)
        turned = hidden_ref[lanes, :].astype(jnp.float32).T
        flipped[:, lanes] = turned
        squares = squares + turned * turned
        gain = gain_ref[:, lanes].astype(jnp.float32)
        scaled[0:DEVS, lanes] = (turned[0:DEVS] * gain[0:1]).astype(jnp.bfloat16)
        scaled[DEVS:128, lanes] = (turned[DEVS:128] * gain[1:2]).astype(jnp.bfloat16)
    chip = chip_ref[0]
    own_ref[0:1, :] = flipped[pl.ds(chip, 1), :]
    own_ref[1:2, :] = flipped[pl.ds(chip + DEVS, 1), :]
    total = jnp.sum(squares, axis=1, keepdims=True)
    factor = lax.rsqrt((total[0:DEVS] + total[DEVS:128]) * (1.0 / D) + epsilon)

    gate = jnp.zeros((DEVS, UNITS), jnp.float32)
    up = jnp.zeros((DEVS, UNITS), jnp.float32)
    for half in range(2):
        for step in range(HALF_D // CHUNK):
            for copy in copies[half * (HALF_D // CHUNK) + step]:
                copy.wait()
            rows = scaled[half * DEVS : half * DEVS + DEVS, step * CHUNK : step * CHUNK + CHUNK]
            part = slice(step * PART, step * PART + PART)
            gate = gate + jnp.dot(
                rows,
                gate_vmem[part, half].reshape(CHUNK, UNITS),
                preferred_element_type=jnp.float32,
            )
            up = up + jnp.dot(
                rows, up_vmem[part, half].reshape(CHUNK, UNITS), preferred_element_type=jnp.float32
            )
    gate = gate * factor
    up = up * factor
    act = (gate / (1.0 + jnp.exp(-gate)) * up).astype(jnp.bfloat16)
    for step in range(4):
        down_copies[step].wait()
        for piece in range(D // 4 // 512):
            first = step * (D // 4) + piece * 512
            block = jnp.dot(
                act, down_vmem[:, first : first + 512], preferred_element_type=jnp.float32
            )
            for column in range(4):
                result[pl.ds(first // 128 + column, DEVS, stride=ROWS), :] = block[
                    :, column * 128 : column * 128 + 128
                ]
    for target in range(DEVS):
        out_ref[target] = result[target * ROWS : target * ROWS + ROWS, :].astype(jnp.bfloat16)


def run_experts(chip, hidden, gain, w_gate, w_up, w_down):
    return pl.pallas_call(
        expert_kernel,
        out_shape=(
            jax.ShapeDtypeStruct((DEVS, ROWS, 128), jnp.bfloat16),
            jax.ShapeDtypeStruct((2, HALF_D), jnp.float32),
        ),
        in_specs=[SMEM_BLOCK, VMEM_BLOCK, VMEM_BLOCK, ANY_BLOCK, ANY_BLOCK, ANY_BLOCK],
        out_specs=(VMEM_BLOCK, VMEM_BLOCK),
        scratch_shapes=[
            pltpu.VMEM((DEVS, 2, HALF, UNITS), jnp.bfloat16),
            pltpu.VMEM((DEVS, 2, HALF, UNITS), jnp.bfloat16),
            pltpu.VMEM((UNITS, D), jnp.bfloat16),
            pltpu.VMEM((128, HALF_D), jnp.float32),
            pltpu.VMEM((128, HALF_D), jnp.bfloat16),
            pltpu.VMEM((DEVS * ROWS, 128), jnp.float32),
            pltpu.SemaphoreType.DMA((3, 2, HALF_D // CHUNK)),
        ],
        compiler_params=pltpu.CompilerParams(vmem_limit_bytes=40 << 20),
        name="experts",
    )(chip, hidden, gain, w_gate, w_up, w_down)


def mix_kernel(core_ref, ids_ref, gates_ref, returned_ref, hidden_ref, kept_ref, given_ref):
    core = core_ref[0]
    total = hidden_ref[...]
    for expert in range(EXPERTS):
        share = jnp.float32(0.0)
        for choice in range(2):
            share = share + jnp.where(
                ids_ref[core, choice] == expert, gates_ref[core, choice], jnp.float32(0.0)
            )
        block = jnp.zeros((ROWS, 128), jnp.float32)
        for source in range(DEVS // EXPERTS):
            block = block + returned_ref[expert * (DEVS // EXPERTS) + source].astype(jnp.float32)
        total = total + block * share
    lower, upper = total[0 : ROWS // 2], total[ROWS // 2 : ROWS]
    kept_ref[...] = jnp.where(core == 0, lower, upper).astype(jnp.bfloat16)
    given_ref[...] = jnp.where(core == 0, upper, lower).astype(jnp.bfloat16)


def mix(core, expert_ids, gate_weights, returned, hidden):
    half = jax.ShapeDtypeStruct((ROWS // 2, 128), jnp.bfloat16)
    return pl.pallas_call(
        mix_kernel,
        out_shape=(half, half),
        in_specs=[SMEM_BLOCK, SMEM_BLOCK, SMEM_BLOCK, VMEM_BLOCK, VMEM_BLOCK],
        out_specs=(VMEM_BLOCK, VMEM_BLOCK),
        compiler_params=pltpu.CompilerParams(vmem_limit_bytes=8 << 20),
        name="mix",
    )(core, expert_ids, gate_weights, returned, hidden)


def exchange(parts):
    return lax.all_to_all(parts, "dev", split_axis=0, concat_axis=0, tiled=True)


def local(
    query,
    new_key,
    new_value,
    key_cache,
    value_cache,
    cached,
    residual,
    out_weight,
    norm_gain,
    expert_ids,
    gate_weights,
    w_gate,
    w_up,
    w_down,
):
    core = lax.axis_index("side").astype(jnp.int32).reshape(1)
    chip = lax.axis_index("dev").astype(jnp.int32).reshape(1)
    gain = norm_gain.reshape(DEVS, 2, HALF).transpose(1, 0, 2).reshape(2, HALF_D)
    outgoing = attend(
        core, cached, query, new_key, new_value, residual, key_cache, value_cache
    )
    arrived = exchange(outgoing)
    hidden = exchange(project(chip, arrived, out_weight.T)).reshape(HALF_D, 128)
    partial_value, own_hidden = run_experts(
        chip,
        hidden,
        gain,
        w_gate.reshape(DEVS, 2, HALF, UNITS),
        w_up.reshape(DEVS, 2, HALF, UNITS),
        w_down,
    )
    returned = exchange(partial_value)
    own_hidden = own_hidden.reshape(2, DEVS, HALF).transpose(1, 0, 2).reshape(ROWS, 128)
    kept, given = mix(core, expert_ids, gate_weights, returned, own_hidden)
    taken = lax.ppermute(given, "side", [(0, 1), (1, 0)])
    first = jnp.where(core == 0, kept, taken)
    second = jnp.where(core == 0, taken, kept)
    return jnp.stack([first.reshape(D // 2), second.reshape(D // 2)])


def solution(mesh):
    in_specs = (
        P("dev", None),
        P("dev", None),
        P("dev", None),
        P("dev", None, None),
        P("dev", None, None),
        P("dev"),
        P("dev", None),
        P(None, "dev"),
        P(),
        P("dev", None),
        P("dev", None),
        P(None, "dev"),
        P(None, "dev"),
        P("dev", None),
    )
    out_specs = P("dev", "side")
    return jax.shard_map(local, mesh=mesh, in_specs=in_specs, out_specs=out_specs, check_vma=False)
```

time: 112 us -> 94.9 us (0.85)
  matrix products: 12.3 us -> 0 us
  Pallas kernels: 0 us -> 11 us
  local copies, waits for them, and re-layouts: 21.6 us -> 13 us
  other arithmetic: 8.14 us -> 0.64 us
    dot_general x6 -> x0, matrix products: 12.3 us -> none  [the longest x1 7.03 us: local(): jnp.dot(act, w_down, preferred_element_type=jnp.float32)]
    unnamed x18 -> x26, local copies, waits for them, and re-layouts: 1.41 us -> 12.4 us
    pallas_call x0 -> x4, Pallas kernels: none -> 11 us  [the longest x1 6.57 us: run_experts(): pl.pallas_call(expert_kernel, out_shape=(jax.ShapeDtypeStruct((DEVS, ROWS...]
    reshape x3 -> x4, local copies, waits for them, and re-layouts: 7.83 us -> 0.42 us  [the longest x2 0.22 us: local(): own_hidden.reshape(2, DEVS, HALF).transpose(1, 0, 2).reshape(ROWS, 128)]
    transpose x1 -> x2, local copies, waits for them, and re-layouts: 6.18 us -> 0.06 us  [the longest x1 0.05 us: local(): own_hidden.reshape(2, DEVS, HALF).transpose(1, 0, 2).reshape(ROWS, 128)]
    reduce_sum x5 -> x0, other arithmetic: 3.69 us -> none  [the longest x1 3.25 us: local(): jnp.mean(widened * widened, axis=1, keepdims=True) + epsilon]
    dynamic_slice x3 -> x0, local copies, waits for them, and re-layouts: 3.33 us -> none  [own(): return lax.dynamic_index_in_dim(value, core, 0, keepdims=False)]
    gather x1 -> x0, local copies, waits for them, and re-layouts: 1.34 us -> none  [local(): residual_rows = own(residual).reshape(ROWS, 128)[wanted]]
where the time goes in v2:
time: 94.9 us; the launch traced here: 94.2 us
  waiting for transfers between devices  42.2 us (44%)
  starting transfers between devices  27.3 us (29%)
  local copies, waits for them, and re-layouts  13 us (14%)
  Pallas kernels  11 us (12%)
    all_to_all x3, waiting for transfers between devices, exchange(): return lax.all_to_all(parts, 'dev', split_axis=0, concat_axis=0, tiled=True)  41.4 us
    all_to_all x3, starting transfers between devices, exchange(): return lax.all_to_all(parts, 'dev', split_axis=0, concat_axis=0, tiled=True)  23.4 us
    unnamed x26, local copies, waits for them, and re-layouts  12.4 us
    pallas_call x1, Pallas kernels, run_experts(): pl.pallas_call(expert_kernel, out_shape=(jax.ShapeDtypeStruct((DEVS, ROWS...  6.57 us
    ppermute x1, starting transfers between devices, local(): taken = lax.ppermute(given, 'side', [(0, 1), (1, 0)])  3.82 us
    pallas_call x1, Pallas kernels, attend(): pl.pallas_call(attend_kernel, out_shape=jax.ShapeDtypeStruct((DEVS, SENT,...  2.05 us
  transfers between devices with their start and end apart: 4, of which 4 were waited for; matrix products, arithmetic and copies ran while one was open for 1% of the time, Pallas kernels for 0%

profile of v2, /device:TPU:1, one launch (start us, length us, event | category | flops | bytes accessed | tf_op | source)
XLA Modules:
  0.0 94.2 jit_solution(4303241853645691268)
XLA Ops:
  0.0 0.0 copy-start.3
  0.0 1.0 %copy-done.3 = bf16[2,128,1024]{2,1,0:T(8,128)(2,1)S(1)} copy-done((bf16[2,128,1024]{2,1,0:T(8,128)(2,1)S(1)}, bf16[2,128,1024]{2,1,0:T(8,128)(2,1)}, u32[]{:S(2)}) %copy-start.3) | copy-done | bytes 524312
  1.0 0.0 copy-start.4
  1.0 1.0 %copy-done.4 = bf16[2,128,1024]{2,1,0:T(8,128)(2,1)S(1)} copy-done((bf16[2,128,1024]{2,1,0:T(8,128)(2,1)S(1)}, bf16[2,128,1024]{2,1,0:T(8,128)(2,1)}, u32[]{:S(2)}) %copy-start.4) | copy-done | bytes 524312
  2.1 0.0 copy-start.5
  2.1 0.7 copy-done.5
  2.8 0.0 copy-start.6
  2.8 0.7 copy-done.6
  3.6 0.0 copy-start.7
  3.6 0.7 copy-done.7
  4.2 0.0 copy-start.8
  4.2 0.7 copy-done.8
  4.9 0.0 copy-start.11
  4.9 0.7 copy-done.11
  5.6 0.0 copy-start.12
  5.6 2.0 %attend.1 = bf16[64,56,128]{2,1,0:T(8,128)(2,1)} custom-call(s32[1]{0:T(128)} %bitcast.core_ref, s32[2]{0:T(128)S(1)} %copy-done.11, bf16[2,6144]{1,0:T(2,128)(2,1)S(1)} %copy-done.5, bf16[2,1024]{1,0:T(2,128)(2,1)S(1)} %copy-done.7, bf16[2,1024]{1,0:T(2,128)(2,1)S(1)} %copy-done.8, bf16[2,6144]{1,0:T(2,128)(2,1)S(1)} %copy-done.6, ...), custom_call_target="tpu_custom_call" | custom-call | tf_op jit(solution)/shard_map/attend/pallas_call | solution.py:109
  7.6 12.0 %all-to-all-start = ((bf16[64,56,128]{2,1,0:T(8,128)(2,1)}), bf16[64,56,128]{2,1,0:T(8,128)(2,1)S(1)}, u32[]{:S(2)}, u32[]{:S(2)}) async-start(bf16[64,56,128]{2,1,0:T(8,128)(2,1)} %attend.1), calls=%async_computation | async-start | bytes 1835008 | tf_op jit(solution)/shard_map/all_to_all | solution.py:313
  19.6 15.3 %all-to-all-done.arrived_ref = bf16[64,56,128]{2,1,0:T(8,128)(2,1)S(1)} async-done(((bf16[64,56,128]{2,1,0:T(8,128)(2,1)}), bf16[64,56,128]{2,1,0:T(8,128)(2,1)S(1)}, u32[]{:S(2)}, u32[]{:S(2)}) %all-to-all-start) | async-done | bytes 917536 | tf_op jit(solution)/shard_map/all_to_all | solution.py:313
  34.9 0.0 copy-start.2
  34.9 1.3 %copy-done.2 = bf16[6144,96]{0,1:T(8,128)(2,1)S(1)} copy-done((bf16[6144,96]{0,1:T(8,128)(2,1)S(1)}, bf16[6144,96]{0,1:T(8,128)(2,1)}, u32[]{:S(2)}) %copy-start.2) | copy-done | bytes 1179672
  36.2 1.7 %project.1 = bf16[64,48,128]{2,1,0:T(8,128)(2,1)} custom-call(s32[1]{0:T(128)} %bitcast.2.chip_ref, bf16[64,56,128]{2,1,0:T(8,128)(2,1)S(1)} %all-to-all-done.arrived_ref, bf16[96,6144]{1,0:T(8,128)(2,1)S(1)} %bitcast.22), custom_call_target="tpu_custom_call" | custom-call | tf_op jit(solution)/shard_map/project/pallas_call | solution.py:158
  37.9 5.6 %all-to-all-start.1 = ((bf16[64,48,128]{2,1,0:T(8,128)(2,1)}), bf16[64,48,128]{2,1,0:T(8,128)(2,1)S(1)}, u32[]{:S(2)}, u32[]{:S(2)}) async-start(bf16[64,48,128]{2,1,0:T(8,128)(2,1)} %project.1), calls=%async_computation.1 | async-start | bytes 1572864 | tf_op jit(solution)/shard_map/all_to_all | solution.py:313
  43.5 0.0 copy-done.12
  43.5 0.1 reshape.31
  43.6 0.1 reshape.32.gain_ref
  43.7 13.3 %all-to-all-done.1 = bf16[64,48,128]{2,1,0:T(8,128)(2,1)S(1)} async-done(((bf16[64,48,128]{2,1,0:T(8,128)(2,1)}), bf16[64,48,128]{2,1,0:T(8,128)(2,1)S(1)}, u32[]{:S(2)}, u32[]{:S(2)}) %all-to-all-start.1) | async-done | bytes 786464 | tf_op jit(solution)/shard_map/all_to_all | solution.py:313
  57.0 0.0 copy-start
  57.0 2.8 %copy-done = bf16[6144,512]{1,0:T(8,128)(2,1)S(1)} copy-done((bf16[6144,512]{1,0:T(8,128)(2,1)S(1)}, bf16[6144,512]{1,0:T(8,128)(2,1)}, u32[]{:S(2)}) %copy-start) | copy-done | bytes 6291480
  59.8 0.0 copy-start.1
  59.8 2.8 %copy-done.1 = bf16[6144,512]{1,0:T(8,128)(2,1)S(1)} copy-done((bf16[6144,512]{1,0:T(8,128)(2,1)S(1)}, bf16[6144,512]{1,0:T(8,128)(2,1)}, u32[]{:S(2)}) %copy-start.1) | copy-done | bytes 6291480
  62.6 0.0 copy-start.9
  62.6 0.0 copy-start.10
  62.6 6.6 %experts.1 = (bf16[64,48,128]{2,1,0:T(8,128)(2,1)}, f32[2,3072]{1,0:T(2,128)S(1)}) custom-call(s32[1]{0:T(128)} %bitcast.2.chip_ref, bf16[3072,128]{1,0:T(8,128)(2,1)S(1)} %bitcast.21, bf16[2,3072]{1,0:T(2,128)(2,1)S(1)} %reshape.32.gain_ref, bf16[64,2,48,512]{3,2,1,0:T(8,128)(2,1)S(1)} %bitcast.19, bf16[64,2,48,512]{3,2,1,0:T(8,128)(2,1)S(1)} %bitcast.20, ...), custom_call_target="tpu_custom_call" | custom-call | tf_op jit(solution)/shard_map/experts/pallas_call | solution.py:260
  69.2 5.9 %all-to-all-start.2 = ((bf16[64,48,128]{2,1,0:T(8,128)(2,1)}), bf16[64,48,128]{2,1,0:T(8,128)(2,1)S(1)}, u32[]{:S(2)}, u32[]{:S(2)}) async-start(bf16[64,48,128]{2,1,0:T(8,128)(2,1)} %get-tuple-element.9), calls=%async_computation.2 | async-start | bytes 1572864 | tf_op jit(solution)/shard_map/all_to_all | solution.py:313
  75.1 0.1 reshape.35
  75.2 0.1 copy.17
  75.3 0.1 reshape.36.hidden_ref
  75.4 12.8 %all-to-all-done.2.returned_ref = bf16[64,48,128]{2,1,0:T(8,128)(2,1)S(1)} async-done(((bf16[64,48,128]{2,1,0:T(8,128)(2,1)}), bf16[64,48,128]{2,1,0:T(8,128)(2,1)S(1)}, u32[]{:S(2)}, u32[]{:S(2)}) %all-to-all-start.2) | async-done | bytes 786464 | tf_op jit(solution)/shard_map/all_to_all | solution.py:313
  88.2 0.0 copy-done.9
  88.2 0.0 copy-done.10
  88.2 0.7 mix.1
  88.9 3.8 %collective-permute-start = (bf16[24,128]{1,0:T(8,128)(2,1)S(1)}, bf16[24,128]{1,0:T(8,128)(2,1)S(1)}, u32[]{:S(2)}, u32[]{:S(2)}) collective-permute-start(bf16[24,128]{1,0:T(8,128)(2,1)S(1)} %get-tuple-element.12), channel_id=1, source_target_pairs={{0,64},{64,0},{1,65},{65,1},{2,66},{66,2},{3,67},{67,3},{4,68},{68... | collective-permute-start | bytes 18440 | tf_op jit(solution)/shard_map/ppermute | solution.py:351
  92.7 0.8 collective-permute-done
  93.5 0.6 pad_maximum_fusion
  (3 shorter events, 0.0 us)
Async XLA Ops:
  0.0 1.0 %copy-start.3 = (bf16[2,128,1024]{2,1,0:T(8,128)(2,1)S(1)}, bf16[2,128,1024]{2,1,0:T(8,128)(2,1)}, u32[]{:S(2)}) copy-start(bf16[2,128,1024]{2,1,0:T(8,128)(2,1)} %key_ref.1) | copy-start | bytes 1572868
  1.0 1.0 %copy-start.4 = (bf16[2,128,1024]{2,1,0:T(8,128)(2,1)S(1)}, bf16[2,128,1024]{2,1,0:T(8,128)(2,1)}, u32[]{:S(2)}) copy-start(bf16[2,128,1024]{2,1,0:T(8,128)(2,1)} %value_ref.1) | copy-start | bytes 1572868
  2.1 0.7 copy-start.5
  2.8 0.7 copy-start.6
  3.6 0.7 copy-start.7
  4.2 0.7 copy-start.8
  4.9 0.7 copy-start.11
  5.6 37.9 %copy-start.12 = (bf16[6144]{0:T(1024)(128)(2,1)S(1)}, bf16[6144]{0:T(1024)(128)(2,1)}, u32[]{:S(2)}) copy-start(bf16[6144]{0:T(1024)(128)(2,1)} %param.22) | copy-start | bytes 36868
  7.6 27.3 %all-to-all-start = ((bf16[64,56,128]{2,1,0:T(8,128)(2,1)}), bf16[64,56,128]{2,1,0:T(8,128)(2,1)S(1)}, u32[]{:S(2)}, u32[]{:S(2)}) async-start(bf16[64,56,128]{2,1,0:T(8,128)(2,1)} %attend.1), calls=%async_computation | async-start | bytes 1835008 | tf_op jit(solution)/shard_map/all_to_all | solution.py:313
  34.9 1.3 %copy-start.2 = (bf16[6144,96]{0,1:T(8,128)(2,1)S(1)}, bf16[6144,96]{0,1:T(8,128)(2,1)}, u32[]{:S(2)}) copy-start(bf16[6144,96]{0,1:T(8,128)(2,1)} %param.21) | copy-start | bytes 3538948
  37.9 19.1 %all-to-all-start.1 = ((bf16[64,48,128]{2,1,0:T(8,128)(2,1)}), bf16[64,48,128]{2,1,0:T(8,128)(2,1)S(1)}, u32[]{:S(2)}, u32[]{:S(2)}) async-start(bf16[64,48,128]{2,1,0:T(8,128)(2,1)} %project.1), calls=%async_computation.1 | async-start | bytes 1572864 | tf_op jit(solution)/shard_map/all_to_all | solution.py:313
  57.0 2.8 %copy-start = (bf16[6144,512]{1,0:T(8,128)(2,1)S(1)}, bf16[6144,512]{1,0:T(8,128)(2,1)}, u32[]{:S(2)}) copy-start(bf16[6144,512]{1,0:T(8,128)(2,1)} %param.25) | copy-start | bytes 18874372
  59.8 2.8 %copy-start.1 = (bf16[6144,512]{1,0:T(8,128)(2,1)S(1)}, bf16[6144,512]{1,0:T(8,128)(2,1)}, u32[]{:S(2)}) copy-start(bf16[6144,512]{1,0:T(8,128)(2,1)} %param.26) | copy-start | bytes 18874372
  62.6 25.6 %copy-start.9 = (s32[2,2]{1,0:T(2,128)S(1)}, s32[2,2]{1,0:T(2,128)}, u32[]{:S(2)}) copy-start(s32[2,2]{1,0:T(2,128)} %ids_ref.1) | copy-start | bytes 52
  62.6 25.6 %copy-start.10 = (f32[2,2]{1,0:T(2,128)S(1)}, f32[2,2]{1,0:T(2,128)}, u32[]{:S(2)}) copy-start(f32[2,2]{1,0:T(2,128)} %gates_ref.1) | copy-start | bytes 52
  69.2 19.0 %all-to-all-start.2 = ((bf16[64,48,128]{2,1,0:T(8,128)(2,1)}), bf16[64,48,128]{2,1,0:T(8,128)(2,1)S(1)}, u32[]{:S(2)}, u32[]{:S(2)}) async-start(bf16[64,48,128]{2,1,0:T(8,128)(2,1)} %get-tuple-element.9), calls=%async_computation.2 | async-start | bytes 1572864 | tf_op jit(solution)/shard_map/all_to_all | solution.py:313
  88.9 4.6 %collective-permute-start = (bf16[24,128]{1,0:T(8,128)(2,1)S(1)}, bf16[24,128]{1,0:T(8,128)(2,1)S(1)}, u32[]{:S(2)}, u32[]{:S(2)}) collective-permute-start(bf16[24,128]{1,0:T(8,128)(2,1)S(1)} %get-tuple-element.12), channel_id=1, source_target_pairs={{0,64},{64,0},{1,65},{65,1},{2,66},{66,2},{3,67},{67,3},{4,68},{68... | collective-permute-start | bytes 18440 | tf_op jit(solution)/shard_map/ppermute | solution.py:351

commit v3 on v2

--- a/solution.py
+++ b/solution.py
@@ -31,6 +31,14 @@
 ANY_BLOCK = pl.BlockSpec(memory_space=pl.ANY)
 
 
+def in_hbm(*arrays):
+    return tuple(pltpu.with_memory_space_constraint(array, pltpu.HBM) for array in arrays)
+
+
+def in_vmem(*arrays):
+    return tuple(pltpu.with_memory_space_constraint(array, pltpu.VMEM) for array in arrays)
+
+
 def last_dims(left, right):
     return lax.dot_general(
         left, right, (((1,), (1,)), ((), ())), preferred_element_type=jnp.float32
@@ -47,6 +55,7 @@
     key_ref,
     value_ref,
     out_ref,
+    mark_ref,
     query_rows,
     context_rows,
     residual_rows,
@@ -95,6 +104,7 @@
         context = context + own_weight[kv * 8 : kv * 8 + 8] * new_value[:, lanes]
         context_rows[kv * GROUP : kv * GROUP + 8, :] = context
     context = context_rows[0:HEADS, :].astype(jnp.bfloat16)
+    mark_ref[...] = context_rows[0:8, :]
     for chip in range(DEVS):
         first = COLS * chip // 128
         out_ref[chip, 0:ROWS, :] = context
@@ -108,7 +118,10 @@
     cache = pl.BlockSpec((1, CACHE_LEN, 1024), lambda step, core, cached: (core[0], 0, 0))
     return pl.pallas_call(
         attend_kernel,
-        out_shape=jax.ShapeDtypeStruct((DEVS, SENT, 128), jnp.bfloat16),
+        out_shape=(
+            jax.ShapeDtypeStruct((DEVS, SENT, 128), jnp.bfloat16),
+            jax.ShapeDtypeStruct((8, 128), jnp.float32),
+        ),
         grid_spec=pltpu.PrefetchScalarGridSpec(
             num_scalar_prefetch=2,
             grid=(1,),
@@ -120,7 +133,7 @@
                 cache,
                 cache,
             ],
-            out_specs=whole((DEVS, SENT, 128)),
+            out_specs=(whole((DEVS, SENT, 128)), whole((8, 128))),
             scratch_shapes=[
                 pltpu.VMEM((64, 128), jnp.float32),
                 pltpu.VMEM((SENT, 128), jnp.float32),
@@ -129,7 +142,32 @@
         ),
         compiler_params=pltpu.CompilerParams(vmem_limit_bytes=8 << 20),
         name="attend",
-    )(core, cached, query, new_key, new_value, residual, key_cache, value_cache)
+    )(core, *in_hbm(cached, query, new_key, new_value, residual, key_cache, value_cache))
+
+
+def fetch_kernel(after_ref, *refs):
+    count = (len(refs) - 1) // 2
+    copies = [
+        pltpu.make_async_copy(refs[i], refs[count + i], refs[-1].at[i]) for i in range(count)
+    ]
+    for copy in copies:
+        copy.start()
+    for copy in copies:
+        copy.wait()
+
+
+def fetch(after, *arrays):
+    size = sum(array.size * array.dtype.itemsize for array in arrays)
+    return pl.pallas_call(
+        fetch_kernel,
+        out_shape=tuple(pltpu.VMEM(array.shape, array.dtype) for array in arrays),
+        in_specs=[ANY_BLOCK] * (len(arrays) + 1),
+        out_specs=(VMEM_BLOCK,) * len(arrays),
+        scratch_shapes=[pltpu.SemaphoreType.DMA((len(arrays),))],
+        compiler_params=pltpu.CompilerParams(vmem_limit_bytes=1 << 20),
+        cost_estimate=pl.CostEstimate(flops=0, bytes_accessed=2 * size, transcendentals=0),
+        name="fetch",
+    )(after, *in_hbm(*arrays))
 
 
 def project_kernel(chip_ref, arrived_ref, weight_ref, out_ref, rows, context):
@@ -166,47 +204,22 @@
         ],
         compiler_params=pltpu.CompilerParams(vmem_limit_bytes=16 << 20),
         name="project",
-    )(chip, arrived, weight)
+    )(chip, arrived, *in_vmem(weight))
 
 
 def expert_kernel(
     chip_ref,
     hidden_ref,
     gain_ref,
-    gate_hbm,
-    up_hbm,
-    down_hbm,
-    out_ref,
-    own_ref,
     gate_vmem,
     up_vmem,
     down_vmem,
+    out_ref,
+    own_ref,
     flipped,
     scaled,
     result,
-    sems,
 ):
-    copies = []
-    for half in range(2):
-        for step in range(HALF_D // CHUNK):
-            part = pl.ds(step * PART, PART)
-            pair = []
-            for source, target, which in ((gate_hbm, gate_vmem, 0), (up_hbm, up_vmem, 1)):
-                copy = pltpu.make_async_copy(
-                    source.at[part, half], target.at[part, half], sems.at[which, half, step]
-                )
-                copy.start()
-                pair.append(copy)
-            copies.append(pair)
-    down_copies = []
-    for step in range(4):
-        part = pl.ds(step * (D // 4), D // 4)
-        copy = pltpu.make_async_copy(
-            down_hbm.at[:, part], down_vmem.at[:, part], sems.at[2, 0, step]
-        )
-        copy.start()
-        down_copies.append(copy)
-
     squares = jnp.zeros((128, 128), jnp.float32)
     for block in range(HALF_D // 128):
         lanes = slice(block * 128, block * 128 + 128)
@@ -226,8 +239,6 @@
     up = jnp.zeros((DEVS, UNITS), jnp.float32)
     for half in range(2):
         for step in range(HALF_D // CHUNK):
-            for copy in copies[half * (HALF_D // CHUNK) + step]:
-                copy.wait()
             rows = scaled[half * DEVS : half * DEVS + DEVS, step * CHUNK : step * CHUNK + CHUNK]
             part = slice(step * PART, step * PART + PART)
             gate = gate + jnp.dot(
@@ -242,7 +253,6 @@
     up = up * factor
     act = (gate / (1.0 + jnp.exp(-gate)) * up).astype(jnp.bfloat16)
     for step in range(4):
-        down_copies[step].wait()
         for piece in range(D // 4 // 512):
             first = step * (D // 4) + piece * 512
             block = jnp.dot(
@@ -263,20 +273,16 @@
             jax.ShapeDtypeStruct((DEVS, ROWS, 128), jnp.bfloat16),
             jax.ShapeDtypeStruct((2, HALF_D), jnp.float32),
         ),
-        in_specs=[SMEM_BLOCK, VMEM_BLOCK, VMEM_BLOCK, ANY_BLOCK, ANY_BLOCK, ANY_BLOCK],
+        in_specs=[SMEM_BLOCK] + [VMEM_BLOCK] * 5,
         out_specs=(VMEM_BLOCK, VMEM_BLOCK),
         scratch_shapes=[
-            pltpu.VMEM((DEVS, 2, HALF, UNITS), jnp.bfloat16),
-            pltpu.VMEM((DEVS, 2, HALF, UNITS), jnp.bfloat16),
-            pltpu.VMEM((UNITS, D), jnp.bfloat16),
             pltpu.VMEM((128, HALF_D), jnp.float32),
             pltpu.VMEM((128, HALF_D), jnp.bfloat16),
             pltpu.VMEM((DEVS * ROWS, 128), jnp.float32),
-            pltpu.SemaphoreType.DMA((3, 2, HALF_D // CHUNK)),
         ],
-        compiler_params=pltpu.CompilerParams(vmem_limit_bytes=40 << 20),
+        compiler_params=pltpu.CompilerParams(vmem_limit_bytes=16 << 20),
         name="experts",
-    )(chip, hidden, gain, w_gate, w_up, w_down)
+    )(chip, hidden, gain, *in_vmem(w_gate, w_up, w_down))
 
 
 def mix_kernel(core_ref, ids_ref, gates_ref, returned_ref, hidden_ref, kept_ref, given_ref):
@@ -332,19 +338,19 @@
     core = lax.axis_index("side").astype(jnp.int32).reshape(1)
     chip = lax.axis_index("dev").astype(jnp.int32).reshape(1)
     gain = norm_gain.reshape(DEVS, 2, HALF).transpose(1, 0, 2).reshape(2, HALF_D)
-    outgoing = attend(
+    outgoing, mark = attend(
         core, cached, query, new_key, new_value, residual, key_cache, value_cache
     )
-    arrived = exchange(outgoing)
-    hidden = exchange(project(chip, arrived, out_weight.T)).reshape(HALF_D, 128)
-    partial_value, own_hidden = run_experts(
-        chip,
-        hidden,
-        gain,
+    projection, gate, up, down = fetch(
+        mark,
+        out_weight.T,
         w_gate.reshape(DEVS, 2, HALF, UNITS),
         w_up.reshape(DEVS, 2, HALF, UNITS),
         w_down,
     )
+    arrived = exchange(outgoing)
+    hidden = exchange(project(chip, arrived, projection)).reshape(HALF_D, 128)
+    partial_value, own_hidden = run_experts(chip, hidden, gain, gate, up, down)
     returned = exchange(partial_value)
     own_hidden = own_hidden.reshape(2, DEVS, HALF).transpose(1, 0, 2).reshape(ROWS, 128)
     kept, given = mix(core, expert_ids, gate_weights, returned, own_hidden)

time: 94.9 us -> 93.4 us (0.984)
  waiting for transfers between devices: 42.2 us -> 27.9 us
  Pallas kernels: 11 us -> 17 us
  local copies, waits for them, and re-layouts: 13 us -> 16.7 us
  starting transfers between devices: 27.3 us -> 30.5 us
    all_to_all x3, waiting for transfers between devices: 41.4 us -> 27 us  [exchange(): return lax.all_to_all(parts, 'dev', split_axis=0, concat_axis=0, tiled=True)]
    pallas_call x1 -> x2, Pallas kernels: 2.05 us -> 10 us  [the longest x1 6.78 us: fetch(): pl.pallas_call(fetch_kernel, out_shape=tuple((pltpu.VMEM(array.shape, arr...]
    unnamed x26 -> x18, local copies, waits for them, and re-layouts: 12.4 us -> 16.2 us
    all_to_all x3, starting transfers between devices: 23.4 us -> 26.7 us  [exchange(): return lax.all_to_all(parts, 'dev', split_axis=0, concat_axis=0, tiled=True)]
    pallas_call x1, Pallas kernels: 6.57 us -> 4.65 us  [run_experts(): pl.pallas_call(expert_kernel, out_shape=(jax.ShapeDtypeStruct((DEVS, ROWS...]
  transfers between devices with their start and end apart: 4 -> 4, of which waited for: 4 -> 4; matrix products, arithmetic and copies ran while one was open for 1% -> 1% of each run, Pallas kernels for 0% -> 7%
where the time goes in v3:
time: 93.4 us; the launch traced here: 92.9 us
  starting transfers between devices  30.5 us (33%)
  waiting for transfers between devices  27.9 us (30%)
  Pallas kernels  17 us (18%)
  local copies, waits for them, and re-layouts  16.7 us (18%)
    all_to_all x3, waiting for transfers between devices, exchange(): return lax.all_to_all(parts, 'dev', split_axis=0, concat_axis=0, tiled=True)  27 us
    all_to_all x3, starting transfers between devices, exchange(): return lax.all_to_all(parts, 'dev', split_axis=0, concat_axis=0, tiled=True)  26.7 us
    unnamed x18, local copies, waits for them, and re-layouts  16.2 us
    pallas_call x1, Pallas kernels, fetch(): pl.pallas_call(fetch_kernel, out_shape=tuple((pltpu.VMEM(array.shape, arr...  6.78 us
    pallas_call x1, Pallas kernels, run_experts(): pl.pallas_call(expert_kernel, out_shape=(jax.ShapeDtypeStruct((DEVS, ROWS...  4.65 us
    ppermute x1, starting transfers between devices, local(): taken = lax.ppermute(given, 'side', [(0, 1), (1, 0)])  3.82 us
    pallas_call x1, Pallas kernels, attend(): pl.pallas_call(attend_kernel, out_shape=(jax.ShapeDtypeStruct((DEVS, SENT...  3.25 us
  transfers between devices with their start and end apart: 4, of which 4 were waited for; matrix products, arithmetic and copies ran while one was open for 1% of the time, Pallas kernels for 7%

profile of v3, /device:TPU:1, one launch (start us, length us, event | category | flops | bytes accessed | tf_op | source)
XLA Modules:
  0.0 92.9 jit_solution(17469408137201973691)
XLA Ops:
  0.0 3.2 %attend.1 = (bf16[64,56,128]{2,1,0:T(8,128)(2,1)}, f32[8,128]{1,0:T(8,128)S(1)}) custom-call(s32[1]{0:T(128)} %bitcast.core_ref, s32[2]{0:T(128)} %cached_ref.1, bf16[2,6144]{1,0:T(2,128)(2,1)} %query_ref.1, bf16[2,1024]{1,0:T(2,128)(2,1)} %new_key_ref.1, bf16[2,1024]{1,0:T(2,128)(2,1)} %new_value_ref.1, bf16[2,6144]{1,0:T(2,128)(2,1)} %residual_ref.1, ...), custom_call_target="tpu_custom_call" | custom-call | tf_op jit(solution)/shard_map/attend/pallas_call | solution.py:119
  3.3 12.0 %all-to-all-start = ((bf16[64,56,128]{2,1,0:T(8,128)(2,1)}), bf16[64,56,128]{2,1,0:T(8,128)(2,1)S(1)}, u32[]{:S(2)}, u32[]{:S(2)}) async-start(bf16[64,56,128]{2,1,0:T(8,128)(2,1)} %get-tuple-element.15), calls=%async_computation | async-start | bytes 1835008 | tf_op jit(solution)/shard_map/all_to_all | solution.py:319
  15.2 0.0 copy-start.8
  15.2 6.8 %fetch.1 = (bf16[96,6144]{1,0:T(8,128)(2,1)S(1)}, bf16[64,2,48,512]{3,2,1,0:T(8,128)(2,1)S(1)}, bf16[64,2,48,512]{3,2,1,0:T(8,128)(2,1)S(1)}, bf16[512,6144]{1,0:T(8,128)(2,1)S(1)}) custom-call(f32[8,128]{1,0:T(8,128)S(1)} %get-tuple-element.16.after_ref, bf16[96,6144]{1,0:T(8,128)(2,1)} %bitcast.22, bf16[64,2,48,512]{3,2,1,0:T(8,128)(2,1)} %bitcast.20, ...), custom_call_target="tpu_custom_call" | custom-call | bytes 40108032 | tf_op jit(solution)/shard_map/fetch/pallas_call | solution.py:161
  22.0 0.0 copy-start
  22.0 2.7 %copy-done = bf16[64,2,48,512]{3,2,1,0:T(8,128)(2,1)} copy-done((bf16[64,2,48,512]{3,2,1,0:T(8,128)(2,1)}, bf16[64,2,48,512]{3,2,1,0:T(8,128)(2,1)S(1)}, u32[]{:S(2)}) %copy-start) | copy-done | bytes 6291480
  24.7 0.0 copy-start.2
  24.7 2.6 %copy-done.2 = bf16[64,2,48,512]{3,2,1,0:T(8,128)(2,1)} copy-done((bf16[64,2,48,512]{3,2,1,0:T(8,128)(2,1)}, bf16[64,2,48,512]{3,2,1,0:T(8,128)(2,1)S(1)}, u32[]{:S(2)}) %copy-start.2) | copy-done | bytes 6291480
  27.3 0.0 copy-start.4
  27.3 2.6 %copy-done.4 = bf16[512,6144]{1,0:T(8,128)(2,1)} copy-done((bf16[512,6144]{1,0:T(8,128)(2,1)}, bf16[512,6144]{1,0:T(8,128)(2,1)S(1)}, u32[]{:S(2)}) %copy-start.4) | copy-done | bytes 6291480
  29.9 0.7 all-to-all-done.arrived_ref
  30.6 1.7 %project.1 = bf16[64,48,128]{2,1,0:T(8,128)(2,1)} custom-call(s32[1]{0:T(128)} %bitcast.2.chip_ref, bf16[64,56,128]{2,1,0:T(8,128)(2,1)S(1)} %all-to-all-done.arrived_ref, bf16[96,6144]{1,0:T(8,128)(2,1)S(1)} %get-tuple-element.17.weight_ref), custom_call_target="tpu_custom_call" | custom-call | tf_op jit(solution)/shard_map/project/pallas_call | solution.py:196
  32.2 9.1 %all-to-all-start.1 = ((bf16[64,48,128]{2,1,0:T(8,128)(2,1)}), bf16[64,48,128]{2,1,0:T(8,128)(2,1)S(1)}, u32[]{:S(2)}, u32[]{:S(2)}) async-start(bf16[64,48,128]{2,1,0:T(8,128)(2,1)} %project.1), calls=%async_computation.1 | async-start | bytes 1572864 | tf_op jit(solution)/shard_map/all_to_all | solution.py:319
  41.4 0.0 copy-done.8
  41.4 0.1 reshape.33
  41.5 0.1 reshape.34.gain_ref
  41.6 13.6 %all-to-all-done.1 = bf16[64,48,128]{2,1,0:T(8,128)(2,1)S(1)} async-done(((bf16[64,48,128]{2,1,0:T(8,128)(2,1)}), bf16[64,48,128]{2,1,0:T(8,128)(2,1)S(1)}, u32[]{:S(2)}, u32[]{:S(2)}) %all-to-all-start.1) | async-done | bytes 786464 | tf_op jit(solution)/shard_map/all_to_all | solution.py:319
  55.2 0.0 copy-start.1
  55.2 2.8 %copy-done.1 = bf16[64,2,48,512]{3,2,1,0:T(8,128)(2,1)S(1)} copy-done((bf16[64,2,48,512]{3,2,1,0:T(8,128)(2,1)S(1)}, bf16[64,2,48,512]{3,2,1,0:T(8,128)(2,1)}, u32[]{:S(2)}) %copy-start.1) | copy-done | bytes 6291480
  57.9 0.0 copy-start.3
  58.0 2.8 %copy-done.3 = bf16[64,2,48,512]{3,2,1,0:T(8,128)(2,1)S(1)} copy-done((bf16[64,2,48,512]{3,2,1,0:T(8,128)(2,1)S(1)}, bf16[64,2,48,512]{3,2,1,0:T(8,128)(2,1)}, u32[]{:S(2)}) %copy-start.3) | copy-done | bytes 6291480
  60.7 0.0 copy-start.5
  60.7 2.8 %copy-done.5 = bf16[512,6144]{1,0:T(8,128)(2,1)S(1)} copy-done((bf16[512,6144]{1,0:T(8,128)(2,1)S(1)}, bf16[512,6144]{1,0:T(8,128)(2,1)}, u32[]{:S(2)}) %copy-start.5) | copy-done | bytes 6291480
  63.5 0.0 copy-start.6
  63.5 0.0 copy-start.7
  63.5 4.7 %experts.1 = (bf16[64,48,128]{2,1,0:T(8,128)(2,1)}, f32[2,3072]{1,0:T(2,128)S(1)}) custom-call(s32[1]{0:T(128)} %bitcast.2.chip_ref, bf16[3072,128]{1,0:T(8,128)(2,1)S(1)} %bitcast.19, bf16[2,3072]{1,0:T(2,128)(2,1)S(1)} %reshape.34.gain_ref, bf16[64,2,48,512]{3,2,1,0:T(8,128)(2,1)S(1)} %copy-done.1, bf16[64,2,48,512]{3,2,1,0:T(8,128)(2,1)S(1)} %copy-done.3, ...), custom_call_target="tpu_custom_call" | custom-call | tf_op jit(solution)/shard_map/experts/pallas_call | solution.py:270
  68.2 5.6 %all-to-all-start.2 = ((bf16[64,48,128]{2,1,0:T(8,128)(2,1)}), bf16[64,48,128]{2,1,0:T(8,128)(2,1)S(1)}, u32[]{:S(2)}, u32[]{:S(2)}) async-start(bf16[64,48,128]{2,1,0:T(8,128)(2,1)} %get-tuple-element.21), calls=%async_computation.2 | async-start | bytes 1572864 | tf_op jit(solution)/shard_map/all_to_all | solution.py:319
  73.8 0.1 reshape.35
  73.9 0.1 copy.17
  73.9 0.1 reshape.36.hidden_ref
  74.1 12.8 %all-to-all-done.2.returned_ref = bf16[64,48,128]{2,1,0:T(8,128)(2,1)S(1)} async-done(((bf16[64,48,128]{2,1,0:T(8,128)(2,1)}), bf16[64,48,128]{2,1,0:T(8,128)(2,1)S(1)}, u32[]{:S(2)}, u32[]{:S(2)}) %all-to-all-start.2) | async-done | bytes 786464 | tf_op jit(solution)/shard_map/all_to_all | solution.py:319
  86.9 0.0 copy-done.6
  86.9 0.0 copy-done.7
  86.9 0.7 mix.1
  87.5 3.8 %collective-permute-start = (bf16[24,128]{1,0:T(8,128)(2,1)S(1)}, bf16[24,128]{1,0:T(8,128)(2,1)S(1)}, u32[]{:S(2)}, u32[]{:S(2)}) collective-permute-start(bf16[24,128]{1,0:T(8,128)(2,1)S(1)} %get-tuple-element.24), channel_id=1, source_target_pairs={{0,64},{64,0},{1,65},{65,1},{2,66},{66,2},{3,67},{67,3},{4,68},{68... | collective-permute-start | bytes 18440 | tf_op jit(solution)/shard_map/ppermute | solution.py:357
  91.4 0.8 collective-permute-done
  92.2 0.6 pad_maximum_fusion
  (3 shorter events, 0.0 us)
Async XLA Ops:
  3.3 27.3 %all-to-all-start = ((bf16[64,56,128]{2,1,0:T(8,128)(2,1)}), bf16[64,56,128]{2,1,0:T(8,128)(2,1)S(1)}, u32[]{:S(2)}, u32[]{:S(2)}) async-start(bf16[64,56,128]{2,1,0:T(8,128)(2,1)} %get-tuple-element.15), calls=%async_computation | async-start | bytes 1835008 | tf_op jit(solution)/shard_map/all_to_all | solution.py:319
  15.2 26.1 %copy-start.8 = (bf16[6144]{0:T(1024)(128)(2,1)S(1)}, bf16[6144]{0:T(1024)(128)(2,1)}, u32[]{:S(2)}) copy-start(bf16[6144]{0:T(1024)(128)(2,1)} %param.22) | copy-start | bytes 36868
  22.0 2.7 %copy-start = (bf16[64,2,48,512]{3,2,1,0:T(8,128)(2,1)}, bf16[64,2,48,512]{3,2,1,0:T(8,128)(2,1)S(1)}, u32[]{:S(2)}) copy-start(bf16[64,2,48,512]{3,2,1,0:T(8,128)(2,1)S(1)} %get-tuple-element.18.gate_vmem) | copy-start | bytes 18874372
  24.7 2.6 %copy-start.2 = (bf16[64,2,48,512]{3,2,1,0:T(8,128)(2,1)}, bf16[64,2,48,512]{3,2,1,0:T(8,128)(2,1)S(1)}, u32[]{:S(2)}) copy-start(bf16[64,2,48,512]{3,2,1,0:T(8,128)(2,1)S(1)} %get-tuple-element.19.up_vmem) | copy-start | bytes 18874372
  27.3 2.6 %copy-start.4 = (bf16[512,6144]{1,0:T(8,128)(2,1)}, bf16[512,6144]{1,0:T(8,128)(2,1)S(1)}, u32[]{:S(2)}) copy-start(bf16[512,6144]{1,0:T(8,128)(2,1)S(1)} %get-tuple-element.20.down_vmem) | copy-start | bytes 18874372
  32.2 22.9 %all-to-all-start.1 = ((bf16[64,48,128]{2,1,0:T(8,128)(2,1)}), bf16[64,48,128]{2,1,0:T(8,128)(2,1)S(1)}, u32[]{:S(2)}, u32[]{:S(2)}) async-start(bf16[64,48,128]{2,1,0:T(8,128)(2,1)} %project.1), calls=%async_computation.1 | async-start | bytes 1572864 | tf_op jit(solution)/shard_map/all_to_all | solution.py:319
  55.2 2.8 %copy-start.1 = (bf16[64,2,48,512]{3,2,1,0:T(8,128)(2,1)S(1)}, bf16[64,2,48,512]{3,2,1,0:T(8,128)(2,1)}, u32[]{:S(2)}) copy-start(bf16[64,2,48,512]{3,2,1,0:T(8,128)(2,1)} %copy-done) | copy-start | bytes 18874372
  57.9 2.8 %copy-start.3 = (bf16[64,2,48,512]{3,2,1,0:T(8,128)(2,1)S(1)}, bf16[64,2,48,512]{3,2,1,0:T(8,128)(2,1)}, u32[]{:S(2)}) copy-start(bf16[64,2,48,512]{3,2,1,0:T(8,128)(2,1)} %copy-done.2) | copy-start | bytes 18874372
  60.7 2.8 %copy-start.5 = (bf16[512,6144]{1,0:T(8,128)(2,1)S(1)}, bf16[512,6144]{1,0:T(8,128)(2,1)}, u32[]{:S(2)}) copy-start(bf16[512,6144]{1,0:T(8,128)(2,1)} %copy-done.4) | copy-start | bytes 18874372
  63.5 23.3 %copy-start.6 = (s32[2,2]{1,0:T(2,128)S(1)}, s32[2,2]{1,0:T(2,128)}, u32[]{:S(2)}) copy-start(s32[2,2]{1,0:T(2,128)} %ids_ref.1) | copy-start | bytes 52
  63.5 23.3 %copy-start.7 = (f32[2,2]{1,0:T(2,128)S(1)}, f32[2,2]{1,0:T(2,128)}, u32[]{:S(2)}) copy-start(f32[2,2]{1,0:T(2,128)} %gates_ref.1) | copy-start | bytes 52
  68.2 18.7 %all-to-all-start.2 = ((bf16[64,48,128]{2,1,0:T(8,128)(2,1)}), bf16[64,48,128]{2,1,0:T(8,128)(2,1)S(1)}, u32[]{:S(2)}, u32[]{:S(2)}) async-start(bf16[64,48,128]{2,1,0:T(8,128)(2,1)} %get-tuple-element.21), calls=%async_computation.2 | async-start | bytes 1572864 | tf_op jit(solution)/shard_map/all_to_all | solution.py:319
  87.5 4.6 %collective-permute-start = (bf16[24,128]{1,0:T(8,128)(2,1)S(1)}, bf16[24,128]{1,0:T(8,128)(2,1)S(1)}, u32[]{:S(2)}, u32[]{:S(2)}) collective-permute-start(bf16[24,128]{1,0:T(8,128)(2,1)S(1)} %get-tuple-element.24), channel_id=1, source_target_pairs={{0,64},{64,0},{1,65},{65,1},{2,66},{66,2},{3,67},{67,3},{4,68},{68... | collective-permute-start | bytes 18440 | tf_op jit(solution)/shard_map/ppermute | solution.py:357

commit v4 on v2

--- a/solution.py
+++ b/solution.py
@@ -31,6 +31,14 @@
 ANY_BLOCK = pl.BlockSpec(memory_space=pl.ANY)
 
 
+def in_hbm(*arrays):
+    return tuple(pltpu.with_memory_space_constraint(array, pltpu.HBM) for array in arrays)
+
+
+def in_vmem(*arrays):
+    return tuple(pltpu.with_memory_space_constraint(array, pltpu.VMEM) for array in arrays)
+
+
 def last_dims(left, right):
     return lax.dot_general(
         left, right, (((1,), (1,)), ((), ())), preferred_element_type=jnp.float32
@@ -47,6 +55,7 @@
     key_ref,
     value_ref,
     out_ref,
+    mark_ref,
     query_rows,
     context_rows,
     residual_rows,
@@ -95,6 +104,7 @@
         context = context + own_weight[kv * 8 : kv * 8 + 8] * new_value[:, lanes]
         context_rows[kv * GROUP : kv * GROUP + 8, :] = context
     context = context_rows[0:HEADS, :].astype(jnp.bfloat16)
+    mark_ref[...] = context_rows[0:8, :]
     for chip in range(DEVS):
         first = COLS * chip // 128
         out_ref[chip, 0:ROWS, :] = context
@@ -108,7 +118,10 @@
     cache = pl.BlockSpec((1, CACHE_LEN, 1024), lambda step, core, cached: (core[0], 0, 0))
     return pl.pallas_call(
         attend_kernel,
-        out_shape=jax.ShapeDtypeStruct((DEVS, SENT, 128), jnp.bfloat16),
+        out_shape=(
+            jax.ShapeDtypeStruct((DEVS, SENT, 128), jnp.bfloat16),
+            jax.ShapeDtypeStruct((8, 128), jnp.float32),
+        ),
         grid_spec=pltpu.PrefetchScalarGridSpec(
             num_scalar_prefetch=2,
             grid=(1,),
@@ -120,7 +133,7 @@
                 cache,
                 cache,
             ],
-            out_specs=whole((DEVS, SENT, 128)),
+            out_specs=(whole((DEVS, SENT, 128)), whole((8, 128))),
             scratch_shapes=[
                 pltpu.VMEM((64, 128), jnp.float32),
                 pltpu.VMEM((SENT, 128), jnp.float32),
@@ -129,7 +142,32 @@
         ),
         compiler_params=pltpu.CompilerParams(vmem_limit_bytes=8 << 20),
         name="attend",
-    )(core, cached, query, new_key, new_value, residual, key_cache, value_cache)
+    )(core, *in_hbm(cached, query, new_key, new_value, residual, key_cache, value_cache))
+
+
+def fetch_kernel(after_ref, *refs):
+    count = (len(refs) - 1) // 2
+    copies = [
+        pltpu.make_async_copy(refs[i], refs[count + i], refs[-1].at[i]) for i in range(count)
+    ]
+    for copy in copies:
+        copy.start()
+    for copy in copies:
+        copy.wait()
+
+
+def fetch(after, *arrays):
+    size = sum(array.size * array.dtype.itemsize for array in arrays)
+    return pl.pallas_call(
+        fetch_kernel,
+        out_shape=tuple(pltpu.VMEM(array.shape, array.dtype) for array in arrays),
+        in_specs=[ANY_BLOCK] * (len(arrays) + 1),
+        out_specs=(VMEM_BLOCK,) * len(arrays),
+        scratch_shapes=[pltpu.SemaphoreType.DMA((len(arrays),))],
+        compiler_params=pltpu.CompilerParams(vmem_limit_bytes=1 << 20),
+        cost_estimate=pl.CostEstimate(flops=0, bytes_accessed=2 * size, transcendentals=0),
+        name="fetch",
+    )(after, *in_hbm(*arrays))
 
 
 def project_kernel(chip_ref, arrived_ref, weight_ref, out_ref, rows, context):
@@ -166,7 +204,7 @@
         ],
         compiler_params=pltpu.CompilerParams(vmem_limit_bytes=16 << 20),
         name="project",
-    )(chip, arrived, weight)
+    )(chip, arrived, *in_vmem(weight))
 
 
 def expert_kernel(
@@ -276,7 +314,7 @@
         ],
         compiler_params=pltpu.CompilerParams(vmem_limit_bytes=40 << 20),
         name="experts",
-    )(chip, hidden, gain, w_gate, w_up, w_down)
+    )(chip, hidden, gain, *in_hbm(w_gate, w_up, w_down))
 
 
 def mix_kernel(core_ref, ids_ref, gates_ref, returned_ref, hidden_ref, kept_ref, given_ref):
@@ -331,12 +369,14 @@
 ):
     core = lax.axis_index("side").astype(jnp.int32).reshape(1)
     chip = lax.axis_index("dev").astype(jnp.int32).reshape(1)
-    gain = norm_gain.reshape(DEVS, 2, HALF).transpose(1, 0, 2).reshape(2, HALF_D)
-    outgoing = attend(
+    outgoing, mark = attend(
         core, cached, query, new_key, new_value, residual, key_cache, value_cache
     )
+    norm_gain, mark = lax.optimization_barrier((norm_gain, mark))
+    gain = norm_gain.reshape(DEVS, 2, HALF).transpose(1, 0, 2).reshape(2, HALF_D)
+    (projection,) = fetch(mark, out_weight.T)
     arrived = exchange(outgoing)
-    hidden = exchange(project(chip, arrived, out_weight.T)).reshape(HALF_D, 128)
+    hidden = exchange(project(chip, arrived, projection)).reshape(HALF_D, 128)
     partial_value, own_hidden = run_experts(
         chip,
         hidden,

time: 94.9 us -> 85.3 us (0.90)
  local copies, waits for them, and re-layouts: 13 us -> 0.52 us
  Pallas kernels: 11 us -> 15.3 us
  waiting for transfers between devices: 42.2 us -> 40.9 us
    unnamed x26 -> x6, local copies, waits for them, and re-layouts: 12.4 us -> 0.01 us
    pallas_call x1 -> x2, Pallas kernels: 2.05 us -> 4.67 us  [the longest x1 3.39 us: attend(): pl.pallas_call(attend_kernel, out_shape=(jax.ShapeDtypeStruct((DEVS, SENT...]
    pallas_call x1, Pallas kernels: 6.57 us -> 8.3 us  [run_experts(): pl.pallas_call(expert_kernel, out_shape=(jax.ShapeDtypeStruct((DEVS, ROWS...]
    all_to_all x3, waiting for transfers between devices: 41.4 us -> 40.1 us  [exchange(): return lax.all_to_all(parts, 'dev', split_axis=0, concat_axis=0, tiled=True)]
  transfers between devices with their start and end apart: 4 -> 4, of which waited for: 4 -> 4; matrix products, arithmetic and copies ran while one was open for 1% -> 1% of each run, Pallas kernels for 0% -> 2%
where the time goes in v4:
time: 85.3 us; the launch traced here: 84.8 us
  waiting for transfers between devices  40.9 us (48%)
  starting transfers between devices  27.3 us (32%)
  Pallas kernels  15.3 us (18%)
    all_to_all x3, waiting for transfers between devices, exchange(): return lax.all_to_all(parts, 'dev', split_axis=0, concat_axis=0, tiled=True)  40.1 us
    all_to_all x3, starting transfers between devices, exchange(): return lax.all_to_all(parts, 'dev', split_axis=0, concat_axis=0, tiled=True)  23.5 us
    pallas_call x1, Pallas kernels, run_experts(): pl.pallas_call(expert_kernel, out_shape=(jax.ShapeDtypeStruct((DEVS, ROWS...  8.3 us
    ppermute x1, starting transfers between devices, local(): taken = lax.ppermute(given, 'side', [(0, 1), (1, 0)])  3.82 us
    pallas_call x1, Pallas kernels, attend(): pl.pallas_call(attend_kernel, out_shape=(jax.ShapeDtypeStruct((DEVS, SENT...  3.39 us
  transfers between devices with their start and end apart: 4, of which 4 were waited for; matrix products, arithmetic and copies ran while one was open for 1% of the time, Pallas kernels for 2%

profile of v4, /device:TPU:1, one launch (start us, length us, event | category | flops | bytes accessed | tf_op | source)
XLA Modules:
  0.0 84.8 jit_solution(15912583241660302285)
XLA Ops:
  0.0 0.0 copy-start.2
  0.0 3.4 %attend.1 = (bf16[64,56,128]{2,1,0:T(8,128)(2,1)}, f32[8,128]{1,0:T(8,128)S(1)}) custom-call(s32[1]{0:T(128)} %bitcast.core_ref, s32[2]{0:T(128)} %cached_ref.1, bf16[2,6144]{1,0:T(2,128)(2,1)} %query_ref.1, bf16[2,1024]{1,0:T(2,128)(2,1)} %new_key_ref.1, bf16[2,1024]{1,0:T(2,128)(2,1)} %new_value_ref.1, bf16[2,6144]{1,0:T(2,128)(2,1)} %residual_ref.1, ...), custom_call_target="tpu_custom_call" | custom-call | tf_op jit(solution)/shard_map/attend/pallas_call | solution.py:119
  3.4 12.0 %all-to-all-start = ((bf16[64,56,128]{2,1,0:T(8,128)(2,1)}), bf16[64,56,128]{2,1,0:T(8,128)(2,1)S(1)}, u32[]{:S(2)}, u32[]{:S(2)}) async-start(bf16[64,56,128]{2,1,0:T(8,128)(2,1)} %get-tuple-element.13), calls=%async_computation | async-start | bytes 1835008 | tf_op jit(solution)/shard_map/all_to_all | solution.py:351
  15.4 1.3 %fetch.1.weight_ref = bf16[96,6144]{1,0:T(8,128)(2,1)S(1)} custom-call(f32[8,128]{1,0:T(8,128)S(1)} %get-tuple-element.15.after_ref, bf16[96,6144]{1,0:T(8,128)(2,1)} %bitcast.22), custom_call_target="tpu_custom_call" | custom-call | bytes 2359296 | tf_op jit(solution)/shard_map/fetch/pallas_call | solution.py:161
  16.7 14.0 %all-to-all-done.arrived_ref = bf16[64,56,128]{2,1,0:T(8,128)(2,1)S(1)} async-done(((bf16[64,56,128]{2,1,0:T(8,128)(2,1)}), bf16[64,56,128]{2,1,0:T(8,128)(2,1)S(1)}, u32[]{:S(2)}, u32[]{:S(2)}) %all-to-all-start) | async-done | bytes 917536 | tf_op jit(solution)/shard_map/all_to_all | solution.py:351
  30.7 1.7 %project.1 = bf16[64,48,128]{2,1,0:T(8,128)(2,1)} custom-call(s32[1]{0:T(128)} %bitcast.2.chip_ref, bf16[64,56,128]{2,1,0:T(8,128)(2,1)S(1)} %all-to-all-done.arrived_ref, bf16[96,6144]{1,0:T(8,128)(2,1)S(1)} %fetch.1.weight_ref), custom_call_target="tpu_custom_call" | custom-call | tf_op jit(solution)/shard_map/project/pallas_call | solution.py:196
  32.4 5.6 %all-to-all-start.1 = ((bf16[64,48,128]{2,1,0:T(8,128)(2,1)}), bf16[64,48,128]{2,1,0:T(8,128)(2,1)S(1)}, u32[]{:S(2)}, u32[]{:S(2)}) async-start(bf16[64,48,128]{2,1,0:T(8,128)(2,1)} %project.1), calls=%async_computation.1 | async-start | bytes 1572864 | tf_op jit(solution)/shard_map/all_to_all | solution.py:351
  38.0 0.0 copy-done.2
  38.0 0.1 reshape.31
  38.1 0.1 reshape.32.gain_ref
  38.2 13.3 %all-to-all-done.1 = bf16[64,48,128]{2,1,0:T(8,128)(2,1)S(1)} async-done(((bf16[64,48,128]{2,1,0:T(8,128)(2,1)}), bf16[64,48,128]{2,1,0:T(8,128)(2,1)S(1)}, u32[]{:S(2)}, u32[]{:S(2)}) %all-to-all-start.1) | async-done | bytes 786464 | tf_op jit(solution)/shard_map/all_to_all | solution.py:351
  51.5 0.0 copy-start
  51.5 0.0 copy-start.1
  51.5 8.3 %experts.1 = (bf16[64,48,128]{2,1,0:T(8,128)(2,1)}, f32[2,3072]{1,0:T(2,128)S(1)}) custom-call(s32[1]{0:T(128)} %bitcast.2.chip_ref, bf16[3072,128]{1,0:T(8,128)(2,1)S(1)} %bitcast.19, bf16[2,3072]{1,0:T(2,128)(2,1)S(1)} %reshape.32.gain_ref, bf16[64,2,48,512]{3,2,1,0:T(8,128)(2,1)} %bitcast.20, bf16[64,2,48,512]{3,2,1,0:T(8,128)(2,1)} %bitcast.21, ...), custom_call_target="tpu_custom_call" | custom-call | tf_op jit(solution)/shard_map/experts/pallas_call | solution.py:298
  59.8 5.9 %all-to-all-start.2 = ((bf16[64,48,128]{2,1,0:T(8,128)(2,1)}), bf16[64,48,128]{2,1,0:T(8,128)(2,1)S(1)}, u32[]{:S(2)}, u32[]{:S(2)}) async-start(bf16[64,48,128]{2,1,0:T(8,128)(2,1)} %get-tuple-element.17), calls=%async_computation.2 | async-start | bytes 1572864 | tf_op jit(solution)/shard_map/all_to_all | solution.py:351
  65.7 0.1 reshape.35
  65.8 0.1 copy.17
  65.9 0.1 reshape.36.hidden_ref
  66.0 12.8 %all-to-all-done.2.returned_ref = bf16[64,48,128]{2,1,0:T(8,128)(2,1)S(1)} async-done(((bf16[64,48,128]{2,1,0:T(8,128)(2,1)}), bf16[64,48,128]{2,1,0:T(8,128)(2,1)S(1)}, u32[]{:S(2)}, u32[]{:S(2)}) %all-to-all-start.2) | async-done | bytes 786464 | tf_op jit(solution)/shard_map/all_to_all | solution.py:351
  78.8 0.0 copy-done
  78.8 0.0 copy-done.1
  78.8 0.7 mix.1
  79.5 3.8 %collective-permute-start = (bf16[24,128]{1,0:T(8,128)(2,1)S(1)}, bf16[24,128]{1,0:T(8,128)(2,1)S(1)}, u32[]{:S(2)}, u32[]{:S(2)}) collective-permute-start(bf16[24,128]{1,0:T(8,128)(2,1)S(1)} %get-tuple-element.20), channel_id=1, source_target_pairs={{0,64},{64,0},{1,65},{65,1},{2,66},{66,2},{3,67},{67,3},{4,68},{68... | collective-permute-start | bytes 18440 | tf_op jit(solution)/shard_map/ppermute | solution.py:391
  83.3 0.8 collective-permute-done
  84.2 0.6 pad_maximum_fusion
  (3 shorter events, 0.0 us)
Async XLA Ops:
  0.0 38.0 %copy-start.2 = (bf16[6144]{0:T(1024)(128)(2,1)S(1)}, bf16[6144]{0:T(1024)(128)(2,1)}, u32[]{:S(2)}) copy-start(bf16[6144]{0:T(1024)(128)(2,1)} %param.22) | copy-start | bytes 36868
  3.4 27.3 %all-to-all-start = ((bf16[64,56,128]{2,1,0:T(8,128)(2,1)}), bf16[64,56,128]{2,1,0:T(8,128)(2,1)S(1)}, u32[]{:S(2)}, u32[]{:S(2)}) async-start(bf16[64,56,128]{2,1,0:T(8,128)(2,1)} %get-tuple-element.13), calls=%async_computation | async-start | bytes 1835008 | tf_op jit(solution)/shard_map/all_to_all | solution.py:351
  32.4 19.1 %all-to-all-start.1 = ((bf16[64,48,128]{2,1,0:T(8,128)(2,1)}), bf16[64,48,128]{2,1,0:T(8,128)(2,1)S(1)}, u32[]{:S(2)}, u32[]{:S(2)}) async-start(bf16[64,48,128]{2,1,0:T(8,128)(2,1)} %project.1), calls=%async_computation.1 | async-start | bytes 1572864 | tf_op jit(solution)/shard_map/all_to_all | solution.py:351
  51.5 27.3 %copy-start = (s32[2,2]{1,0:T(2,128)S(1)}, s32[2,2]{1,0:T(2,128)}, u32[]{:S(2)}) copy-start(s32[2,2]{1,0:T(2,128)} %ids_ref.1) | copy-start | bytes 52
  51.5 27.3 %copy-start.1 = (f32[2,2]{1,0:T(2,128)S(1)}, f32[2,2]{1,0:T(2,128)}, u32[]{:S(2)}) copy-start(f32[2,2]{1,0:T(2,128)} %gates_ref.1) | copy-start | bytes 52
  59.8 19.0 %all-to-all-start.2 = ((bf16[64,48,128]{2,1,0:T(8,128)(2,1)}), bf16[64,48,128]{2,1,0:T(8,128)(2,1)S(1)}, u32[]{:S(2)}, u32[]{:S(2)}) async-start(bf16[64,48,128]{2,1,0:T(8,128)(2,1)} %get-tuple-element.17), calls=%async_computation.2 | async-start | bytes 1572864 | tf_op jit(solution)/shard_map/all_to_all | solution.py:351
  79.5 4.6 %collective-permute-start = (bf16[24,128]{1,0:T(8,128)(2,1)S(1)}, bf16[24,128]{1,0:T(8,128)(2,1)S(1)}, u32[]{:S(2)}, u32[]{:S(2)}) collective-permute-start(bf16[24,128]{1,0:T(8,128)(2,1)S(1)} %get-tuple-element.20), channel_id=1, source_target_pairs={{0,64},{64,0},{1,65},{65,1},{2,66},{66,2},{3,67},{67,3},{4,68},{68... | collective-permute-start | bytes 18440 | tf_op jit(solution)/shard_map/ppermute | solution.py:391

commit v5 on v3

--- a/solution.py
+++ b/solution.py
@@ -23,6 +23,7 @@
 HALF_D = D // 2
 CHUNK = 768
 PART = CHUNK // HALF
+EARLY = 3
 
 epsilon = 1e-05
 
@@ -170,7 +171,60 @@
     )(after, *in_hbm(*arrays))
 
 
-def project_kernel(chip_ref, arrived_ref, weight_ref, out_ref, rows, context):
+def early_kernel(after_ref, gate_hbm, out_ref, sems):
+    copies = [
+        pltpu.make_async_copy(
+            gate_hbm.at[pl.ds(step * PART, PART), 0], out_ref.at[step], sems.at[step]
+        )
+        for step in range(EARLY)
+    ]
+    for copy in copies:
+        copy.start()
+    for copy in copies:
+        copy.wait()
+
+
+def fetch_early(after, w_gate):
+    return pl.pallas_call(
+        early_kernel,
+        out_shape=pltpu.VMEM((EARLY, PART, HALF, UNITS), w_gate.dtype),
+        in_specs=[ANY_BLOCK] * 2,
+        out_specs=VMEM_BLOCK,
+        scratch_shapes=[pltpu.SemaphoreType.DMA((EARLY,))],
+        compiler_params=pltpu.CompilerParams(vmem_limit_bytes=1 << 20),
+        name="fetch_early",
+    )(after, *in_hbm(w_gate))
+
+
+def half_kernel(core_ref, after_ref, down_hbm, out_ref, sems):
+    first = core_ref[0] * HALF_D
+    copies = [
+        pltpu.make_async_copy(
+            down_hbm.at[pl.ds(step * 128, 128), pl.ds(pl.multiple_of(first, HALF_D), HALF_D)],
+            out_ref.at[pl.ds(step * 128, 128)],
+            sems.at[step],
+        )
+        for step in range(4)
+    ]
+    for copy in copies:
+        copy.start()
+    for copy in copies:
+        copy.wait()
+
+
+def fetch_half(core, after, w_down):
+    return pl.pallas_call(
+        half_kernel,
+        out_shape=pltpu.VMEM((UNITS, HALF_D), w_down.dtype),
+        in_specs=[SMEM_BLOCK, ANY_BLOCK, ANY_BLOCK],
+        out_specs=VMEM_BLOCK,
+        scratch_shapes=[pltpu.SemaphoreType.DMA((4,))],
+        compiler_params=pltpu.CompilerParams(vmem_limit_bytes=1 << 20),
+        name="fetch_half",
+    )(core, after, *in_hbm(w_down))
+
+
+def project_kernel(chip_ref, arrived_ref, weight_ref, out_ref, mark_ref, rows, context):
     for source in range(DEVS):
         rows[source * SENT : source * SENT + SENT, :] = arrived_ref[source].astype(jnp.float32)
     for head in range(HEADS):
@@ -188,6 +242,7 @@
     hidden = rows[pl.ds(first, COLS), :] + projected
     lane = lax.broadcasted_iota(jnp.int32, (HALF, 128), 1)
     packed = jnp.where(lane < DEVS, hidden[0:HALF], hidden[HALF:COLS]).astype(jnp.bfloat16)
+    mark_ref[...] = hidden[0:8]
     for target in range(DEVS):
         out_ref[target] = packed
 
@@ -195,9 +250,12 @@
 def project(chip, arrived, weight):
     return pl.pallas_call(
         project_kernel,
-        out_shape=jax.ShapeDtypeStruct((DEVS, HALF, 128), jnp.bfloat16),
+        out_shape=(
+            jax.ShapeDtypeStruct((DEVS, HALF, 128), jnp.bfloat16),
+            jax.ShapeDtypeStruct((8, 128), jnp.float32),
+        ),
         in_specs=[SMEM_BLOCK, VMEM_BLOCK, VMEM_BLOCK],
-        out_specs=VMEM_BLOCK,
+        out_specs=(VMEM_BLOCK, VMEM_BLOCK),
         scratch_shapes=[
             pltpu.VMEM((DEVS * SENT, 128), jnp.float32),
             pltpu.VMEM((DEVS, D), jnp.bfloat16),
@@ -211,15 +269,33 @@
     chip_ref,
     hidden_ref,
     gain_ref,
+    early_ref,
+    gate_hbm,
+    up_hbm,
+    act_ref,
+    own_ref,
     gate_vmem,
     up_vmem,
-    down_vmem,
-    out_ref,
-    own_ref,
     flipped,
     scaled,
-    result,
+    sems,
 ):
+    pieces = [(half, step) for half in range(2) for step in range(HALF_D // CHUNK)]
+    copies = {}
+    for index, (half, step) in enumerate(pieces):
+        part = pl.ds(step * PART, PART)
+        for which, source, target in ((0, gate_hbm, gate_vmem), (1, up_hbm, up_vmem)):
+            if which == 0 and index < EARLY:
+                continue
+            copies[which, index] = pltpu.make_async_copy(
+                source.at[part, half], target.at[part, half], sems.at[which, index]
+            )
+    for index in range(EARLY, len(pieces)):
+        copies[0, index].start()
+        copies[1, index].start()
+    for index in range(EARLY):
+        copies[1, index].start()
+
     squares = jnp.zeros((128, 128), jnp.float32)
     for block in range(HALF_D // 128):
         lanes = slice(block * 128, block * 128 + 128)
@@ -237,86 +313,121 @@
 
     gate = jnp.zeros((DEVS, UNITS), jnp.float32)
     up = jnp.zeros((DEVS, UNITS), jnp.float32)
-    for half in range(2):
-        for step in range(HALF_D // CHUNK):
-            rows = scaled[half * DEVS : half * DEVS + DEVS, step * CHUNK : step * CHUNK + CHUNK]
-            part = slice(step * PART, step * PART + PART)
-            gate = gate + jnp.dot(
-                rows,
-                gate_vmem[part, half].reshape(CHUNK, UNITS),
-                preferred_element_type=jnp.float32,
-            )
-            up = up + jnp.dot(
-                rows, up_vmem[part, half].reshape(CHUNK, UNITS), preferred_element_type=jnp.float32
-            )
+
+    def product(index, weights):
+        half, step = pieces[index]
+        rows = scaled[half * DEVS : half * DEVS + DEVS, step * CHUNK : step * CHUNK + CHUNK]
+        return jnp.dot(rows, weights.reshape(CHUNK, UNITS), preferred_element_type=jnp.float32)
+
+    def part_of(ref, index):
+        half, step = pieces[index]
+        return ref[step * PART : step * PART + PART, half]
+
+    for index in range(EARLY):
+        gate = gate + product(index, early_ref[index])
+    for index in list(range(EARLY, len(pieces))) + list(range(EARLY)):
+        if index >= EARLY:
+            copies[0, index].wait()
+            gate = gate + product(index, part_of(gate_vmem, index))
+        copies[1, index].wait()
+        up = up + product(index, part_of(up_vmem, index))
     gate = gate * factor
     up = up * factor
-    act = (gate / (1.0 + jnp.exp(-gate)) * up).astype(jnp.bfloat16)
-    for step in range(4):
-        for piece in range(D // 4 // 512):
-            first = step * (D // 4) + piece * 512
-            block = jnp.dot(
-                act, down_vmem[:, first : first + 512], preferred_element_type=jnp.float32
-            )
-            for column in range(4):
-                result[pl.ds(first // 128 + column, DEVS, stride=ROWS), :] = block[
-                    :, column * 128 : column * 128 + 128
-                ]
+    act_ref[...] = (gate / (1.0 + jnp.exp(-gate)) * up).astype(jnp.bfloat16)
+
+
+def expert_units(chip, hidden, gain, early, w_gate, w_up):
+    return pl.pallas_call(
+        expert_kernel,
+        out_shape=(
+            jax.ShapeDtypeStruct((DEVS, UNITS), jnp.bfloat16),
+            jax.ShapeDtypeStruct((2, HALF_D), jnp.float32),
+        ),
+        in_specs=[SMEM_BLOCK, VMEM_BLOCK, VMEM_BLOCK, VMEM_BLOCK, ANY_BLOCK, ANY_BLOCK],
+        out_specs=(VMEM_BLOCK, VMEM_BLOCK),
+        scratch_shapes=[
+            pltpu.VMEM((DEVS, 2, HALF, UNITS), jnp.bfloat16),
+            pltpu.VMEM((DEVS, 2, HALF, UNITS), jnp.bfloat16),
+            pltpu.VMEM((128, HALF_D), jnp.float32),
+            pltpu.VMEM((128, HALF_D), jnp.bfloat16),
+            pltpu.SemaphoreType.DMA((2, 2 * HALF_D // CHUNK)),
+        ],
+        compiler_params=pltpu.CompilerParams(vmem_limit_bytes=24 << 20),
+        name="expert_units",
+    )(chip, hidden, gain, *in_vmem(early), *in_hbm(w_gate, w_up))
+
+
+def down_kernel(core_ref, act_ref, other_ref, down_ref, out_ref, both, result):
+    core = core_ref[0]
+    both[pl.ds(pl.multiple_of(core * DEVS, DEVS), DEVS), :] = act_ref[...]
+    both[pl.ds(pl.multiple_of((1 - core) * DEVS, DEVS), DEVS), :] = other_ref[...]
+    act = both[...]
+    for first in range(0, HALF_D, 512):
+        block = jnp.dot(act, down_ref[:, first : first + 512], preferred_element_type=jnp.float32)
+        for column in range(4):
+            row = first // 128 + column
+            lanes = slice(column * 128, column * 128 + 128)
+            result[pl.ds(row, DEVS, stride=ROWS), :] = block[0:DEVS, lanes]
+            result[pl.ds(row + ROWS // 2, DEVS, stride=ROWS), :] = block[DEVS:128, lanes]
     for target in range(DEVS):
         out_ref[target] = result[target * ROWS : target * ROWS + ROWS, :].astype(jnp.bfloat16)
 
 
-def run_experts(chip, hidden, gain, w_gate, w_up, w_down):
-    return pl.pallas_call(
-        expert_kernel,
-        out_shape=(
-            jax.ShapeDtypeStruct((DEVS, ROWS, 128), jnp.bfloat16),
-            jax.ShapeDtypeStruct((2, HALF_D), jnp.float32),
-        ),
-        in_specs=[SMEM_BLOCK] + [VMEM_BLOCK] * 5,
-        out_specs=(VMEM_BLOCK, VMEM_BLOCK),
+def expert_down(core, act, other, w_down):
+    return pl.pallas_call(
+        down_kernel,
+        out_shape=jax.ShapeDtypeStruct((DEVS, ROWS, 128), jnp.bfloat16),
+        in_specs=[SMEM_BLOCK, VMEM_BLOCK, VMEM_BLOCK, VMEM_BLOCK],
+        out_specs=VMEM_BLOCK,
         scratch_shapes=[
-            pltpu.VMEM((128, HALF_D), jnp.float32),
-            pltpu.VMEM((128, HALF_D), jnp.bfloat16),
+            pltpu.VMEM((128, UNITS), jnp.bfloat16),
             pltpu.VMEM((DEVS * ROWS, 128), jnp.float32),
         ],
         compiler_params=pltpu.CompilerParams(vmem_limit_bytes=16 << 20),
-        name="experts",
-    )(chip, hidden, gain, *in_vmem(w_gate, w_up, w_down))
-
-
-def mix_kernel(core_ref, ids_ref, gates_ref, returned_ref, hidden_ref, kept_ref, given_ref):
+        name="expert_down",
+    )(core, act, other, *in_vmem(w_down))
+
+
+def mix_kernel(core_ref, ids_ref, gates_ref, returned_ref, kept_ref, taken_ref, out_ref, rows):
     core = core_ref[0]
-    total = hidden_ref[...]
+    half = ROWS // 2
+    kept, taken = kept_ref[...], taken_ref[...]
+    totals = [jnp.where(core == 0, kept, taken), jnp.where(core == 0, taken, kept)]
     for expert in range(EXPERTS):
-        share = jnp.float32(0.0)
-        for choice in range(2):
-            share = share + jnp.where(
-                ids_ref[core, choice] == expert, gates_ref[core, choice], jnp.float32(0.0)
-            )
         block = jnp.zeros((ROWS, 128), jnp.float32)
         for source in range(DEVS // EXPERTS):
             block = block + returned_ref[expert * (DEVS // EXPERTS) + source].astype(jnp.float32)
-        total = total + block * share
-    lower, upper = total[0 : ROWS // 2], total[ROWS // 2 : ROWS]
-    kept_ref[...] = jnp.where(core == 0, lower, upper).astype(jnp.bfloat16)
-    given_ref[...] = jnp.where(core == 0, upper, lower).astype(jnp.bfloat16)
-
-
-def mix(core, expert_ids, gate_weights, returned, hidden):
-    half = jax.ShapeDtypeStruct((ROWS // 2, 128), jnp.bfloat16)
+        for token in range(2):
+            share = jnp.float32(0.0)
+            for choice in range(2):
+                share = share + jnp.where(
+                    ids_ref[token, choice] == expert, gates_ref[token, choice], jnp.float32(0.0)
+                )
+            totals[token] = totals[token] + block[token * half : token * half + half] * share
+    for token in range(2):
+        for row in range(half):
+            rows[token : token + 1, row * 128 : row * 128 + 128] = totals[token][row : row + 1]
+    out_ref[...] = rows[...].astype(jnp.bfloat16)
+
+
+def mix(core, expert_ids, gate_weights, returned, kept, taken):
     return pl.pallas_call(
         mix_kernel,
-        out_shape=(half, half),
-        in_specs=[SMEM_BLOCK, SMEM_BLOCK, SMEM_BLOCK, VMEM_BLOCK, VMEM_BLOCK],
-        out_specs=(VMEM_BLOCK, VMEM_BLOCK),
+        out_shape=jax.ShapeDtypeStruct((2, HALF_D), jnp.bfloat16),
+        in_specs=[SMEM_BLOCK, SMEM_BLOCK, SMEM_BLOCK, VMEM_BLOCK, VMEM_BLOCK, VMEM_BLOCK],
+        out_specs=VMEM_BLOCK,
+        scratch_shapes=[pltpu.VMEM((2, HALF_D), jnp.float32)],
         compiler_params=pltpu.CompilerParams(vmem_limit_bytes=8 << 20),
         name="mix",
-    )(core, expert_ids, gate_weights, returned, hidden)
+    )(core, expert_ids, gate_weights, returned, kept, taken)
 
 
 def exchange(parts):
     return lax.all_to_all(parts, "dev", split_axis=0, concat_axis=0, tiled=True)
+
+
+def swap(value):
+    return lax.ppermute(value, "side", [(0, 1), (1, 0)])
 
 
 def local(
@@ -337,27 +448,26 @@
 ):
     core = lax.axis_index("side").astype(jnp.int32).reshape(1)
     chip = lax.axis_index("dev").astype(jnp.int32).reshape(1)
-    gain = norm_gain.reshape(DEVS, 2, HALF).transpose(1, 0, 2).reshape(2, HALF_D)
     outgoing, mark = attend(
         core, cached, query, new_key, new_value, residual, key_cache, value_cache
     )
-    projection, gate, up, down = fetch(
-        mark,
-        out_weight.T,
-        w_gate.reshape(DEVS, 2, HALF, UNITS),
-        w_up.reshape(DEVS, 2, HALF, UNITS),
-        w_down,
-    )
+    norm_gain, mark = lax.optimization_barrier((norm_gain, mark))
+    gain = norm_gain.reshape(DEVS, 2, HALF).transpose(1, 0, 2).reshape(2, HALF_D)
+    (projection,) = fetch(mark, out_weight.T)
     arrived = exchange(outgoing)
-    hidden = exchange(project(chip, arrived, projection)).reshape(HALF_D, 128)
-    partial_value, own_hidden = run_experts(chip, hidden, gain, gate, up, down)
+    packed, mark = project(chip, arrived, projection)
+    w_gate = w_gate.reshape(DEVS, 2, HALF, UNITS)
+    w_up = w_up.reshape(DEVS, 2, HALF, UNITS)
+    early = fetch_early(mark, w_gate)
+    hidden = exchange(packed).reshape(HALF_D, 128)
+    act, own_hidden = expert_units(chip, hidden, gain, early, w_gate, w_up)
+    down = fetch_half(core, own_hidden, w_down)
+    partial_value = expert_down(core, act, swap(act), down)
     returned = exchange(partial_value)
-    own_hidden = own_hidden.reshape(2, DEVS, HALF).transpose(1, 0, 2).reshape(ROWS, 128)
-    kept, given = mix(core, expert_ids, gate_weights, returned, own_hidden)
-    taken = lax.ppermute(given, "side", [(0, 1), (1, 0)])
-    first = jnp.where(core == 0, kept, taken)
-    second = jnp.where(core == 0, taken, kept)
-    return jnp.stack([first.reshape(D // 2), second.reshape(D // 2)])
+    halves = own_hidden.reshape(2, DEVS, HALF).transpose(1, 0, 2).reshape(2, ROWS // 2, 128)
+    kept = lax.dynamic_index_in_dim(halves, core[0], 0, keepdims=False)
+    given = lax.dynamic_index_in_dim(halves, 1 - core[0], 0, keepdims=False)
+    return mix(core, expert_ids, gate_weights, returned, kept, swap(given))
 
 
 def solution(mesh):

time: 93.4 us -> 84.9 us (0.909)
  local copies, waits for them, and re-layouts: 16.7 us -> 0.51 us
  waiting for transfers between devices: 27.9 us -> 40.2 us
  starting transfers between devices: 30.5 us -> 25.8 us
    unnamed x18 -> x6, local copies, waits for them, and re-layouts: 16.2 us -> 0.02 us
    all_to_all x3, waiting for transfers between devices: 27 us -> 39.1 us  [exchange(): return lax.all_to_all(parts, 'dev', split_axis=0, concat_axis=0, tiled=True)]
    pallas_call x3 -> x6, Pallas kernels: 7 us -> 13 us  [the longest x1 4.68 us: expert_units(): pl.pallas_call(expert_kernel, out_shape=(jax.ShapeDtypeStruct((DEVS, UNIT...]
    pallas_call x1, Pallas kernels: 6.78 us -> 1.29 us  [fetch(): pl.pallas_call(fetch_kernel, out_shape=tuple((pltpu.VMEM(array.shape, arr...]
    all_to_all x3, starting transfers between devices: 26.7 us -> 22.2 us  [exchange(): return lax.all_to_all(parts, 'dev', split_axis=0, concat_axis=0, tiled=True)]
    ppermute x1 -> x2, starting transfers between devices: 3.82 us -> 3.57 us  [swap(): return lax.ppermute(value, 'side', [(0, 1), (1, 0)])]
  transfers between devices with their start and end apart: 4 -> 5, of which waited for: 4 -> 4; matrix products, arithmetic and copies ran while one was open for 1% -> 1% of each run, Pallas kernels for 7% -> 6%
where the time goes in v5:
time: 84.9 us; the launch traced here: 84.1 us
  waiting for transfers between devices  40.2 us (47%)
  starting transfers between devices  25.8 us (30%)
  Pallas kernels  17.5 us (21%)
    all_to_all x3, waiting for transfers between devices, exchange(): return lax.all_to_all(parts, 'dev', split_axis=0, concat_axis=0, tiled=True)  39.1 us
    all_to_all x3, starting transfers between devices, exchange(): return lax.all_to_all(parts, 'dev', split_axis=0, concat_axis=0, tiled=True)  22.2 us
    pallas_call x1, Pallas kernels, expert_units(): pl.pallas_call(expert_kernel, out_shape=(jax.ShapeDtypeStruct((DEVS, UNIT...  4.68 us
    ppermute x2, starting transfers between devices, swap(): return lax.ppermute(value, 'side', [(0, 1), (1, 0)])  3.57 us
    pallas_call x1, Pallas kernels, attend(): pl.pallas_call(attend_kernel, out_shape=(jax.ShapeDtypeStruct((DEVS, SENT...  3.25 us
    pallas_call x1, Pallas kernels, fetch_half(): pl.pallas_call(half_kernel, out_shape=pltpu.VMEM((UNITS, HALF_D), w_down....  1.88 us
    pallas_call x1, Pallas kernels, expert_down(): pl.pallas_call(down_kernel, out_shape=jax.ShapeDtypeStruct((DEVS, ROWS, 1...  1.78 us
    pallas_call x1, Pallas kernels, project(): pl.pallas_call(project_kernel, out_shape=(jax.ShapeDtypeStruct((DEVS, HAL...  1.7 us
  transfers between devices with their start and end apart: 5, of which 4 were waited for; matrix products, arithmetic and copies ran while one was open for 1% of the time, Pallas kernels for 6%

profile of v5, /device:TPU:1, one launch (start us, length us, event | category | flops | bytes accessed | tf_op | source)
XLA Modules:
  0.0 84.1 jit_solution(9376711753447124713)
XLA Ops:
  0.0 3.3 %attend.1 = (bf16[64,56,128]{2,1,0:T(8,128)(2,1)}, f32[8,128]{1,0:T(8,128)S(1)}) custom-call(s32[1]{0:T(128)} %bitcast.core_ref, s32[2]{0:T(128)} %cached_ref.1, bf16[2,6144]{1,0:T(2,128)(2,1)} %query_ref.1, bf16[2,1024]{1,0:T(2,128)(2,1)} %new_key_ref.1, bf16[2,1024]{1,0:T(2,128)(2,1)} %new_value_ref.1, bf16[2,6144]{1,0:T(2,128)(2,1)} %residual_ref.1, ...), custom_call_target="tpu_custom_call" | custom-call | tf_op jit(solution)/shard_map/attend/pallas_call | solution.py:120
  3.3 12.0 %all-to-all-start = ((bf16[64,56,128]{2,1,0:T(8,128)(2,1)}), bf16[64,56,128]{2,1,0:T(8,128)(2,1)S(1)}, u32[]{:S(2)}, u32[]{:S(2)}) async-start(bf16[64,56,128]{2,1,0:T(8,128)(2,1)} %get-tuple-element.13), calls=%async_computation | async-start | bytes 1835008 | tf_op jit(solution)/shard_map/all_to_all | solution.py:426
  15.2 0.0 copy-start.2
  15.2 1.3 %fetch.1.weight_ref = bf16[96,6144]{1,0:T(8,128)(2,1)S(1)} custom-call(f32[8,128]{1,0:T(8,128)S(1)} %get-tuple-element.15.after_ref, bf16[96,6144]{1,0:T(8,128)(2,1)} %bitcast.16), custom_call_target="tpu_custom_call" | custom-call | bytes 2359296 | tf_op jit(solution)/shard_map/fetch/pallas_call | solution.py:162
  16.5 14.0 %all-to-all-done.arrived_ref = bf16[64,56,128]{2,1,0:T(8,128)(2,1)S(1)} async-done(((bf16[64,56,128]{2,1,0:T(8,128)(2,1)}), bf16[64,56,128]{2,1,0:T(8,128)(2,1)S(1)}, u32[]{:S(2)}, u32[]{:S(2)}) %all-to-all-start) | async-done | bytes 917536 | tf_op jit(solution)/shard_map/all_to_all | solution.py:426
  30.6 1.7 %project.1 = (bf16[64,48,128]{2,1,0:T(8,128)(2,1)}, f32[8,128]{1,0:T(8,128)S(1)}) custom-call(s32[1]{0:T(128)} %bitcast.1.chip_ref, bf16[64,56,128]{2,1,0:T(8,128)(2,1)S(1)} %all-to-all-done.arrived_ref, bf16[96,6144]{1,0:T(8,128)(2,1)S(1)} %fetch.1.weight_ref), custom_call_target="tpu_custom_call" | custom-call | tf_op jit(solution)/shard_map/project/pallas_call | solution.py:251
  32.3 5.6 %all-to-all-start.1 = ((bf16[64,48,128]{2,1,0:T(8,128)(2,1)}), bf16[64,48,128]{2,1,0:T(8,128)(2,1)S(1)}, u32[]{:S(2)}, u32[]{:S(2)}) async-start(bf16[64,48,128]{2,1,0:T(8,128)(2,1)} %get-tuple-element.16), calls=%async_computation.1 | async-start | bytes 1572864 | tf_op jit(solution)/shard_map/all_to_all | solution.py:426
  37.8 0.0 copy-done.2
  37.9 0.1 reshape.30
  38.0 0.1 reshape.31.gain_ref
  38.1 1.6 %fetch_early.1.early_ref = bf16[3,16,48,512]{3,2,1,0:T(8,128)(2,1)S(1)} custom-call(f32[8,128]{1,0:T(8,128)S(1)} %get-tuple-element.18.after_ref, bf16[64,2,48,512]{3,2,1,0:T(8,128)(2,1)} %bitcast.13), custom_call_target="tpu_custom_call" | custom-call | tf_op jit(solution)/shard_map/fetch_early/pallas_call | solution.py:188
  39.7 11.6 %all-to-all-done.1 = bf16[64,48,128]{2,1,0:T(8,128)(2,1)S(1)} async-done(((bf16[64,48,128]{2,1,0:T(8,128)(2,1)}), bf16[64,48,128]{2,1,0:T(8,128)(2,1)S(1)}, u32[]{:S(2)}, u32[]{:S(2)}) %all-to-all-start.1) | async-done | bytes 786464 | tf_op jit(solution)/shard_map/all_to_all | solution.py:426
  51.4 4.7 %expert_units.1 = (bf16[64,512]{1,0:T(8,128)(2,1)S(1)}, f32[2,3072]{1,0:T(2,128)S(1)}) custom-call(s32[1]{0:T(128)} %bitcast.1.chip_ref, bf16[3072,128]{1,0:T(8,128)(2,1)S(1)} %bitcast.12, bf16[2,3072]{1,0:T(2,128)(2,1)S(1)} %reshape.31.gain_ref, bf16[3,16,48,512]{3,2,1,0:T(8,128)(2,1)S(1)} %fetch_early.1.early_ref, bf16[64,2,48,512]{3,2,1,0:T(8,128)(2,1)} %bitcast.14, ...), custom_call_target="tpu_custom_call" | custom-call | tf_op jit(solution)/shard_map/expert_units/pallas_call | solution.py:340
  56.1 3.4 %collective-permute-start = (bf16[64,512]{1,0:T(8,128)(2,1)S(1)}, bf16[64,512]{1,0:T(8,128)(2,1)S(1)}, u32[]{:S(2)}, u32[]{:S(2)}) collective-permute-start(bf16[64,512]{1,0:T(8,128)(2,1)S(1)} %get-tuple-element.19.act_ref), channel_id=1, source_target_pairs={{0,64},{64,0},{1,65},{65,1},{2,66},{66,2},{3,67},{67,3},{4,68},{68... | collective-permute-start | bytes 196616 | tf_op jit(solution)/shard_map/ppermute | solution.py:430
  59.4 1.9 %fetch_half.1.down_ref = bf16[512,3072]{1,0:T(8,128)(2,1)S(1)} custom-call(s32[1]{0:T(128)} %bitcast.core_ref, f32[2,3072]{1,0:T(2,128)S(1)} %get-tuple-element.20.after_ref, bf16[512,6144]{1,0:T(8,128)(2,1)} %down_hbm.1), custom_call_target="tpu_custom_call" | custom-call | tf_op jit(solution)/shard_map/fetch_half/pallas_call | solution.py:216
  61.3 0.0 copy-start
  61.3 0.0 copy-start.1
  61.3 0.0 collective-permute-done.other_ref
  61.4 1.8 %expert_down.1 = bf16[64,48,128]{2,1,0:T(8,128)(2,1)} custom-call(s32[1]{0:T(128)} %bitcast.core_ref, bf16[64,512]{1,0:T(8,128)(2,1)S(1)} %get-tuple-element.19.act_ref, bf16[64,512]{1,0:T(8,128)(2,1)S(1)} %collective-permute-done.other_ref, bf16[512,3072]{1,0:T(8,128)(2,1)S(1)} %fetch_half.1.down_ref), custom_call_target="tpu_custom_call" | custom-call | tf_op jit(solution)/shard_map/expert_down/pallas_call | solution.py:377
  63.1 4.6 %all-to-all-start.2 = ((bf16[64,48,128]{2,1,0:T(8,128)(2,1)}), bf16[64,48,128]{2,1,0:T(8,128)(2,1)S(1)}, u32[]{:S(2)}, u32[]{:S(2)}) async-start(bf16[64,48,128]{2,1,0:T(8,128)(2,1)} %expert_down.1), calls=%async_computation.2 | async-start | bytes 1572864 | tf_op jit(solution)/shard_map/all_to_all | solution.py:426
  67.8 0.1 reshape.34
  67.9 0.1 copy.17
  67.9 0.1 reshape.35
  68.1 0.2 collective-permute-start.1
  68.3 1.1 %collective-permute-done.1.taken_ref = f32[24,128]{1,0:T(8,128)S(1)} collective-permute-done((f32[24,128]{1,0:T(8,128)S(1)}, f32[24,128]{1,0:T(8,128)S(1)}, u32[]{:S(2)}, u32[]{:S(2)}) %collective-permute-start.1) | collective-permute-done | bytes 12320 | tf_op jit(solution)/shard_map/ppermute | solution.py:430
  69.3 13.5 %all-to-all-done.2.returned_ref = bf16[64,48,128]{2,1,0:T(8,128)(2,1)S(1)} async-done(((bf16[64,48,128]{2,1,0:T(8,128)(2,1)}), bf16[64,48,128]{2,1,0:T(8,128)(2,1)S(1)}, u32[]{:S(2)}, u32[]{:S(2)}) %all-to-all-start.2) | async-done | bytes 786464 | tf_op jit(solution)/shard_map/all_to_all | solution.py:426
  82.8 0.0 copy-done
  82.8 0.0 copy-done.1
  82.8 1.3 %mix.1 = bf16[2,3072]{1,0:T(2,128)(2,1)} custom-call(s32[1]{0:T(128)} %bitcast.core_ref, s32[2,2]{1,0:T(2,128)S(1)} %copy-done, f32[2,2]{1,0:T(2,128)S(1)} %copy-done.1, bf16[64,48,128]{2,1,0:T(8,128)(2,1)S(1)} %all-to-all-done.2.returned_ref, f32[24,128]{1,0:T(8,128)S(1)} %get-tuple-element.22.kept_ref, f32[24,128]{1,0:T(8,128)S(1)} %collective-permute-done.1.taken_ref), custom_call_target="tpu_custom_call" | custom-call | tf_op jit(solution)/shard_map/mix/pallas_call | solution.py:414
  (2 shorter events, 0.0 us)
Async XLA Ops:
  3.3 27.3 %all-to-all-start = ((bf16[64,56,128]{2,1,0:T(8,128)(2,1)}), bf16[64,56,128]{2,1,0:T(8,128)(2,1)S(1)}, u32[]{:S(2)}, u32[]{:S(2)}) async-start(bf16[64,56,128]{2,1,0:T(8,128)(2,1)} %get-tuple-element.13), calls=%async_computation | async-start | bytes 1835008 | tf_op jit(solution)/shard_map/all_to_all | solution.py:426
  15.2 22.6 %copy-start.2 = (bf16[6144]{0:T(1024)(128)(2,1)S(1)}, bf16[6144]{0:T(1024)(128)(2,1)}, u32[]{:S(2)}) copy-start(bf16[6144]{0:T(1024)(128)(2,1)} %param.22) | copy-start | bytes 36868
  32.3 19.1 %all-to-all-start.1 = ((bf16[64,48,128]{2,1,0:T(8,128)(2,1)}), bf16[64,48,128]{2,1,0:T(8,128)(2,1)S(1)}, u32[]{:S(2)}, u32[]{:S(2)}) async-start(bf16[64,48,128]{2,1,0:T(8,128)(2,1)} %get-tuple-element.16), calls=%async_computation.1 | async-start | bytes 1572864 | tf_op jit(solution)/shard_map/all_to_all | solution.py:426
  56.1 5.3 %collective-permute-start = (bf16[64,512]{1,0:T(8,128)(2,1)S(1)}, bf16[64,512]{1,0:T(8,128)(2,1)S(1)}, u32[]{:S(2)}, u32[]{:S(2)}) collective-permute-start(bf16[64,512]{1,0:T(8,128)(2,1)S(1)} %get-tuple-element.19.act_ref), channel_id=1, source_target_pairs={{0,64},{64,0},{1,65},{65,1},{2,66},{66,2},{3,67},{67,3},{4,68},{68... | collective-permute-start | bytes 196616 | tf_op jit(solution)/shard_map/ppermute | solution.py:430
  61.3 21.5 %copy-start = (s32[2,2]{1,0:T(2,128)S(1)}, s32[2,2]{1,0:T(2,128)}, u32[]{:S(2)}) copy-start(s32[2,2]{1,0:T(2,128)} %ids_ref.1) | copy-start | bytes 52
  61.3 21.5 %copy-start.1 = (f32[2,2]{1,0:T(2,128)S(1)}, f32[2,2]{1,0:T(2,128)}, u32[]{:S(2)}) copy-start(f32[2,2]{1,0:T(2,128)} %gates_ref.1) | copy-start | bytes 52
  63.1 19.7 %all-to-all-start.2 = ((bf16[64,48,128]{2,1,0:T(8,128)(2,1)}), bf16[64,48,128]{2,1,0:T(8,128)(2,1)S(1)}, u32[]{:S(2)}, u32[]{:S(2)}) async-start(bf16[64,48,128]{2,1,0:T(8,128)(2,1)} %expert_down.1), calls=%async_computation.2 | async-start | bytes 1572864 | tf_op jit(solution)/shard_map/all_to_all | solution.py:426
  68.1 1.3 %collective-permute-start.1 = (f32[24,128]{1,0:T(8,128)S(1)}, f32[24,128]{1,0:T(8,128)S(1)}, u32[]{:S(2)}, u32[]{:S(2)}) collective-permute-start(f32[24,128]{1,0:T(8,128)S(1)} %get-tuple-element.21), channel_id=1, source_target_pairs={{0,64},{64,0},{1,65},{65,1},{2,66},{66,2},{3,67},{67,3},{4,68},{68... | collective-permute-start | bytes 36872 | tf_op jit(solution)/shard_map/ppermute | solution.py:430

commit v6 on v3

--- a/solution.py
+++ b/solution.py
@@ -18,11 +18,15 @@
 COLS = D // DEVS
 HALF = COLS // 2
 ROWS = D // 128
-SENT = ROWS + 8
+SENT = ROWS + 2
+BATCH = 8
 UNITS = 512
 HALF_D = D // 2
 CHUNK = 768
 PART = CHUNK // HALF
+STEPS = HALF_D // CHUNK
+EARLY = 3
+DOWN = 1024
 
 epsilon = 1e-05
 
@@ -57,28 +61,30 @@
     out_ref,
     mark_ref,
     query_rows,
+    residual_rows,
     context_rows,
-    residual_rows,
+    pattern,
 ):
     core = core_ref[0]
+    first_row = pl.multiple_of(core * 64, 64)
 
     def own(ref):
         both = ref[...].astype(jnp.float32)
         return jnp.where(core == 0, both[0:1], both[1:2])
 
-    query = own(query_ref)
+    query_rows[...] = jnp.zeros_like(query_rows)
+    residual_rows[...] = jnp.zeros_like(residual_rows)
+    both = query_ref[...].astype(jnp.float32)
+    for head in range(HEADS):
+        row = head // GROUP * 8 + head % GROUP
+        query_rows[pl.ds(row, 2, stride=64), :] = both[:, head * 128 : head * 128 + 128]
+    both = residual_ref[...].astype(jnp.float32)
+    for row in range(ROWS):
+        residual_rows[pl.ds(row, 2, stride=64), :] = both[:, row * 128 : row * 128 + 128]
+    queries = query_rows[pl.ds(first_row, 64), :]
+    narrow = queries.astype(jnp.bfloat16)
     new_key = own(new_key_ref)
     new_value = own(new_value_ref)
-    residual = own(residual_ref)
-    query_rows[...] = jnp.zeros_like(query_rows)
-    for head in range(HEADS):
-        row = head // GROUP * 8 + head % GROUP
-        query_rows[row : row + 1, :] = query[:, head * 128 : head * 128 + 128]
-    for row in range(ROWS):
-        residual_rows[row : row + 1, :] = residual[:, row * 128 : row * 128 + 128]
-    residual_rows[ROWS:SENT, :] = jnp.zeros((SENT - ROWS, 128), jnp.float32)
-    queries = query_rows[...]
-    narrow = queries.astype(jnp.bfloat16)
     scale = 1.0 / math.sqrt(HEAD_DIM)
     scores = []
     own_keys = []
@@ -103,12 +109,18 @@
         )
         context = context + own_weight[kv * 8 : kv * 8 + 8] * new_value[:, lanes]
         context_rows[kv * GROUP : kv * GROUP + 8, :] = context
-    context = context_rows[0:HEADS, :].astype(jnp.bfloat16)
-    mark_ref[...] = context_rows[0:8, :]
-    for chip in range(DEVS):
-        first = COLS * chip // 128
-        out_ref[chip, 0:ROWS, :] = context
-        out_ref[chip, ROWS:SENT, :] = residual_rows[first : first + 8, :].astype(jnp.bfloat16)
+    context = context_rows[0:ROWS, :]
+    mark_ref[...] = context[0:8]
+    for chip in range(BATCH):
+        pattern[chip * SENT : chip * SENT + ROWS, :] = context
+    for group in range(DEVS // BATCH):
+        for chip in range(BATCH):
+            wanted = COLS * (group * BATCH + chip) // 128
+            pattern[chip * SENT + ROWS : chip * SENT + SENT, :] = residual_rows[
+                pl.ds(first_row + wanted, 2), :
+            ]
+        first = group * BATCH * SENT
+        out_ref[first : first + BATCH * SENT, :] = pattern[...].astype(jnp.bfloat16)
 
 
 def attend(core, cached, query, new_key, new_value, residual, key_cache, value_cache):
@@ -119,7 +131,7 @@
     return pl.pallas_call(
         attend_kernel,
         out_shape=(
-            jax.ShapeDtypeStruct((DEVS, SENT, 128), jnp.bfloat16),
+            jax.ShapeDtypeStruct((DEVS * SENT, 128), jnp.bfloat16),
             jax.ShapeDtypeStruct((8, 128), jnp.float32),
         ),
         grid_spec=pltpu.PrefetchScalarGridSpec(
@@ -133,11 +145,12 @@
                 cache,
                 cache,
             ],
-            out_specs=(whole((DEVS, SENT, 128)), whole((8, 128))),
+            out_specs=(whole((DEVS * SENT, 128)), whole((8, 128))),
             scratch_shapes=[
-                pltpu.VMEM((64, 128), jnp.float32),
-                pltpu.VMEM((SENT, 128), jnp.float32),
-                pltpu.VMEM((SENT, 128), jnp.float32),
+                pltpu.VMEM((128, 128), jnp.float32),
+                pltpu.VMEM((128, 128), jnp.float32),
+                pltpu.VMEM((ROWS + 8, 128), jnp.float32),
+                pltpu.VMEM((BATCH * SENT, 128), jnp.float32),
             ],
         ),
         compiler_params=pltpu.CompilerParams(vmem_limit_bytes=8 << 20),
@@ -170,9 +183,9 @@
     )(after, *in_hbm(*arrays))
 
 
-def project_kernel(chip_ref, arrived_ref, weight_ref, out_ref, rows, context):
-    for source in range(DEVS):
-        rows[source * SENT : source * SENT + SENT, :] = arrived_ref[source].astype(jnp.float32)
+def project_kernel(chip_ref, arrived_ref, weight_ref, out_ref, mark_ref, rows, context):
+    for source in range(0, DEVS * SENT, 400):
+        rows[source : source + 400, :] = arrived_ref[source : source + 400, :].astype(jnp.float32)
     for head in range(HEADS):
         context[:, head * 128 : head * 128 + 128] = rows[pl.ds(head, DEVS, stride=SENT), :].astype(
             jnp.bfloat16
@@ -188,6 +201,7 @@
     hidden = rows[pl.ds(first, COLS), :] + projected
     lane = lax.broadcasted_iota(jnp.int32, (HALF, 128), 1)
     packed = jnp.where(lane < DEVS, hidden[0:HALF], hidden[HALF:COLS]).astype(jnp.bfloat16)
+    mark_ref[...] = hidden[0:8]
     for target in range(DEVS):
         out_ref[target] = packed
 
@@ -195,9 +209,12 @@
 def project(chip, arrived, weight):
     return pl.pallas_call(
         project_kernel,
-        out_shape=jax.ShapeDtypeStruct((DEVS, HALF, 128), jnp.bfloat16),
+        out_shape=(
+            jax.ShapeDtypeStruct((DEVS, HALF, 128), jnp.bfloat16),
+            jax.ShapeDtypeStruct((8, 128), jnp.float32),
+        ),
         in_specs=[SMEM_BLOCK, VMEM_BLOCK, VMEM_BLOCK],
-        out_specs=VMEM_BLOCK,
+        out_specs=(VMEM_BLOCK, VMEM_BLOCK),
         scratch_shapes=[
             pltpu.VMEM((DEVS * SENT, 128), jnp.float32),
             pltpu.VMEM((DEVS, D), jnp.bfloat16),
@@ -207,19 +224,68 @@
     )(chip, arrived, *in_vmem(weight))
 
 
+def early_kernel(after_ref, gate_hbm, out_ref, sems):
+    copies = [
+        pltpu.make_async_copy(
+            gate_hbm.at[pl.ds(step * PART, PART), 0], out_ref.at[step], sems.at[step]
+        )
+        for step in range(EARLY)
+    ]
+    for copy in copies:
+        copy.start()
+    for copy in copies:
+        copy.wait()
+
+
+def fetch_early(after, w_gate):
+    return pl.pallas_call(
+        early_kernel,
+        out_shape=pltpu.VMEM((EARLY, PART, HALF, UNITS), w_gate.dtype),
+        in_specs=[ANY_BLOCK] * 2,
+        out_specs=VMEM_BLOCK,
+        scratch_shapes=[pltpu.SemaphoreType.DMA((EARLY,))],
+        compiler_params=pltpu.CompilerParams(vmem_limit_bytes=1 << 20),
+        name="fetch_early",
+    )(after, *in_hbm(w_gate))
+
+
 def expert_kernel(
     chip_ref,
     hidden_ref,
     gain_ref,
+    early_ref,
+    gate_hbm,
+    up_hbm,
+    down_hbm,
+    out_ref,
+    own_ref,
     gate_vmem,
     up_vmem,
     down_vmem,
-    out_ref,
-    own_ref,
     flipped,
     scaled,
     result,
+    sems,
 ):
+    pieces = [(half, step) for half in range(2) for step in range(STEPS)]
+    order = list(range(EARLY, len(pieces))) + list(range(EARLY))
+    copies = {}
+    for index in order:
+        half, step = pieces[index]
+        part = pl.ds(step * PART, PART)
+        for which, source, target in ((0, gate_hbm, gate_vmem), (1, up_hbm, up_vmem)):
+            if which == 1 or index >= EARLY:
+                copies[which, index] = pltpu.make_async_copy(
+                    source.at[part, half], target.at[part, half], sems.at[which, index]
+                )
+                copies[which, index].start()
+    for step in range(D // DOWN):
+        part = pl.ds(step * DOWN, DOWN)
+        copies[2, step] = pltpu.make_async_copy(
+            down_hbm.at[:, part], down_vmem.at[:, part], sems.at[2, step]
+        )
+        copies[2, step].start()
+
     squares = jnp.zeros((128, 128), jnp.float32)
     for block in range(HALF_D // 128):
         lanes = slice(block * 128, block * 128 + 128)
@@ -235,54 +301,71 @@
     total = jnp.sum(squares, axis=1, keepdims=True)
     factor = lax.rsqrt((total[0:DEVS] + total[DEVS:128]) * (1.0 / D) + epsilon)
 
+    def product(index, weights):
+        half, step = pieces[index]
+        rows = scaled[half * DEVS : half * DEVS + DEVS, step * CHUNK : step * CHUNK + CHUNK]
+        return jnp.dot(rows, weights.reshape(CHUNK, UNITS), preferred_element_type=jnp.float32)
+
+    def part_of(ref, index):
+        half, step = pieces[index]
+        return ref[step * PART : step * PART + PART, half]
+
     gate = jnp.zeros((DEVS, UNITS), jnp.float32)
     up = jnp.zeros((DEVS, UNITS), jnp.float32)
-    for half in range(2):
-        for step in range(HALF_D // CHUNK):
-            rows = scaled[half * DEVS : half * DEVS + DEVS, step * CHUNK : step * CHUNK + CHUNK]
-            part = slice(step * PART, step * PART + PART)
-            gate = gate + jnp.dot(
-                rows,
-                gate_vmem[part, half].reshape(CHUNK, UNITS),
-                preferred_element_type=jnp.float32,
-            )
-            up = up + jnp.dot(
-                rows, up_vmem[part, half].reshape(CHUNK, UNITS), preferred_element_type=jnp.float32
-            )
+    for index in range(EARLY):
+        gate = gate + product(index, early_ref[index])
+    for index in order:
+        if index >= EARLY:
+            copies[0, index].wait()
+            gate = gate + product(index, part_of(gate_vmem, index))
+        copies[1, index].wait()
+        up = up + product(index, part_of(up_vmem, index))
     gate = gate * factor
     up = up * factor
     act = (gate / (1.0 + jnp.exp(-gate)) * up).astype(jnp.bfloat16)
-    for step in range(4):
-        for piece in range(D // 4 // 512):
-            first = step * (D // 4) + piece * 512
-            block = jnp.dot(
-                act, down_vmem[:, first : first + 512], preferred_element_type=jnp.float32
-            )
-            for column in range(4):
-                result[pl.ds(first // 128 + column, DEVS, stride=ROWS), :] = block[
-                    :, column * 128 : column * 128 + 128
-                ]
+    span = DOWN // 128
+    for step in range(D // DOWN):
+        copies[2, step].wait()
+        block = jnp.dot(
+            act, down_vmem[:, step * DOWN : step * DOWN + DOWN], preferred_element_type=jnp.float32
+        )
+        for column in range(span):
+            result[pl.ds(step * span + column, DEVS, stride=ROWS), :] = block[
+                :, column * 128 : column * 128 + 128
+            ]
+        last = (step + 1) * span
+        if last % 16 == 0 and last < ROWS:
+            for target in range(DEVS):
+                out_ref[target, last - 16 : last, :] = result[
+                    target * ROWS + last - 16 : target * ROWS + last, :
+                ].astype(jnp.bfloat16)
     for target in range(DEVS):
-        out_ref[target] = result[target * ROWS : target * ROWS + ROWS, :].astype(jnp.bfloat16)
-
-
-def run_experts(chip, hidden, gain, w_gate, w_up, w_down):
+        out_ref[target, ROWS - 16 : ROWS, :] = result[
+            target * ROWS + ROWS - 16 : target * ROWS + ROWS, :
+        ].astype(jnp.bfloat16)
+
+
+def run_experts(chip, hidden, gain, early, w_gate, w_up, w_down):
     return pl.pallas_call(
         expert_kernel,
         out_shape=(
-            jax.ShapeDtypeStruct((DEVS, ROWS, 128), jnp.bfloat16),
+            pltpu.HBM((DEVS, ROWS, 128), jnp.bfloat16),
             jax.ShapeDtypeStruct((2, HALF_D), jnp.float32),
         ),
-        in_specs=[SMEM_BLOCK] + [VMEM_BLOCK] * 5,
+        in_specs=[SMEM_BLOCK] + [VMEM_BLOCK] * 3 + [ANY_BLOCK] * 3,
         out_specs=(VMEM_BLOCK, VMEM_BLOCK),
         scratch_shapes=[
+            pltpu.VMEM((DEVS, 2, HALF, UNITS), jnp.bfloat16),
+            pltpu.VMEM((DEVS, 2, HALF, UNITS), jnp.bfloat16),
+            pltpu.VMEM((UNITS, D), jnp.bfloat16),
             pltpu.VMEM((128, HALF_D), jnp.float32),
             pltpu.VMEM((128, HALF_D), jnp.bfloat16),
             pltpu.VMEM((DEVS * ROWS, 128), jnp.float32),
+            pltpu.SemaphoreType.DMA((3, 2 * STEPS)),
         ],
-        compiler_params=pltpu.CompilerParams(vmem_limit_bytes=16 << 20),
+        compiler_params=pltpu.CompilerParams(vmem_limit_bytes=40 << 20),
         name="experts",
-    )(chip, hidden, gain, *in_vmem(w_gate, w_up, w_down))
+    )(chip, hidden, gain, *in_vmem(early), *in_hbm(w_gate, w_up, w_down))
 
 
 def mix_kernel(core_ref, ids_ref, gates_ref, returned_ref, hidden_ref, kept_ref, given_ref):
@@ -337,20 +420,19 @@
 ):
     core = lax.axis_index("side").astype(jnp.int32).reshape(1)
     chip = lax.axis_index("dev").astype(jnp.int32).reshape(1)
-    gain = norm_gain.reshape(DEVS, 2, HALF).transpose(1, 0, 2).reshape(2, HALF_D)
     outgoing, mark = attend(
         core, cached, query, new_key, new_value, residual, key_cache, value_cache
     )
-    projection, gate, up, down = fetch(
-        mark,
-        out_weight.T,
-        w_gate.reshape(DEVS, 2, HALF, UNITS),
-        w_up.reshape(DEVS, 2, HALF, UNITS),
-        w_down,
-    )
-    arrived = exchange(outgoing)
-    hidden = exchange(project(chip, arrived, projection)).reshape(HALF_D, 128)
-    partial_value, own_hidden = run_experts(chip, hidden, gain, gate, up, down)
+    norm_gain, mark = lax.optimization_barrier((norm_gain, mark))
+    gain = norm_gain.reshape(DEVS, 2, HALF).transpose(1, 0, 2).reshape(2, HALF_D)
+    (projection,) = fetch(mark, out_weight.T)
+    arrived = exchange(outgoing.reshape(DEVS, SENT // 2, 2, 128)).reshape(DEVS * SENT, 128)
+    packed, mark = project(chip, arrived, projection)
+    w_gate = w_gate.reshape(DEVS, 2, HALF, UNITS)
+    w_up = w_up.reshape(DEVS, 2, HALF, UNITS)
+    early = fetch_early(mark, w_gate)
+    hidden = exchange(packed).reshape(HALF_D, 128)
+    partial_value, own_hidden = run_experts(chip, hidden, gain, early, w_gate, w_up, w_down)
     returned = exchange(partial_value)
     own_hidden = own_hidden.reshape(2, DEVS, HALF).transpose(1, 0, 2).reshape(ROWS, 128)
     kept, given = mix(core, expert_ids, gate_weights, returned, own_hidden)

time: 93.4 us -> 83.5 us (0.89)
  local copies, waits for them, and re-layouts: 16.7 us -> 0.52 us
  waiting for transfers between devices: 27.9 us -> 38.1 us
  starting transfers between devices: 30.5 us -> 27.4 us
    unnamed x18 -> x6, local copies, waits for them, and re-layouts: 16.2 us -> 0.01 us
    all_to_all x3, waiting for transfers between devices: 27 us -> 37.3 us  [exchange(): return lax.all_to_all(parts, 'dev', split_axis=0, concat_axis=0, tiled=True)]
    pallas_call x1, Pallas kernels: 6.78 us -> 1.28 us  [fetch(): pl.pallas_call(fetch_kernel, out_shape=tuple((pltpu.VMEM(array.shape, arr...]
    pallas_call x3 -> x4, Pallas kernels: 9.58 us -> 14.3 us  [the longest x1 7.58 us: run_experts(): pl.pallas_call(expert_kernel, out_shape=(pltpu.HBM((DEVS, ROWS, 128), jnp...]
    all_to_all x3, starting transfers between devices: 26.7 us -> 23.5 us  [exchange(): return lax.all_to_all(parts, 'dev', split_axis=0, concat_axis=0, tiled=True)]
  transfers between devices with their start and end apart: 4 -> 4, of which waited for: 4 -> 4; matrix products, arithmetic and copies ran while one was open for 1% -> 1% of each run, Pallas kernels for 7% -> 4%
where the time goes in v6:
time: 83.5 us; the launch traced here: 83 us
  waiting for transfers between devices  38.1 us (46%)
  starting transfers between devices  27.4 us (33%)
  Pallas kernels  16.3 us (20%)
    all_to_all x3, waiting for transfers between devices, exchange(): return lax.all_to_all(parts, 'dev', split_axis=0, concat_axis=0, tiled=True)  37.3 us
    all_to_all x3, starting transfers between devices, exchange(): return lax.all_to_all(parts, 'dev', split_axis=0, concat_axis=0, tiled=True)  23.5 us
    pallas_call x1, Pallas kernels, run_experts(): pl.pallas_call(expert_kernel, out_shape=(pltpu.HBM((DEVS, ROWS, 128), jnp...  7.58 us
    ppermute x1, starting transfers between devices, local(): taken = lax.ppermute(given, 'side', [(0, 1), (1, 0)])  3.82 us
    pallas_call x1, Pallas kernels, attend(): pl.pallas_call(attend_kernel, out_shape=(jax.ShapeDtypeStruct((DEVS * SEN...  3.42 us
    pallas_call x1, Pallas kernels, project(): pl.pallas_call(project_kernel, out_shape=(jax.ShapeDtypeStruct((DEVS, HAL...  1.69 us
  transfers between devices with their start and end apart: 4, of which 4 were waited for; matrix products, arithmetic and copies ran while one was open for 1% of the time, Pallas kernels for 4%

profile of v6, /device:TPU:1, one launch (start us, length us, event | category | flops | bytes accessed | tf_op | source)
XLA Modules:
  0.0 83.0 jit_solution(13432689279489376029)
XLA Ops:
  0.0 0.0 copy-start.2
  0.0 3.4 %attend.1 = (bf16[3200,128]{1,0:T(8,128)(2,1)}, f32[8,128]{1,0:T(8,128)S(1)}) custom-call(s32[1]{0:T(128)} %bitcast.core_ref, s32[2]{0:T(128)} %cached_ref.1, bf16[2,6144]{1,0:T(2,128)(2,1)} %query_ref.1, bf16[2,1024]{1,0:T(2,128)(2,1)} %new_key_ref.1, bf16[2,1024]{1,0:T(2,128)(2,1)} %new_value_ref.1, bf16[2,6144]{1,0:T(2,128)(2,1)} %residual_ref.1, ...), custom_call_target="tpu_custom_call" | custom-call | tf_op jit(solution)/shard_map/attend/pallas_call | solution.py:131
  3.4 12.0 %all-to-all-start = ((bf16[64,25,2,128]{3,2,1,0:T(2,128)(2,1)}), bf16[64,25,2,128]{3,2,1,0:T(2,128)(2,1)S(1)}, u32[]{:S(2)}, u32[]{:S(2)}) async-start(bf16[64,25,2,128]{3,2,1,0:T(2,128)(2,1)} %bitcast.3), calls=%async_computation | async-start | bytes 1638400 | tf_op jit(solution)/shard_map/all_to_all | solution.py:402
  15.4 1.3 %fetch.1.weight_ref = bf16[96,6144]{1,0:T(8,128)(2,1)S(1)} custom-call(f32[8,128]{1,0:T(8,128)S(1)} %get-tuple-element.17.after_ref, bf16[96,6144]{1,0:T(8,128)(2,1)} %bitcast.26), custom_call_target="tpu_custom_call" | custom-call | bytes 2359296 | tf_op jit(solution)/shard_map/fetch/pallas_call | solution.py:174
  16.7 13.2 %all-to-all-done = bf16[64,25,2,128]{3,2,1,0:T(2,128)(2,1)S(1)} async-done(((bf16[64,25,2,128]{3,2,1,0:T(2,128)(2,1)}), bf16[64,25,2,128]{3,2,1,0:T(2,128)(2,1)S(1)}, u32[]{:S(2)}, u32[]{:S(2)}) %all-to-all-start) | async-done | bytes 819232 | tf_op jit(solution)/shard_map/all_to_all | solution.py:402
  29.9 1.7 %project.1 = (bf16[64,48,128]{2,1,0:T(8,128)(2,1)}, f32[8,128]{1,0:T(8,128)S(1)}) custom-call(s32[1]{0:T(128)} %bitcast.2.chip_ref, bf16[3200,128]{1,0:T(8,128)(2,1)S(1)} %bitcast.21, bf16[96,6144]{1,0:T(8,128)(2,1)S(1)} %fetch.1.weight_ref), custom_call_target="tpu_custom_call" | custom-call | tf_op jit(solution)/shard_map/project/pallas_call | solution.py:210
  31.6 5.3 %all-to-all-start.1 = ((bf16[64,48,128]{2,1,0:T(8,128)(2,1)}), bf16[64,48,128]{2,1,0:T(8,128)(2,1)S(1)}, u32[]{:S(2)}, u32[]{:S(2)}) async-start(bf16[64,48,128]{2,1,0:T(8,128)(2,1)} %get-tuple-element.18), calls=%async_computation.1 | async-start | bytes 1572864 | tf_op jit(solution)/shard_map/all_to_all | solution.py:402
  36.9 0.0 copy-done.2
  36.9 0.1 reshape.39
  37.0 0.1 reshape.40.gain_ref
  37.1 1.6 %fetch_early.1.early_ref = bf16[3,16,48,512]{3,2,1,0:T(8,128)(2,1)S(1)} custom-call(f32[8,128]{1,0:T(8,128)S(1)} %get-tuple-element.20.after_ref, bf16[64,2,48,512]{3,2,1,0:T(8,128)(2,1)} %bitcast.23), custom_call_target="tpu_custom_call" | custom-call | tf_op jit(solution)/shard_map/fetch_early/pallas_call | solution.py:241
  38.8 11.2 %all-to-all-done.1 = bf16[64,48,128]{2,1,0:T(8,128)(2,1)S(1)} async-done(((bf16[64,48,128]{2,1,0:T(8,128)(2,1)}), bf16[64,48,128]{2,1,0:T(8,128)(2,1)S(1)}, u32[]{:S(2)}, u32[]{:S(2)}) %all-to-all-start.1) | async-done | bytes 786464 | tf_op jit(solution)/shard_map/all_to_all | solution.py:402
  50.0 0.0 copy-start
  50.0 0.0 copy-start.1
  50.0 7.6 %experts.1 = (bf16[64,48,128]{2,1,0:T(8,128)(2,1)}, f32[2,3072]{1,0:T(2,128)S(1)}) custom-call(s32[1]{0:T(128)} %bitcast.2.chip_ref, bf16[3072,128]{1,0:T(8,128)(2,1)S(1)} %bitcast.22, bf16[2,3072]{1,0:T(2,128)(2,1)S(1)} %reshape.40.gain_ref, bf16[3,16,48,512]{3,2,1,0:T(8,128)(2,1)S(1)} %fetch_early.1.early_ref, bf16[64,2,48,512]{3,2,1,0:T(8,128)(2,1)} %bitcast.24, ...), custom_call_target="tpu_custom_call" | custom-call | tf_op jit(solution)/shard_map/experts/pallas_call | solution.py:349
  57.6 6.3 %all-to-all-start.2 = ((bf16[64,48,128]{2,1,0:T(8,128)(2,1)}), bf16[64,48,128]{2,1,0:T(8,128)(2,1)S(1)}, u32[]{:S(2)}, u32[]{:S(2)}) async-start(bf16[64,48,128]{2,1,0:T(8,128)(2,1)} %get-tuple-element.21), calls=%async_computation.2 | async-start | bytes 1572864 | tf_op jit(solution)/shard_map/all_to_all | solution.py:402
  63.9 0.1 reshape.43
  64.0 0.1 copy.17
  64.1 0.1 reshape.44.hidden_ref
  64.2 12.8 %all-to-all-done.2.returned_ref = bf16[64,48,128]{2,1,0:T(8,128)(2,1)S(1)} async-done(((bf16[64,48,128]{2,1,0:T(8,128)(2,1)}), bf16[64,48,128]{2,1,0:T(8,128)(2,1)S(1)}, u32[]{:S(2)}, u32[]{:S(2)}) %all-to-all-start.2) | async-done | bytes 786464 | tf_op jit(solution)/shard_map/all_to_all | solution.py:402
  77.0 0.0 copy-done
  77.0 0.0 copy-done.1
  77.0 0.7 mix.1
  77.7 3.8 %collective-permute-start = (bf16[24,128]{1,0:T(8,128)(2,1)S(1)}, bf16[24,128]{1,0:T(8,128)(2,1)S(1)}, u32[]{:S(2)}, u32[]{:S(2)}) collective-permute-start(bf16[24,128]{1,0:T(8,128)(2,1)S(1)} %get-tuple-element.24), channel_id=1, source_target_pairs={{0,64},{64,0},{1,65},{65,1},{2,66},{66,2},{3,67},{67,3},{4,68},{68... | collective-permute-start | bytes 18440 | tf_op jit(solution)/shard_map/ppermute | solution.py:439
  81.5 0.8 collective-permute-done
  82.4 0.6 pad_maximum_fusion
  (3 shorter events, 0.0 us)
Async XLA Ops:
  0.0 36.9 %copy-start.2 = (bf16[6144]{0:T(1024)(128)(2,1)S(1)}, bf16[6144]{0:T(1024)(128)(2,1)}, u32[]{:S(2)}) copy-start(bf16[6144]{0:T(1024)(128)(2,1)} %param.22) | copy-start | bytes 36868
  3.4 26.5 %all-to-all-start = ((bf16[64,25,2,128]{3,2,1,0:T(2,128)(2,1)}), bf16[64,25,2,128]{3,2,1,0:T(2,128)(2,1)S(1)}, u32[]{:S(2)}, u32[]{:S(2)}) async-start(bf16[64,25,2,128]{3,2,1,0:T(2,128)(2,1)} %bitcast.3), calls=%async_computation | async-start | bytes 1638400 | tf_op jit(solution)/shard_map/all_to_all | solution.py:402
  31.6 18.4 %all-to-all-start.1 = ((bf16[64,48,128]{2,1,0:T(8,128)(2,1)}), bf16[64,48,128]{2,1,0:T(8,128)(2,1)S(1)}, u32[]{:S(2)}, u32[]{:S(2)}) async-start(bf16[64,48,128]{2,1,0:T(8,128)(2,1)} %get-tuple-element.18), calls=%async_computation.1 | async-start | bytes 1572864 | tf_op jit(solution)/shard_map/all_to_all | solution.py:402
  50.0 27.0 %copy-start = (s32[2,2]{1,0:T(2,128)S(1)}, s32[2,2]{1,0:T(2,128)}, u32[]{:S(2)}) copy-start(s32[2,2]{1,0:T(2,128)} %ids_ref.1) | copy-start | bytes 52
  50.0 27.0 %copy-start.1 = (f32[2,2]{1,0:T(2,128)S(1)}, f32[2,2]{1,0:T(2,128)}, u32[]{:S(2)}) copy-start(f32[2,2]{1,0:T(2,128)} %gates_ref.1) | copy-start | bytes 52
  57.6 19.4 %all-to-all-start.2 = ((bf16[64,48,128]{2,1,0:T(8,128)(2,1)}), bf16[64,48,128]{2,1,0:T(8,128)(2,1)S(1)}, u32[]{:S(2)}, u32[]{:S(2)}) async-start(bf16[64,48,128]{2,1,0:T(8,128)(2,1)} %get-tuple-element.21), calls=%async_computation.2 | async-start | bytes 1572864 | tf_op jit(solution)/shard_map/all_to_all | solution.py:402
  77.7 4.6 %collective-permute-start = (bf16[24,128]{1,0:T(8,128)(2,1)S(1)}, bf16[24,128]{1,0:T(8,128)(2,1)S(1)}, u32[]{:S(2)}, u32[]{:S(2)}) collective-permute-start(bf16[24,128]{1,0:T(8,128)(2,1)S(1)} %get-tuple-element.24), channel_id=1, source_target_pairs={{0,64},{64,0},{1,65},{65,1},{2,66},{66,2},{3,67},{67,3},{4,68},{68... | collective-permute-start | bytes 18440 | tf_op jit(solution)/shard_map/ppermute | solution.py:439

commit v7 on v6

--- a/solution.py
+++ b/solution.py
@@ -29,6 +29,18 @@
 DOWN = 1024
 
 epsilon = 1e-05
+
+
+def walk():
+    places = []
+    for step in range(DEVS):
+        x, y, z = (step * 43 % 64 // 16, step * 43 % 16 // 4, step * 43 % 4)
+        places.append((x + 2) % 4 * 16 + (y + 2) % 4 * 4 + (z + 2) % 4)
+    return places
+
+
+ORDER = walk()
+PLACE = [ORDER.index(chip) for chip in range(DEVS)]
 
 VMEM_BLOCK = pl.BlockSpec(memory_space=pltpu.VMEM)
 SMEM_BLOCK = pl.BlockSpec(memory_space=pltpu.SMEM)
@@ -115,7 +127,7 @@
         pattern[chip * SENT : chip * SENT + ROWS, :] = context
     for group in range(DEVS // BATCH):
         for chip in range(BATCH):
-            wanted = COLS * (group * BATCH + chip) // 128
+            wanted = COLS * ORDER[group * BATCH + chip] // 128
             pattern[chip * SENT + ROWS : chip * SENT + SENT, :] = residual_rows[
                 pl.ds(first_row + wanted, 2), :
             ]
@@ -250,7 +262,7 @@
 
 
 def expert_kernel(
-    chip_ref,
+    place_ref,
     hidden_ref,
     gain_ref,
     early_ref,
@@ -287,17 +299,25 @@
         copies[2, step].start()
 
     squares = jnp.zeros((128, 128), jnp.float32)
-    for block in range(HALF_D // 128):
-        lanes = slice(block * 128, block * 128 + 128)
-        turned = hidden_ref[lanes, :].astype(jnp.float32).T
-        flipped[:, lanes] = turned
-        squares = squares + turned * turned
-        gain = gain_ref[:, lanes].astype(jnp.float32)
-        scaled[0:DEVS, lanes] = (turned[0:DEVS] * gain[0:1]).astype(jnp.bfloat16)
-        scaled[DEVS:128, lanes] = (turned[DEVS:128] * gain[1:2]).astype(jnp.bfloat16)
-    chip = chip_ref[0]
-    own_ref[0:1, :] = flipped[pl.ds(chip, 1), :]
-    own_ref[1:2, :] = flipped[pl.ds(chip + DEVS, 1), :]
+    for block in range(HALF_D // 384):
+        columns = jnp.concatenate(
+            [
+                hidden_ref[PLACE[chip] * HALF : PLACE[chip] * HALF + HALF, :].astype(jnp.float32)
+                for chip in range(block * 8, block * 8 + 8)
+            ],
+            axis=0,
+        )
+        for third in range(3):
+            turned = columns[third * 128 : third * 128 + 128].T
+            lanes = slice(block * 384 + third * 128, block * 384 + third * 128 + 128)
+            flipped[:, lanes] = turned
+            squares = squares + turned * turned
+            gain = gain_ref[:, lanes].astype(jnp.float32)
+            scaled[0:DEVS, lanes] = (turned[0:DEVS] * gain[0:1]).astype(jnp.bfloat16)
+            scaled[DEVS:128, lanes] = (turned[DEVS:128] * gain[1:2]).astype(jnp.bfloat16)
+    place = place_ref[0]
+    own_ref[0:1, :] = flipped[pl.ds(place, 1), :]
+    own_ref[1:2, :] = flipped[pl.ds(place + DEVS, 1), :]
     total = jnp.sum(squares, axis=1, keepdims=True)
     factor = lax.rsqrt((total[0:DEVS] + total[DEVS:128]) * (1.0 / D) + epsilon)
 
@@ -345,7 +365,7 @@
         ].astype(jnp.bfloat16)
 
 
-def run_experts(chip, hidden, gain, early, w_gate, w_up, w_down):
+def run_experts(place, hidden, gain, early, w_gate, w_up, w_down):
     return pl.pallas_call(
         expert_kernel,
         out_shape=(
@@ -365,7 +385,7 @@
         ],
         compiler_params=pltpu.CompilerParams(vmem_limit_bytes=40 << 20),
         name="experts",
-    )(chip, hidden, gain, *in_vmem(early), *in_hbm(w_gate, w_up, w_down))
+    )(place, hidden, gain, *in_vmem(early), *in_hbm(w_gate, w_up, w_down))
 
 
 def mix_kernel(core_ref, ids_ref, gates_ref, returned_ref, hidden_ref, kept_ref, given_ref):
@@ -378,8 +398,9 @@
                 ids_ref[core, choice] == expert, gates_ref[core, choice], jnp.float32(0.0)
             )
         block = jnp.zeros((ROWS, 128), jnp.float32)
-        for source in range(DEVS // EXPERTS):
-            block = block + returned_ref[expert * (DEVS // EXPERTS) + source].astype(jnp.float32)
+        for place in range(DEVS):
+            if ORDER[place] // (DEVS // EXPERTS) == expert:
+                block = block + returned_ref[place].astype(jnp.float32)
         total = total + block * share
     lower, upper = total[0 : ROWS // 2], total[ROWS // 2 : ROWS]
     kept_ref[...] = jnp.where(core == 0, lower, upper).astype(jnp.bfloat16)
@@ -399,7 +420,9 @@
 
 
 def exchange(parts):
-    return lax.all_to_all(parts, "dev", split_axis=0, concat_axis=0, tiled=True)
+    return lax.all_to_all(
+        parts, "dev", split_axis=0, concat_axis=0, tiled=True, axis_index_groups=[ORDER]
+    )
 
 
 def local(
@@ -420,6 +443,7 @@
 ):
     core = lax.axis_index("side").astype(jnp.int32).reshape(1)
     chip = lax.axis_index("dev").astype(jnp.int32).reshape(1)
+    place = jnp.asarray(PLACE, jnp.int32)[chip]
     outgoing, mark = attend(
         core, cached, query, new_key, new_value, residual, key_cache, value_cache
     )
@@ -432,7 +456,7 @@
     w_up = w_up.reshape(DEVS, 2, HALF, UNITS)
     early = fetch_early(mark, w_gate)
     hidden = exchange(packed).reshape(HALF_D, 128)
-    partial_value, own_hidden = run_experts(chip, hidden, gain, early, w_gate, w_up, w_down)
+    partial_value, own_hidden = run_experts(place, hidden, gain, early, w_gate, w_up, w_down)
     returned = exchange(partial_value)
     own_hidden = own_hidden.reshape(2, DEVS, HALF).transpose(1, 0, 2).reshape(ROWS, 128)
     kept, given = mix(core, expert_ids, gate_weights, returned, own_hidden)

time: 83.5 us -> 78.4 us (0.939)
  waiting for transfers between devices: 38.1 us -> 19.2 us
  starting transfers between devices: 27.4 us -> 39.9 us
    all_to_all x3, waiting for transfers between devices: 37.3 us -> 18.4 us  [exchange(): lax.all_to_all(parts, 'dev', split_axis=0, concat_axis=0, tiled=True, axi...]
    all_to_all x3, starting transfers between devices: 23.5 us -> 36.4 us  [exchange(): lax.all_to_all(parts, 'dev', split_axis=0, concat_axis=0, tiled=True, axi...]
where the time goes in v7:
time: 78.4 us; the launch traced here: 77.8 us
  starting transfers between devices  39.9 us (51%)
  waiting for transfers between devices  19.2 us (24%)
  Pallas kernels  16.9 us (22%)
  local copies, waits for them, and re-layouts  1.11 us (1%)
    all_to_all x3, starting transfers between devices, exchange(): lax.all_to_all(parts, 'dev', split_axis=0, concat_axis=0, tiled=True, axi...  36.4 us
    all_to_all x3, waiting for transfers between devices, exchange(): lax.all_to_all(parts, 'dev', split_axis=0, concat_axis=0, tiled=True, axi...  18.4 us
    pallas_call x1, Pallas kernels, run_experts(): pl.pallas_call(expert_kernel, out_shape=(pltpu.HBM((DEVS, ROWS, 128), jnp...  8.16 us
    ppermute x1, starting transfers between devices, local(): taken = lax.ppermute(given, 'side', [(0, 1), (1, 0)])  3.54 us
    pallas_call x1, Pallas kernels, attend(): pl.pallas_call(attend_kernel, out_shape=(jax.ShapeDtypeStruct((DEVS * SEN...  3.42 us
    pallas_call x1, Pallas kernels, project(): pl.pallas_call(project_kernel, out_shape=(jax.ShapeDtypeStruct((DEVS, HAL...  1.69 us
    pallas_call x1, Pallas kernels, fetch_early(): pl.pallas_call(early_kernel, out_shape=pltpu.VMEM((EARLY, PART, HALF, UNI...  1.63 us
  transfers between devices with their start and end apart: 4, of which 4 were waited for; matrix products, arithmetic and copies ran while one was open for 1% of the time, Pallas kernels for 4%

profile of v7, /device:TPU:1, one launch (start us, length us, event | category | flops | bytes accessed | tf_op | source)
XLA Modules:
  0.0 77.8 jit_solution(14528029840666262174)
XLA Ops:
  0.0 0.0 copy-start.3
  0.0 0.0 copy-start.2
  0.0 3.4 %attend.1 = (bf16[3200,128]{1,0:T(8,128)(2,1)}, f32[8,128]{1,0:T(8,128)S(1)}) custom-call(s32[1]{0:T(128)} %bitcast.core_ref, s32[2]{0:T(128)} %cached_ref.1, bf16[2,6144]{1,0:T(2,128)(2,1)} %query_ref.1, bf16[2,1024]{1,0:T(2,128)(2,1)} %new_key_ref.1, bf16[2,1024]{1,0:T(2,128)(2,1)} %new_value_ref.1, bf16[2,6144]{1,0:T(2,128)(2,1)} %residual_ref.1, ...), custom_call_target="tpu_custom_call" | custom-call | tf_op jit(solution)/shard_map/attend/pallas_call | solution.py:143
  3.4 14.3 %all-to-all-start = ((bf16[64,25,2,128]{3,2,1,0:T(2,128)(2,1)}), bf16[64,25,2,128]{3,2,1,0:T(2,128)(2,1)S(1)}, u32[]{:S(2)}, u32[]{:S(2)}) async-start(bf16[64,25,2,128]{3,2,1,0:T(2,128)(2,1)} %bitcast.4), calls=%async_computation | async-start | bytes 1638400 | tf_op jit(solution)/shard_map/all_to_all | solution.py:423
  17.8 1.3 %fetch.1.weight_ref = bf16[96,6144]{1,0:T(8,128)(2,1)S(1)} custom-call(f32[8,128]{1,0:T(8,128)S(1)} %get-tuple-element.17.after_ref, bf16[96,6144]{1,0:T(8,128)(2,1)} %bitcast.27), custom_call_target="tpu_custom_call" | custom-call | bytes 2359296 | tf_op jit(solution)/shard_map/fetch/pallas_call | solution.py:186
  19.1 7.2 %all-to-all-done = bf16[64,25,2,128]{3,2,1,0:T(2,128)(2,1)S(1)} async-done(((bf16[64,25,2,128]{3,2,1,0:T(2,128)(2,1)}), bf16[64,25,2,128]{3,2,1,0:T(2,128)(2,1)S(1)}, u32[]{:S(2)}, u32[]{:S(2)}) %all-to-all-start) | async-done | bytes 819232 | tf_op jit(solution)/shard_map/all_to_all | solution.py:423
  26.2 1.7 %project.1 = (bf16[64,48,128]{2,1,0:T(8,128)(2,1)}, f32[8,128]{1,0:T(8,128)S(1)}) custom-call(s32[1]{0:T(128)} %bitcast.2.chip_ref, bf16[3200,128]{1,0:T(8,128)(2,1)S(1)} %bitcast.22, bf16[96,6144]{1,0:T(8,128)(2,1)S(1)} %fetch.1.weight_ref), custom_call_target="tpu_custom_call" | custom-call | tf_op jit(solution)/shard_map/project/pallas_call | solution.py:222
  27.9 11.2 %all-to-all-start.1 = ((bf16[64,48,128]{2,1,0:T(8,128)(2,1)}), bf16[64,48,128]{2,1,0:T(8,128)(2,1)S(1)}, u32[]{:S(2)}, u32[]{:S(2)}) async-start(bf16[64,48,128]{2,1,0:T(8,128)(2,1)} %get-tuple-element.18), calls=%async_computation.1 | async-start | bytes 1572864 | tf_op jit(solution)/shard_map/all_to_all | solution.py:423
  39.1 0.0 copy-done.2
  39.1 0.1 reshape.39
  39.2 0.1 reshape.40.gain_ref
  39.3 0.0 copy-done.3
  39.3 0.6 dynamic-slice.4.place_ref
  39.9 1.6 %fetch_early.1.early_ref = bf16[3,16,48,512]{3,2,1,0:T(8,128)(2,1)S(1)} custom-call(f32[8,128]{1,0:T(8,128)S(1)} %get-tuple-element.20.after_ref, bf16[64,2,48,512]{3,2,1,0:T(8,128)(2,1)} %bitcast.24), custom_call_target="tpu_custom_call" | custom-call | tf_op jit(solution)/shard_map/fetch_early/pallas_call | solution.py:253
  41.6 5.0 %all-to-all-done.1 = bf16[64,48,128]{2,1,0:T(8,128)(2,1)S(1)} async-done(((bf16[64,48,128]{2,1,0:T(8,128)(2,1)}), bf16[64,48,128]{2,1,0:T(8,128)(2,1)S(1)}, u32[]{:S(2)}, u32[]{:S(2)}) %all-to-all-start.1) | async-done | bytes 786464 | tf_op jit(solution)/shard_map/all_to_all | solution.py:423
  46.6 0.0 copy-start
  46.6 0.0 copy-start.1
  46.6 8.2 %experts.1 = (bf16[64,48,128]{2,1,0:T(8,128)(2,1)}, f32[2,3072]{1,0:T(2,128)S(1)}) custom-call(s32[1]{0:T(128)} %dynamic-slice.4.place_ref, bf16[3072,128]{1,0:T(8,128)(2,1)S(1)} %bitcast.23, bf16[2,3072]{1,0:T(2,128)(2,1)S(1)} %reshape.40.gain_ref, bf16[3,16,48,512]{3,2,1,0:T(8,128)(2,1)S(1)} %fetch_early.1.early_ref, bf16[64,2,48,512]{3,2,1,0:T(8,128)(2,1)} %bitcast.25, ...), custom_call_target="tpu_custom_call" | custom-call | tf_op jit(solution)/shard_map/experts/pallas_call | solution.py:369
  54.7 10.9 %all-to-all-start.2 = ((bf16[64,48,128]{2,1,0:T(8,128)(2,1)}), bf16[64,48,128]{2,1,0:T(8,128)(2,1)S(1)}, u32[]{:S(2)}, u32[]{:S(2)}) async-start(bf16[64,48,128]{2,1,0:T(8,128)(2,1)} %get-tuple-element.21), calls=%async_computation.2 | async-start | bytes 1572864 | tf_op jit(solution)/shard_map/all_to_all | solution.py:423
  65.6 0.1 reshape.43
  65.7 0.1 copy.18
  65.8 0.1 reshape.44.hidden_ref
  65.9 6.2 %all-to-all-done.2.returned_ref = bf16[64,48,128]{2,1,0:T(8,128)(2,1)S(1)} async-done(((bf16[64,48,128]{2,1,0:T(8,128)(2,1)}), bf16[64,48,128]{2,1,0:T(8,128)(2,1)S(1)}, u32[]{:S(2)}, u32[]{:S(2)}) %all-to-all-start.2) | async-done | bytes 786464 | tf_op jit(solution)/shard_map/all_to_all | solution.py:423
  72.1 0.0 copy-done
  72.1 0.0 copy-done.1
  72.1 0.7 mix.1
  72.8 3.5 %collective-permute-start = (bf16[24,128]{1,0:T(8,128)(2,1)S(1)}, bf16[24,128]{1,0:T(8,128)(2,1)S(1)}, u32[]{:S(2)}, u32[]{:S(2)}) collective-permute-start(bf16[24,128]{1,0:T(8,128)(2,1)S(1)} %get-tuple-element.24), channel_id=1, source_target_pairs={{0,64},{64,0},{1,65},{65,1},{2,66},{66,2},{3,67},{67,3},{4,68},{68... | collective-permute-start | bytes 18440 | tf_op jit(solution)/shard_map/ppermute | solution.py:463
  76.4 0.8 %collective-permute-done = bf16[24,128]{1,0:T(8,128)(2,1)S(1)} collective-permute-done((bf16[24,128]{1,0:T(8,128)(2,1)S(1)}, bf16[24,128]{1,0:T(8,128)(2,1)S(1)}, u32[]{:S(2)}, u32[]{:S(2)}) %collective-permute-start) | collective-permute-done | bytes 6176 | tf_op jit(solution)/shard_map/ppermute | solution.py:463
  77.2 0.6 pad_maximum_fusion
  (3 shorter events, 0.0 us)
Async XLA Ops:
  0.0 39.3 %copy-start.3 = (s32[64]{0:T(128)S(1)}, s32[64]{0:T(128)}, u32[]{:S(2)}) copy-start(s32[64]{0:T(128)} %constant.15.clone..sunk.2) | copy-start | bytes 772
  0.0 39.1 %copy-start.2 = (bf16[6144]{0:T(1024)(128)(2,1)S(1)}, bf16[6144]{0:T(1024)(128)(2,1)}, u32[]{:S(2)}) copy-start(bf16[6144]{0:T(1024)(128)(2,1)} %param.23) | copy-start | bytes 36868
  3.4 22.8 %all-to-all-start = ((bf16[64,25,2,128]{3,2,1,0:T(2,128)(2,1)}), bf16[64,25,2,128]{3,2,1,0:T(2,128)(2,1)S(1)}, u32[]{:S(2)}, u32[]{:S(2)}) async-start(bf16[64,25,2,128]{3,2,1,0:T(2,128)(2,1)} %bitcast.4), calls=%async_computation | async-start | bytes 1638400 | tf_op jit(solution)/shard_map/all_to_all | solution.py:423
  27.9 18.6 %all-to-all-start.1 = ((bf16[64,48,128]{2,1,0:T(8,128)(2,1)}), bf16[64,48,128]{2,1,0:T(8,128)(2,1)S(1)}, u32[]{:S(2)}, u32[]{:S(2)}) async-start(bf16[64,48,128]{2,1,0:T(8,128)(2,1)} %get-tuple-element.18), calls=%async_computation.1 | async-start | bytes 1572864 | tf_op jit(solution)/shard_map/all_to_all | solution.py:423
  46.6 25.6 %copy-start = (s32[2,2]{1,0:T(2,128)S(1)}, s32[2,2]{1,0:T(2,128)}, u32[]{:S(2)}) copy-start(s32[2,2]{1,0:T(2,128)} %ids_ref.1) | copy-start | bytes 52
  46.6 25.6 %copy-start.1 = (f32[2,2]{1,0:T(2,128)S(1)}, f32[2,2]{1,0:T(2,128)}, u32[]{:S(2)}) copy-start(f32[2,2]{1,0:T(2,128)} %gates_ref.1) | copy-start | bytes 52
  54.7 17.4 %all-to-all-start.2 = ((bf16[64,48,128]{2,1,0:T(8,128)(2,1)}), bf16[64,48,128]{2,1,0:T(8,128)(2,1)S(1)}, u32[]{:S(2)}, u32[]{:S(2)}) async-start(bf16[64,48,128]{2,1,0:T(8,128)(2,1)} %get-tuple-element.21), calls=%async_computation.2 | async-start | bytes 1572864 | tf_op jit(solution)/shard_map/all_to_all | solution.py:423
  72.8 4.4 %collective-permute-start = (bf16[24,128]{1,0:T(8,128)(2,1)S(1)}, bf16[24,128]{1,0:T(8,128)(2,1)S(1)}, u32[]{:S(2)}, u32[]{:S(2)}) collective-permute-start(bf16[24,128]{1,0:T(8,128)(2,1)S(1)} %get-tuple-element.24), channel_id=1, source_target_pairs={{0,64},{64,0},{1,65},{65,1},{2,66},{66,2},{3,67},{67,3},{4,68},{68... | collective-permute-start | bytes 18440 | tf_op jit(solution)/shard_map/ppermute | solution.py:463

commit v8 on v7

--- a/solution.py
+++ b/solution.py
@@ -31,15 +31,8 @@
 epsilon = 1e-05
 
 
-def walk():
-    places = []
-    for step in range(DEVS):
-        x, y, z = (step * 43 % 64 // 16, step * 43 % 16 // 4, step * 43 % 4)
-        places.append((x + 2) % 4 * 16 + (y + 2) % 4 * 4 + (z + 2) % 4)
-    return places
-
-
-ORDER = walk()
+STRIDE, UNSTRIDE, FIRST = 43, 3, 42
+ORDER = [step * STRIDE % DEVS ^ FIRST for step in range(DEVS)]
 PLACE = [ORDER.index(chip) for chip in range(DEVS)]
 
 VMEM_BLOCK = pl.BlockSpec(memory_space=pltpu.VMEM)
@@ -102,7 +95,7 @@
     own_keys = []
     for kv in range(KV_HEADS):
         lanes = slice(kv * 128, kv * 128 + 128)
-        scores.append(last_dims(narrow[kv * 8 : kv * 8 + 8], key_ref[0, :, lanes]))
+        scores.append(last_dims(narrow[kv * 8 : kv * 8 + 8], key_ref[core, :, lanes]))
         own_keys.append(jnp.broadcast_to(new_key[:, lanes], (8, 128)))
     scores = jnp.concatenate(scores, axis=0) * scale
     own_score = jnp.sum(queries * jnp.concatenate(own_keys, axis=0), axis=1, keepdims=True) * scale
@@ -117,7 +110,7 @@
     for kv in range(KV_HEADS):
         lanes = slice(kv * 128, kv * 128 + 128)
         context = jnp.dot(
-            weights[kv * 8 : kv * 8 + 8], value_ref[0, :, lanes], preferred_element_type=jnp.float32
+            weights[kv * 8 : kv * 8 + 8], value_ref[core, :, lanes], preferred_element_type=jnp.float32
         )
         context = context + own_weight[kv * 8 : kv * 8 + 8] * new_value[:, lanes]
         context_rows[kv * GROUP : kv * GROUP + 8, :] = context
@@ -136,35 +129,20 @@
 
 
 def attend(core, cached, query, new_key, new_value, residual, key_cache, value_cache):
-    def whole(shape):
-        return pl.BlockSpec(shape, lambda step, core, cached: (0,) * len(shape))
-
-    cache = pl.BlockSpec((1, CACHE_LEN, 1024), lambda step, core, cached: (core[0], 0, 0))
     return pl.pallas_call(
         attend_kernel,
         out_shape=(
             jax.ShapeDtypeStruct((DEVS * SENT, 128), jnp.bfloat16),
             jax.ShapeDtypeStruct((8, 128), jnp.float32),
         ),
-        grid_spec=pltpu.PrefetchScalarGridSpec(
-            num_scalar_prefetch=2,
-            grid=(1,),
-            in_specs=[
-                whole((2, D)),
-                whole((2, 1024)),
-                whole((2, 1024)),
-                whole((2, D)),
-                cache,
-                cache,
-            ],
-            out_specs=(whole((DEVS * SENT, 128)), whole((8, 128))),
-            scratch_shapes=[
-                pltpu.VMEM((128, 128), jnp.float32),
-                pltpu.VMEM((128, 128), jnp.float32),
-                pltpu.VMEM((ROWS + 8, 128), jnp.float32),
-                pltpu.VMEM((BATCH * SENT, 128), jnp.float32),
-            ],
-        ),
+        in_specs=[SMEM_BLOCK, SMEM_BLOCK] + [VMEM_BLOCK] * 6,
+        out_specs=(VMEM_BLOCK, VMEM_BLOCK),
+        scratch_shapes=[
+            pltpu.VMEM((128, 128), jnp.float32),
+            pltpu.VMEM((128, 128), jnp.float32),
+            pltpu.VMEM((ROWS + 8, 128), jnp.float32),
+            pltpu.VMEM((BATCH * SENT, 128), jnp.float32),
+        ],
         compiler_params=pltpu.CompilerParams(vmem_limit_bytes=8 << 20),
         name="attend",
     )(core, *in_hbm(cached, query, new_key, new_value, residual, key_cache, value_cache))
@@ -262,7 +240,7 @@
 
 
 def expert_kernel(
-    place_ref,
+    chip_ref,
     hidden_ref,
     gain_ref,
     early_ref,
@@ -315,7 +293,7 @@
             gain = gain_ref[:, lanes].astype(jnp.float32)
             scaled[0:DEVS, lanes] = (turned[0:DEVS] * gain[0:1]).astype(jnp.bfloat16)
             scaled[DEVS:128, lanes] = (turned[DEVS:128] * gain[1:2]).astype(jnp.bfloat16)
-    place = place_ref[0]
+    place = lax.rem(jnp.bitwise_xor(chip_ref[0], FIRST) * UNSTRIDE, DEVS)
     own_ref[0:1, :] = flipped[pl.ds(place, 1), :]
     own_ref[1:2, :] = flipped[pl.ds(place + DEVS, 1), :]
     total = jnp.sum(squares, axis=1, keepdims=True)
@@ -365,7 +343,7 @@
         ].astype(jnp.bfloat16)
 
 
-def run_experts(place, hidden, gain, early, w_gate, w_up, w_down):
+def run_experts(chip, hidden, gain, early, w_gate, w_up, w_down):
     return pl.pallas_call(
         expert_kernel,
         out_shape=(
@@ -385,7 +363,7 @@
         ],
         compiler_params=pltpu.CompilerParams(vmem_limit_bytes=40 << 20),
         name="experts",
-    )(place, hidden, gain, *in_vmem(early), *in_hbm(w_gate, w_up, w_down))
+    )(chip, hidden, gain, *in_vmem(early), *in_hbm(w_gate, w_up, w_down))
 
 
 def mix_kernel(core_ref, ids_ref, gates_ref, returned_ref, hidden_ref, kept_ref, given_ref):
@@ -443,7 +421,6 @@
 ):
     core = lax.axis_index("side").astype(jnp.int32).reshape(1)
     chip = lax.axis_index("dev").astype(jnp.int32).reshape(1)
-    place = jnp.asarray(PLACE, jnp.int32)[chip]
     outgoing, mark = attend(
         core, cached, query, new_key, new_value, residual, key_cache, value_cache
     )
@@ -456,7 +433,7 @@
     w_up = w_up.reshape(DEVS, 2, HALF, UNITS)
     early = fetch_early(mark, w_gate)
     hidden = exchange(packed).reshape(HALF_D, 128)
-    partial_value, own_hidden = run_experts(place, hidden, gain, early, w_gate, w_up, w_down)
+    partial_value, own_hidden = run_experts(chip, hidden, gain, early, w_gate, w_up, w_down)
     returned = exchange(partial_value)
     own_hidden = own_hidden.reshape(2, DEVS, HALF).transpose(1, 0, 2).reshape(ROWS, 128)
     kept, given = mix(core, expert_ids, gate_weights, returned, own_hidden)

time: 78.4 us -> 77.3 us (0.986)
  Pallas kernels: 16.9 us -> 15.9 us
where the time goes in v8:
time: 77.3 us; the launch traced here: 76.8 us
  starting transfers between devices  39.9 us (52%)
  waiting for transfers between devices  19.8 us (26%)
  Pallas kernels  15.9 us (21%)
    all_to_all x3, starting transfers between devices, exchange(): lax.all_to_all(parts, 'dev', split_axis=0, concat_axis=0, tiled=True, axi...  36.4 us
    all_to_all x3, waiting for transfers between devices, exchange(): lax.all_to_all(parts, 'dev', split_axis=0, concat_axis=0, tiled=True, axi...  19 us
    pallas_call x1, Pallas kernels, run_experts(): pl.pallas_call(expert_kernel, out_shape=(pltpu.HBM((DEVS, ROWS, 128), jnp...  7.75 us
    ppermute x1, starting transfers between devices, local(): taken = lax.ppermute(given, 'side', [(0, 1), (1, 0)])  3.54 us
    pallas_call x1, Pallas kernels, attend(): pl.pallas_call(attend_kernel, out_shape=(jax.ShapeDtypeStruct((DEVS * SEN...  2.82 us
    pallas_call x1, Pallas kernels, project(): pl.pallas_call(project_kernel, out_shape=(jax.ShapeDtypeStruct((DEVS, HAL...  1.7 us
    pallas_call x1, Pallas kernels, fetch_early(): pl.pallas_call(early_kernel, out_shape=pltpu.VMEM((EARLY, PART, HALF, UNI...  1.64 us
  transfers between devices with their start and end apart: 4, of which 4 were waited for; matrix products, arithmetic and copies ran while one was open for 1% of the time, Pallas kernels for 4%

profile of v8, /device:TPU:1, one launch (start us, length us, event | category | flops | bytes accessed | tf_op | source)
XLA Modules:
  0.0 76.8 jit_solution(3517033878645777825)
XLA Ops:
  0.0 0.0 copy-start.2
  0.0 2.8 %attend.1 = (bf16[3200,128]{1,0:T(8,128)(2,1)}, f32[8,128]{1,0:T(8,128)S(1)}) custom-call(s32[1]{0:T(128)} %bitcast.core_ref, s32[2]{0:T(128)} %cached_ref.1, bf16[2,6144]{1,0:T(2,128)(2,1)} %query_ref.1, bf16[2,1024]{1,0:T(2,128)(2,1)} %new_key_ref.1, bf16[2,1024]{1,0:T(2,128)(2,1)} %new_value_ref.1, bf16[2,6144]{1,0:T(2,128)(2,1)} %residual_ref.1, ...), custom_call_target="tpu_custom_call" | custom-call | tf_op jit(solution)/shard_map/attend/pallas_call | solution.py:132
  2.8 14.3 %all-to-all-start = ((bf16[64,25,2,128]{3,2,1,0:T(2,128)(2,1)}), bf16[64,25,2,128]{3,2,1,0:T(2,128)(2,1)S(1)}, u32[]{:S(2)}, u32[]{:S(2)}) async-start(bf16[64,25,2,128]{3,2,1,0:T(2,128)(2,1)} %bitcast.3), calls=%async_computation | async-start | bytes 1638400 | tf_op jit(solution)/shard_map/all_to_all | solution.py:401
  17.2 1.3 %fetch.1.weight_ref = bf16[96,6144]{1,0:T(8,128)(2,1)S(1)} custom-call(f32[8,128]{1,0:T(8,128)S(1)} %get-tuple-element.17.after_ref, bf16[96,6144]{1,0:T(8,128)(2,1)} %bitcast.26), custom_call_target="tpu_custom_call" | custom-call | bytes 2359296 | tf_op jit(solution)/shard_map/fetch/pallas_call | solution.py:164
  18.5 7.2 %all-to-all-done = bf16[64,25,2,128]{3,2,1,0:T(2,128)(2,1)S(1)} async-done(((bf16[64,25,2,128]{3,2,1,0:T(2,128)(2,1)}), bf16[64,25,2,128]{3,2,1,0:T(2,128)(2,1)S(1)}, u32[]{:S(2)}, u32[]{:S(2)}) %all-to-all-start) | async-done | bytes 819232 | tf_op jit(solution)/shard_map/all_to_all | solution.py:401
  25.6 1.7 %project.1 = (bf16[64,48,128]{2,1,0:T(8,128)(2,1)}, f32[8,128]{1,0:T(8,128)S(1)}) custom-call(s32[1]{0:T(128)} %bitcast.2.chip_ref, bf16[3200,128]{1,0:T(8,128)(2,1)S(1)} %bitcast.21, bf16[96,6144]{1,0:T(8,128)(2,1)S(1)} %fetch.1.weight_ref), custom_call_target="tpu_custom_call" | custom-call | tf_op jit(solution)/shard_map/project/pallas_call | solution.py:200
  27.3 11.2 %all-to-all-start.1 = ((bf16[64,48,128]{2,1,0:T(8,128)(2,1)}), bf16[64,48,128]{2,1,0:T(8,128)(2,1)S(1)}, u32[]{:S(2)}, u32[]{:S(2)}) async-start(bf16[64,48,128]{2,1,0:T(8,128)(2,1)} %get-tuple-element.18), calls=%async_computation.1 | async-start | bytes 1572864 | tf_op jit(solution)/shard_map/all_to_all | solution.py:401
  38.5 0.0 copy-done.2
  38.5 0.1 reshape.39
  38.6 0.1 reshape.40.gain_ref
  38.7 1.6 %fetch_early.1.early_ref = bf16[3,16,48,512]{3,2,1,0:T(8,128)(2,1)S(1)} custom-call(f32[8,128]{1,0:T(8,128)S(1)} %get-tuple-element.20.after_ref, bf16[64,2,48,512]{3,2,1,0:T(8,128)(2,1)} %bitcast.23), custom_call_target="tpu_custom_call" | custom-call | tf_op jit(solution)/shard_map/fetch_early/pallas_call | solution.py:231
  40.4 5.6 %all-to-all-done.1 = bf16[64,48,128]{2,1,0:T(8,128)(2,1)S(1)} async-done(((bf16[64,48,128]{2,1,0:T(8,128)(2,1)}), bf16[64,48,128]{2,1,0:T(8,128)(2,1)S(1)}, u32[]{:S(2)}, u32[]{:S(2)}) %all-to-all-start.1) | async-done | bytes 786464 | tf_op jit(solution)/shard_map/all_to_all | solution.py:401
  46.0 0.0 copy-start
  46.0 0.0 copy-start.1
  46.0 7.8 %experts.1 = (bf16[64,48,128]{2,1,0:T(8,128)(2,1)}, f32[2,3072]{1,0:T(2,128)S(1)}) custom-call(s32[1]{0:T(128)} %bitcast.2.chip_ref, bf16[3072,128]{1,0:T(8,128)(2,1)S(1)} %bitcast.22, bf16[2,3072]{1,0:T(2,128)(2,1)S(1)} %reshape.40.gain_ref, bf16[3,16,48,512]{3,2,1,0:T(8,128)(2,1)S(1)} %fetch_early.1.early_ref, bf16[64,2,48,512]{3,2,1,0:T(8,128)(2,1)} %bitcast.24, ...), custom_call_target="tpu_custom_call" | custom-call | tf_op jit(solution)/shard_map/experts/pallas_call | solution.py:347
  53.7 10.9 %all-to-all-start.2 = ((bf16[64,48,128]{2,1,0:T(8,128)(2,1)}), bf16[64,48,128]{2,1,0:T(8,128)(2,1)S(1)}, u32[]{:S(2)}, u32[]{:S(2)}) async-start(bf16[64,48,128]{2,1,0:T(8,128)(2,1)} %get-tuple-element.21), calls=%async_computation.2 | async-start | bytes 1572864 | tf_op jit(solution)/shard_map/all_to_all | solution.py:401
  64.6 0.1 reshape.43
  64.7 0.1 copy.17
  64.8 0.1 reshape.44.hidden_ref
  64.9 6.2 %all-to-all-done.2.returned_ref = bf16[64,48,128]{2,1,0:T(8,128)(2,1)S(1)} async-done(((bf16[64,48,128]{2,1,0:T(8,128)(2,1)}), bf16[64,48,128]{2,1,0:T(8,128)(2,1)S(1)}, u32[]{:S(2)}, u32[]{:S(2)}) %all-to-all-start.2) | async-done | bytes 786464 | tf_op jit(solution)/shard_map/all_to_all | solution.py:401
  71.1 0.0 copy-done
  71.1 0.0 copy-done.1
  71.1 0.7 mix.1
  71.8 3.5 %collective-permute-start = (bf16[24,128]{1,0:T(8,128)(2,1)S(1)}, bf16[24,128]{1,0:T(8,128)(2,1)S(1)}, u32[]{:S(2)}, u32[]{:S(2)}) collective-permute-start(bf16[24,128]{1,0:T(8,128)(2,1)S(1)} %get-tuple-element.24), channel_id=1, source_target_pairs={{0,64},{64,0},{1,65},{65,1},{2,66},{66,2},{3,67},{67,3},{4,68},{68... | collective-permute-start | bytes 18440 | tf_op jit(solution)/shard_map/ppermute | solution.py:440
  75.4 0.8 %collective-permute-done = bf16[24,128]{1,0:T(8,128)(2,1)S(1)} collective-permute-done((bf16[24,128]{1,0:T(8,128)(2,1)S(1)}, bf16[24,128]{1,0:T(8,128)(2,1)S(1)}, u32[]{:S(2)}, u32[]{:S(2)}) %collective-permute-start) | collective-permute-done | bytes 6176 | tf_op jit(solution)/shard_map/ppermute | solution.py:440
  76.2 0.6 pad_maximum_fusion
  (3 shorter events, 0.0 us)
Async XLA Ops:
  0.0 38.5 %copy-start.2 = (bf16[6144]{0:T(1024)(128)(2,1)S(1)}, bf16[6144]{0:T(1024)(128)(2,1)}, u32[]{:S(2)}) copy-start(bf16[6144]{0:T(1024)(128)(2,1)} %param.22) | copy-start | bytes 36868
  2.8 22.8 %all-to-all-start = ((bf16[64,25,2,128]{3,2,1,0:T(2,128)(2,1)}), bf16[64,25,2,128]{3,2,1,0:T(2,128)(2,1)S(1)}, u32[]{:S(2)}, u32[]{:S(2)}) async-start(bf16[64,25,2,128]{3,2,1,0:T(2,128)(2,1)} %bitcast.3), calls=%async_computation | async-start | bytes 1638400 | tf_op jit(solution)/shard_map/all_to_all | solution.py:401
  27.3 18.6 %all-to-all-start.1 = ((bf16[64,48,128]{2,1,0:T(8,128)(2,1)}), bf16[64,48,128]{2,1,0:T(8,128)(2,1)S(1)}, u32[]{:S(2)}, u32[]{:S(2)}) async-start(bf16[64,48,128]{2,1,0:T(8,128)(2,1)} %get-tuple-element.18), calls=%async_computation.1 | async-start | bytes 1572864 | tf_op jit(solution)/shard_map/all_to_all | solution.py:401
  46.0 25.2 %copy-start = (s32[2,2]{1,0:T(2,128)S(1)}, s32[2,2]{1,0:T(2,128)}, u32[]{:S(2)}) copy-start(s32[2,2]{1,0:T(2,128)} %ids_ref.1) | copy-start | bytes 52
  46.0 25.2 %copy-start.1 = (f32[2,2]{1,0:T(2,128)S(1)}, f32[2,2]{1,0:T(2,128)}, u32[]{:S(2)}) copy-start(f32[2,2]{1,0:T(2,128)} %gates_ref.1) | copy-start | bytes 52
  53.7 17.4 %all-to-all-start.2 = ((bf16[64,48,128]{2,1,0:T(8,128)(2,1)}), bf16[64,48,128]{2,1,0:T(8,128)(2,1)S(1)}, u32[]{:S(2)}, u32[]{:S(2)}) async-start(bf16[64,48,128]{2,1,0:T(8,128)(2,1)} %get-tuple-element.21), calls=%async_computation.2 | async-start | bytes 1572864 | tf_op jit(solution)/shard_map/all_to_all | solution.py:401
  71.8 4.4 %collective-permute-start = (bf16[24,128]{1,0:T(8,128)(2,1)S(1)}, bf16[24,128]{1,0:T(8,128)(2,1)S(1)}, u32[]{:S(2)}, u32[]{:S(2)}) collective-permute-start(bf16[24,128]{1,0:T(8,128)(2,1)S(1)} %get-tuple-element.24), channel_id=1, source_target_pairs={{0,64},{64,0},{1,65},{65,1},{2,66},{66,2},{3,67},{67,3},{4,68},{68... | collective-permute-start | bytes 18440 | tf_op jit(solution)/shard_map/ppermute | solution.py:440

commit v9 on v7

--- a/solution.py
+++ b/solution.py
@@ -31,15 +31,8 @@
 epsilon = 1e-05
 
 
-def walk():
-    places = []
-    for step in range(DEVS):
-        x, y, z = (step * 43 % 64 // 16, step * 43 % 16 // 4, step * 43 % 4)
-        places.append((x + 2) % 4 * 16 + (y + 2) % 4 * 4 + (z + 2) % 4)
-    return places
-
-
-ORDER = walk()
+STRIDE, UNSTRIDE, FIRST = 3, 43, 42
+ORDER = [step * STRIDE % DEVS ^ FIRST for step in range(DEVS)]
 PLACE = [ORDER.index(chip) for chip in range(DEVS)]
 
 VMEM_BLOCK = pl.BlockSpec(memory_space=pltpu.VMEM)
@@ -137,9 +130,9 @@
 
 def attend(core, cached, query, new_key, new_value, residual, key_cache, value_cache):
     def whole(shape):
-        return pl.BlockSpec(shape, lambda step, core, cached: (0,) * len(shape))
-
-    cache = pl.BlockSpec((1, CACHE_LEN, 1024), lambda step, core, cached: (core[0], 0, 0))
+        return pl.BlockSpec(shape, lambda step, core: (0,) * len(shape))
+
+    cache = pl.BlockSpec((1, CACHE_LEN, 1024), lambda step, core: (core[0], 0, 0))
     return pl.pallas_call(
         attend_kernel,
         out_shape=(
@@ -147,9 +140,10 @@
             jax.ShapeDtypeStruct((8, 128), jnp.float32),
         ),
         grid_spec=pltpu.PrefetchScalarGridSpec(
-            num_scalar_prefetch=2,
+            num_scalar_prefetch=1,
             grid=(1,),
             in_specs=[
+                SMEM_BLOCK,
                 whole((2, D)),
                 whole((2, 1024)),
                 whole((2, 1024)),
@@ -262,7 +256,7 @@
 
 
 def expert_kernel(
-    place_ref,
+    chip_ref,
     hidden_ref,
     gain_ref,
     early_ref,
@@ -315,7 +309,7 @@
             gain = gain_ref[:, lanes].astype(jnp.float32)
             scaled[0:DEVS, lanes] = (turned[0:DEVS] * gain[0:1]).astype(jnp.bfloat16)
             scaled[DEVS:128, lanes] = (turned[DEVS:128] * gain[1:2]).astype(jnp.bfloat16)
-    place = place_ref[0]
+    place = lax.rem(jnp.bitwise_xor(chip_ref[0], FIRST) * UNSTRIDE, DEVS)
     own_ref[0:1, :] = flipped[pl.ds(place, 1), :]
     own_ref[1:2, :] = flipped[pl.ds(place + DEVS, 1), :]
     total = jnp.sum(squares, axis=1, keepdims=True)
@@ -365,7 +359,7 @@
         ].astype(jnp.bfloat16)
 
 
-def run_experts(place, hidden, gain, early, w_gate, w_up, w_down):
+def run_experts(chip, hidden, gain, early, w_gate, w_up, w_down):
     return pl.pallas_call(
         expert_kernel,
         out_shape=(
@@ -385,7 +379,7 @@
         ],
         compiler_params=pltpu.CompilerParams(vmem_limit_bytes=40 << 20),
         name="experts",
-    )(place, hidden, gain, *in_vmem(early), *in_hbm(w_gate, w_up, w_down))
+    )(chip, hidden, gain, *in_vmem(early), *in_hbm(w_gate, w_up, w_down))
 
 
 def mix_kernel(core_ref, ids_ref, gates_ref, returned_ref, hidden_ref, kept_ref, given_ref):
@@ -443,7 +437,6 @@
 ):
     core = lax.axis_index("side").astype(jnp.int32).reshape(1)
     chip = lax.axis_index("dev").astype(jnp.int32).reshape(1)
-    place = jnp.asarray(PLACE, jnp.int32)[chip]
     outgoing, mark = attend(
         core, cached, query, new_key, new_value, residual, key_cache, value_cache
     )
@@ -456,7 +449,7 @@
     w_up = w_up.reshape(DEVS, 2, HALF, UNITS)
     early = fetch_early(mark, w_gate)
     hidden = exchange(packed).reshape(HALF_D, 128)
-    partial_value, own_hidden = run_experts(place, hidden, gain, early, w_gate, w_up, w_down)
+    partial_value, own_hidden = run_experts(chip, hidden, gain, early, w_gate, w_up, w_down)
     returned = exchange(partial_value)
     own_hidden = own_hidden.reshape(2, DEVS, HALF).transpose(1, 0, 2).reshape(ROWS, 128)
     kept, given = mix(core, expert_ids, gate_weights, returned, own_hidden)

time: 78.4 us -> 76.6 us (0.977)
  Pallas kernels: 16.9 us -> 15.7 us
    ppermute x1, starting transfers between devices: 3.54 us -> 5.01 us  [local(): taken = lax.ppermute(given, 'side', [(0, 1), (1, 0)])]
    all_to_all x3, starting transfers between devices: 36.4 us -> 35.2 us  [exchange(): lax.all_to_all(parts, 'dev', split_axis=0, concat_axis=0, tiled=True, axi...]
where the time goes in v9:
time: 76.6 us; the launch traced here: 76.1 us
  starting transfers between devices  40.2 us (52%)
  waiting for transfers between devices  18.9 us (25%)
  Pallas kernels  15.7 us (20%)
    all_to_all x3, starting transfers between devices, exchange(): lax.all_to_all(parts, 'dev', split_axis=0, concat_axis=0, tiled=True, axi...  35.2 us
    all_to_all x3, waiting for transfers between devices, exchange(): lax.all_to_all(parts, 'dev', split_axis=0, concat_axis=0, tiled=True, axi...  18.1 us
    pallas_call x1, Pallas kernels, run_experts(): pl.pallas_call(expert_kernel, out_shape=(pltpu.HBM((DEVS, ROWS, 128), jnp...  7.75 us
    ppermute x1, starting transfers between devices, local(): taken = lax.ppermute(given, 'side', [(0, 1), (1, 0)])  5.01 us
    pallas_call x1, Pallas kernels, attend(): pl.pallas_call(attend_kernel, out_shape=(jax.ShapeDtypeStruct((DEVS * SEN...  2.65 us
    pallas_call x1, Pallas kernels, project(): pl.pallas_call(project_kernel, out_shape=(jax.ShapeDtypeStruct((DEVS, HAL...  1.69 us
    pallas_call x1, Pallas kernels, fetch_early(): pl.pallas_call(early_kernel, out_shape=pltpu.VMEM((EARLY, PART, HALF, UNI...  1.64 us
  transfers between devices with their start and end apart: 4, of which 4 were waited for; matrix products, arithmetic and copies ran while one was open for 1% of the time, Pallas kernels for 4%

profile of v9, /device:TPU:1, one launch (start us, length us, event | category | flops | bytes accessed | tf_op | source)
XLA Modules:
  0.0 76.1 jit_solution(1547981722297461758)
XLA Ops:
  0.0 0.0 copy-start.2
  0.0 2.6 %attend.1 = (bf16[3200,128]{1,0:T(8,128)(2,1)}, f32[8,128]{1,0:T(8,128)S(1)}) custom-call(s32[1]{0:T(128)} %bitcast.core_ref, s32[2]{0:T(128)} %cached_ref.1, bf16[2,6144]{1,0:T(2,128)(2,1)} %query_ref.1, bf16[2,1024]{1,0:T(2,128)(2,1)} %new_key_ref.1, bf16[2,1024]{1,0:T(2,128)(2,1)} %new_value_ref.1, bf16[2,6144]{1,0:T(2,128)(2,1)} %residual_ref.1, ...), custom_call_target="tpu_custom_call" | custom-call | tf_op jit(solution)/shard_map/attend/pallas_call | solution.py:136
  2.7 14.1 %all-to-all-start = ((bf16[64,25,2,128]{3,2,1,0:T(2,128)(2,1)}), bf16[64,25,2,128]{3,2,1,0:T(2,128)(2,1)S(1)}, u32[]{:S(2)}, u32[]{:S(2)}) async-start(bf16[64,25,2,128]{3,2,1,0:T(2,128)(2,1)} %bitcast.3), calls=%async_computation | async-start | bytes 1638400 | tf_op jit(solution)/shard_map/all_to_all | solution.py:417
  16.7 1.3 %fetch.1.weight_ref = bf16[96,6144]{1,0:T(8,128)(2,1)S(1)} custom-call(f32[8,128]{1,0:T(8,128)S(1)} %get-tuple-element.17.after_ref, bf16[96,6144]{1,0:T(8,128)(2,1)} %bitcast.26), custom_call_target="tpu_custom_call" | custom-call | bytes 2359296 | tf_op jit(solution)/shard_map/fetch/pallas_call | solution.py:180
  18.0 7.6 %all-to-all-done = bf16[64,25,2,128]{3,2,1,0:T(2,128)(2,1)S(1)} async-done(((bf16[64,25,2,128]{3,2,1,0:T(2,128)(2,1)}), bf16[64,25,2,128]{3,2,1,0:T(2,128)(2,1)S(1)}, u32[]{:S(2)}, u32[]{:S(2)}) %all-to-all-start) | async-done | bytes 819232 | tf_op jit(solution)/shard_map/all_to_all | solution.py:417
  25.6 1.7 %project.1 = (bf16[64,48,128]{2,1,0:T(8,128)(2,1)}, f32[8,128]{1,0:T(8,128)S(1)}) custom-call(s32[1]{0:T(128)} %bitcast.2.chip_ref, bf16[3200,128]{1,0:T(8,128)(2,1)S(1)} %bitcast.21, bf16[96,6144]{1,0:T(8,128)(2,1)S(1)} %fetch.1.weight_ref), custom_call_target="tpu_custom_call" | custom-call | tf_op jit(solution)/shard_map/project/pallas_call | solution.py:216
  27.3 10.4 %all-to-all-start.1 = ((bf16[64,48,128]{2,1,0:T(8,128)(2,1)}), bf16[64,48,128]{2,1,0:T(8,128)(2,1)S(1)}, u32[]{:S(2)}, u32[]{:S(2)}) async-start(bf16[64,48,128]{2,1,0:T(8,128)(2,1)} %get-tuple-element.18), calls=%async_computation.1 | async-start | bytes 1572864 | tf_op jit(solution)/shard_map/all_to_all | solution.py:417
  37.7 0.0 copy-done.2
  37.7 0.1 reshape.39
  37.8 0.1 reshape.40.gain_ref
  38.0 1.6 %fetch_early.1.early_ref = bf16[3,16,48,512]{3,2,1,0:T(8,128)(2,1)S(1)} custom-call(f32[8,128]{1,0:T(8,128)S(1)} %get-tuple-element.20.after_ref, bf16[64,2,48,512]{3,2,1,0:T(8,128)(2,1)} %bitcast.23), custom_call_target="tpu_custom_call" | custom-call | tf_op jit(solution)/shard_map/fetch_early/pallas_call | solution.py:247
  39.6 5.0 %all-to-all-done.1 = bf16[64,48,128]{2,1,0:T(8,128)(2,1)S(1)} async-done(((bf16[64,48,128]{2,1,0:T(8,128)(2,1)}), bf16[64,48,128]{2,1,0:T(8,128)(2,1)S(1)}, u32[]{:S(2)}, u32[]{:S(2)}) %all-to-all-start.1) | async-done | bytes 786464 | tf_op jit(solution)/shard_map/all_to_all | solution.py:417
  44.6 0.0 copy-start
  44.6 0.0 copy-start.1
  44.6 7.8 %experts.1 = (bf16[64,48,128]{2,1,0:T(8,128)(2,1)}, f32[2,3072]{1,0:T(2,128)S(1)}) custom-call(s32[1]{0:T(128)} %bitcast.2.chip_ref, bf16[3072,128]{1,0:T(8,128)(2,1)S(1)} %bitcast.22, bf16[2,3072]{1,0:T(2,128)(2,1)S(1)} %reshape.40.gain_ref, bf16[3,16,48,512]{3,2,1,0:T(8,128)(2,1)S(1)} %fetch_early.1.early_ref, bf16[64,2,48,512]{3,2,1,0:T(8,128)(2,1)} %bitcast.24, ...), custom_call_target="tpu_custom_call" | custom-call | tf_op jit(solution)/shard_map/experts/pallas_call | solution.py:363
  52.4 10.7 %all-to-all-start.2 = ((bf16[64,48,128]{2,1,0:T(8,128)(2,1)}), bf16[64,48,128]{2,1,0:T(8,128)(2,1)S(1)}, u32[]{:S(2)}, u32[]{:S(2)}) async-start(bf16[64,48,128]{2,1,0:T(8,128)(2,1)} %get-tuple-element.21), calls=%async_computation.2 | async-start | bytes 1572864 | tf_op jit(solution)/shard_map/all_to_all | solution.py:417
  63.1 0.1 reshape.43
  63.2 0.1 copy.17
  63.3 0.1 reshape.44.hidden_ref
  63.4 5.5 %all-to-all-done.2.returned_ref = bf16[64,48,128]{2,1,0:T(8,128)(2,1)S(1)} async-done(((bf16[64,48,128]{2,1,0:T(8,128)(2,1)}), bf16[64,48,128]{2,1,0:T(8,128)(2,1)S(1)}, u32[]{:S(2)}, u32[]{:S(2)}) %all-to-all-start.2) | async-done | bytes 786464 | tf_op jit(solution)/shard_map/all_to_all | solution.py:417
  68.9 0.0 copy-done
  68.9 0.0 copy-done.1
  68.9 0.7 mix.1
  69.6 5.0 %collective-permute-start = (bf16[24,128]{1,0:T(8,128)(2,1)S(1)}, bf16[24,128]{1,0:T(8,128)(2,1)S(1)}, u32[]{:S(2)}, u32[]{:S(2)}) collective-permute-start(bf16[24,128]{1,0:T(8,128)(2,1)S(1)} %get-tuple-element.24), channel_id=1, source_target_pairs={{0,64},{64,0},{1,65},{65,1},{2,66},{66,2},{3,67},{67,3},{4,68},{68... | collective-permute-start | bytes 18440 | tf_op jit(solution)/shard_map/ppermute | solution.py:456
  74.6 0.8 %collective-permute-done = bf16[24,128]{1,0:T(8,128)(2,1)S(1)} collective-permute-done((bf16[24,128]{1,0:T(8,128)(2,1)S(1)}, bf16[24,128]{1,0:T(8,128)(2,1)S(1)}, u32[]{:S(2)}, u32[]{:S(2)}) %collective-permute-start) | collective-permute-done | bytes 6176 | tf_op jit(solution)/shard_map/ppermute | solution.py:456
  75.5 0.6 pad_maximum_fusion
  (3 shorter events, 0.0 us)
Async XLA Ops:
  0.0 37.7 %copy-start.2 = (bf16[6144]{0:T(1024)(128)(2,1)S(1)}, bf16[6144]{0:T(1024)(128)(2,1)}, u32[]{:S(2)}) copy-start(bf16[6144]{0:T(1024)(128)(2,1)} %param.22) | copy-start | bytes 36868
  2.7 22.9 %all-to-all-start = ((bf16[64,25,2,128]{3,2,1,0:T(2,128)(2,1)}), bf16[64,25,2,128]{3,2,1,0:T(2,128)(2,1)S(1)}, u32[]{:S(2)}, u32[]{:S(2)}) async-start(bf16[64,25,2,128]{3,2,1,0:T(2,128)(2,1)} %bitcast.3), calls=%async_computation | async-start | bytes 1638400 | tf_op jit(solution)/shard_map/all_to_all | solution.py:417
  27.3 17.4 %all-to-all-start.1 = ((bf16[64,48,128]{2,1,0:T(8,128)(2,1)}), bf16[64,48,128]{2,1,0:T(8,128)(2,1)S(1)}, u32[]{:S(2)}, u32[]{:S(2)}) async-start(bf16[64,48,128]{2,1,0:T(8,128)(2,1)} %get-tuple-element.18), calls=%async_computation.1 | async-start | bytes 1572864 | tf_op jit(solution)/shard_map/all_to_all | solution.py:417
  44.6 24.3 %copy-start = (s32[2,2]{1,0:T(2,128)S(1)}, s32[2,2]{1,0:T(2,128)}, u32[]{:S(2)}) copy-start(s32[2,2]{1,0:T(2,128)} %ids_ref.1) | copy-start | bytes 52
  44.6 24.3 %copy-start.1 = (f32[2,2]{1,0:T(2,128)S(1)}, f32[2,2]{1,0:T(2,128)}, u32[]{:S(2)}) copy-start(f32[2,2]{1,0:T(2,128)} %gates_ref.1) | copy-start | bytes 52
  52.4 16.5 %all-to-all-start.2 = ((bf16[64,48,128]{2,1,0:T(8,128)(2,1)}), bf16[64,48,128]{2,1,0:T(8,128)(2,1)S(1)}, u32[]{:S(2)}, u32[]{:S(2)}) async-start(bf16[64,48,128]{2,1,0:T(8,128)(2,1)} %get-tuple-element.21), calls=%async_computation.2 | async-start | bytes 1572864 | tf_op jit(solution)/shard_map/all_to_all | solution.py:417
  69.6 5.8 %collective-permute-start = (bf16[24,128]{1,0:T(8,128)(2,1)S(1)}, bf16[24,128]{1,0:T(8,128)(2,1)S(1)}, u32[]{:S(2)}, u32[]{:S(2)}) collective-permute-start(bf16[24,128]{1,0:T(8,128)(2,1)S(1)} %get-tuple-element.24), channel_id=1, source_target_pairs={{0,64},{64,0},{1,65},{65,1},{2,66},{66,2},{3,67},{67,3},{4,68},{68... | collective-permute-start | bytes 18440 | tf_op jit(solution)/shard_map/ppermute | solution.py:456

commit v10 on v9

--- a/solution.py
+++ b/solution.py
@@ -31,9 +31,20 @@
 epsilon = 1e-05
 
 
-STRIDE, UNSTRIDE, FIRST = 3, 43, 42
-ORDER = [step * STRIDE % DEVS ^ FIRST for step in range(DEVS)]
+FIRST = 42
+STRIDE, UNSTRIDE = 3, 43
+HIDDEN_STRIDE, BACK_STRIDE = 13, 47
+
+
+def order_by(stride):
+    return [step * stride % DEVS ^ FIRST for step in range(DEVS)]
+
+
+ORDER = order_by(STRIDE)
 PLACE = [ORDER.index(chip) for chip in range(DEVS)]
+HIDDEN_ORDER = order_by(HIDDEN_STRIDE)
+HIDDEN_PLACE = [HIDDEN_ORDER.index(chip) for chip in range(DEVS)]
+BACK_ORDER = order_by(BACK_STRIDE)
 
 VMEM_BLOCK = pl.BlockSpec(memory_space=pltpu.VMEM)
 SMEM_BLOCK = pl.BlockSpec(memory_space=pltpu.SMEM)
@@ -153,8 +164,8 @@
             ],
             out_specs=(whole((DEVS * SENT, 128)), whole((8, 128))),
             scratch_shapes=[
-                pltpu.VMEM((128, 128), jnp.float32),
-                pltpu.VMEM((128, 128), jnp.float32),
+                pltpu.VMEM((192, 128), jnp.float32),
+                pltpu.VMEM((192, 128), jnp.float32),
                 pltpu.VMEM((ROWS + 8, 128), jnp.float32),
                 pltpu.VMEM((BATCH * SENT, 128), jnp.float32),
             ],
@@ -222,7 +233,7 @@
         in_specs=[SMEM_BLOCK, VMEM_BLOCK, VMEM_BLOCK],
         out_specs=(VMEM_BLOCK, VMEM_BLOCK),
         scratch_shapes=[
-            pltpu.VMEM((DEVS * SENT, 128), jnp.float32),
+            pltpu.VMEM((DEVS * SENT + 56, 128), jnp.float32),
             pltpu.VMEM((DEVS, D), jnp.bfloat16),
         ],
         compiler_params=pltpu.CompilerParams(vmem_limit_bytes=16 << 20),
@@ -296,7 +307,7 @@
     for block in range(HALF_D // 384):
         columns = jnp.concatenate(
             [
-                hidden_ref[PLACE[chip] * HALF : PLACE[chip] * HALF + HALF, :].astype(jnp.float32)
+                hidden_ref[HIDDEN_PLACE[chip] * HALF : HIDDEN_PLACE[chip] * HALF + HALF, :].astype(jnp.float32)
                 for chip in range(block * 8, block * 8 + 8)
             ],
             axis=0,
@@ -338,6 +349,7 @@
     up = up * factor
     act = (gate / (1.0 + jnp.exp(-gate)) * up).astype(jnp.bfloat16)
     span = DOWN // 128
+    token_rows = [PLACE[chip] * ROWS for chip in BACK_ORDER]
     for step in range(D // DOWN):
         copies[2, step].wait()
         block = jnp.dot(
@@ -349,13 +361,13 @@
             ]
         last = (step + 1) * span
         if last % 16 == 0 and last < ROWS:
-            for target in range(DEVS):
+            for target, first in enumerate(token_rows):
                 out_ref[target, last - 16 : last, :] = result[
-                    target * ROWS + last - 16 : target * ROWS + last, :
+                    first + last - 16 : first + last, :
                 ].astype(jnp.bfloat16)
-    for target in range(DEVS):
+    for target, first in enumerate(token_rows):
         out_ref[target, ROWS - 16 : ROWS, :] = result[
-            target * ROWS + ROWS - 16 : target * ROWS + ROWS, :
+            first + ROWS - 16 : first + ROWS, :
         ].astype(jnp.bfloat16)
 
 
@@ -374,7 +386,7 @@
             pltpu.VMEM((UNITS, D), jnp.bfloat16),
             pltpu.VMEM((128, HALF_D), jnp.float32),
             pltpu.VMEM((128, HALF_D), jnp.bfloat16),
-            pltpu.VMEM((DEVS * ROWS, 128), jnp.float32),
+            pltpu.VMEM((DEVS * ROWS + ROWS, 128), jnp.float32),
             pltpu.SemaphoreType.DMA((3, 2 * STEPS)),
         ],
         compiler_params=pltpu.CompilerParams(vmem_limit_bytes=40 << 20),
@@ -393,7 +405,7 @@
             )
         block = jnp.zeros((ROWS, 128), jnp.float32)
         for place in range(DEVS):
-            if ORDER[place] // (DEVS // EXPERTS) == expert:
+            if BACK_ORDER[place] // (DEVS // EXPERTS) == expert:
                 block = block + returned_ref[place].astype(jnp.float32)
         total = total + block * share
     lower, upper = total[0 : ROWS // 2], total[ROWS // 2 : ROWS]
@@ -413,9 +425,9 @@
     )(core, expert_ids, gate_weights, returned, hidden)
 
 
-def exchange(parts):
+def exchange(parts, order):
     return lax.all_to_all(
-        parts, "dev", split_axis=0, concat_axis=0, tiled=True, axis_index_groups=[ORDER]
+        parts, "dev", split_axis=0, concat_axis=0, tiled=True, axis_index_groups=[order]
     )
 
 
@@ -443,14 +455,14 @@
     norm_gain, mark = lax.optimization_barrier((norm_gain, mark))
     gain = norm_gain.reshape(DEVS, 2, HALF).transpose(1, 0, 2).reshape(2, HALF_D)
     (projection,) = fetch(mark, out_weight.T)
-    arrived = exchange(outgoing.reshape(DEVS, SENT // 2, 2, 128)).reshape(DEVS * SENT, 128)
+    arrived = exchange(outgoing.reshape(DEVS, SENT // 2, 2, 128), ORDER).reshape(DEVS * SENT, 128)
     packed, mark = project(chip, arrived, projection)
     w_gate = w_gate.reshape(DEVS, 2, HALF, UNITS)
     w_up = w_up.reshape(DEVS, 2, HALF, UNITS)
     early = fetch_early(mark, w_gate)
-    hidden = exchange(packed).reshape(HALF_D, 128)
+    hidden = exchange(packed, HIDDEN_ORDER).reshape(HALF_D, 128)
     partial_value, own_hidden = run_experts(chip, hidden, gain, early, w_gate, w_up, w_down)
-    returned = exchange(partial_value)
+    returned = exchange(partial_value, BACK_ORDER)
     own_hidden = own_hidden.reshape(2, DEVS, HALF).transpose(1, 0, 2).reshape(ROWS, 128)
     kept, given = mix(core, expert_ids, gate_weights, returned, own_hidden)
     taken = lax.ppermute(given, "side", [(0, 1), (1, 0)])

time: 76.6 us -> 75.9 us (level)
  starting transfers between devices: 40.2 us -> 38.9 us
    ppermute x1, starting transfers between devices: 5.01 us -> 3.49 us  [local(): taken = lax.ppermute(given, 'side', [(0, 1), (1, 0)])]
where the time goes in v10:
time: 75.9 us; the launch traced here: 75.4 us
  starting transfers between devices  38.9 us (51%)
  waiting for transfers between devices  19.5 us (26%)
  Pallas kernels  15.7 us (21%)
    all_to_all x3, starting transfers between devices, exchange(): lax.all_to_all(parts, 'dev', split_axis=0, concat_axis=0, tiled=True, axi...  35.5 us
    all_to_all x3, waiting for transfers between devices, exchange(): lax.all_to_all(parts, 'dev', split_axis=0, concat_axis=0, tiled=True, axi...  18.7 us
    pallas_call x1, Pallas kernels, run_experts(): pl.pallas_call(expert_kernel, out_shape=(pltpu.HBM((DEVS, ROWS, 128), jnp...  7.76 us
    ppermute x1, starting transfers between devices, local(): taken = lax.ppermute(given, 'side', [(0, 1), (1, 0)])  3.49 us
    pallas_call x1, Pallas kernels, attend(): pl.pallas_call(attend_kernel, out_shape=(jax.ShapeDtypeStruct((DEVS * SEN...  2.65 us
    pallas_call x1, Pallas kernels, project(): pl.pallas_call(project_kernel, out_shape=(jax.ShapeDtypeStruct((DEVS, HAL...  1.71 us
    pallas_call x1, Pallas kernels, fetch_early(): pl.pallas_call(early_kernel, out_shape=pltpu.VMEM((EARLY, PART, HALF, UNI...  1.64 us
  transfers between devices with their start and end apart: 4, of which 4 were waited for; matrix products, arithmetic and copies ran while one was open for 1% of the time, Pallas kernels for 4%

profile of v10, /device:TPU:1, one launch (start us, length us, event | category | flops | bytes accessed | tf_op | source)
XLA Modules:
  0.0 75.4 jit_solution(1188396199435076082)
XLA Ops:
  0.0 0.0 copy-start.2
  0.0 2.7 %attend.1 = (bf16[3200,128]{1,0:T(8,128)(2,1)}, f32[8,128]{1,0:T(8,128)S(1)}) custom-call(s32[1]{0:T(128)} %bitcast.core_ref, s32[2]{0:T(128)} %cached_ref.1, bf16[2,6144]{1,0:T(2,128)(2,1)} %query_ref.1, bf16[2,1024]{1,0:T(2,128)(2,1)} %new_key_ref.1, bf16[2,1024]{1,0:T(2,128)(2,1)} %new_value_ref.1, bf16[2,6144]{1,0:T(2,128)(2,1)} %residual_ref.1, ...), custom_call_target="tpu_custom_call" | custom-call | tf_op jit(solution)/shard_map/attend/pallas_call | solution.py:147
  2.7 14.1 %all-to-all-start = ((bf16[64,25,2,128]{3,2,1,0:T(2,128)(2,1)}), bf16[64,25,2,128]{3,2,1,0:T(2,128)(2,1)S(1)}, u32[]{:S(2)}, u32[]{:S(2)}) async-start(bf16[64,25,2,128]{3,2,1,0:T(2,128)(2,1)} %bitcast.3), calls=%async_computation | async-start | bytes 1638400 | tf_op jit(solution)/shard_map/all_to_all | solution.py:429
  16.7 1.3 %fetch.1.weight_ref = bf16[96,6144]{1,0:T(8,128)(2,1)S(1)} custom-call(f32[8,128]{1,0:T(8,128)S(1)} %get-tuple-element.17.after_ref, bf16[96,6144]{1,0:T(8,128)(2,1)} %bitcast.26), custom_call_target="tpu_custom_call" | custom-call | bytes 2359296 | tf_op jit(solution)/shard_map/fetch/pallas_call | solution.py:191
  18.0 7.6 %all-to-all-done = bf16[64,25,2,128]{3,2,1,0:T(2,128)(2,1)S(1)} async-done(((bf16[64,25,2,128]{3,2,1,0:T(2,128)(2,1)}), bf16[64,25,2,128]{3,2,1,0:T(2,128)(2,1)S(1)}, u32[]{:S(2)}, u32[]{:S(2)}) %all-to-all-start) | async-done | bytes 819232 | tf_op jit(solution)/shard_map/all_to_all | solution.py:429
  25.6 1.7 %project.1 = (bf16[64,48,128]{2,1,0:T(8,128)(2,1)}, f32[8,128]{1,0:T(8,128)S(1)}) custom-call(s32[1]{0:T(128)} %bitcast.2.chip_ref, bf16[3200,128]{1,0:T(8,128)(2,1)S(1)} %bitcast.21, bf16[96,6144]{1,0:T(8,128)(2,1)S(1)} %fetch.1.weight_ref), custom_call_target="tpu_custom_call" | custom-call | tf_op jit(solution)/shard_map/project/pallas_call | solution.py:227
  27.3 10.4 %all-to-all-start.1 = ((bf16[64,48,128]{2,1,0:T(8,128)(2,1)}), bf16[64,48,128]{2,1,0:T(8,128)(2,1)S(1)}, u32[]{:S(2)}, u32[]{:S(2)}) async-start(bf16[64,48,128]{2,1,0:T(8,128)(2,1)} %get-tuple-element.18), calls=%async_computation.1 | async-start | bytes 1572864 | tf_op jit(solution)/shard_map/all_to_all | solution.py:429
  37.7 0.0 copy-done.2
  37.7 0.1 reshape.39
  37.9 0.1 reshape.40.gain_ref
  38.0 1.6 %fetch_early.1.early_ref = bf16[3,16,48,512]{3,2,1,0:T(8,128)(2,1)S(1)} custom-call(f32[8,128]{1,0:T(8,128)S(1)} %get-tuple-element.20.after_ref, bf16[64,2,48,512]{3,2,1,0:T(8,128)(2,1)} %bitcast.23), custom_call_target="tpu_custom_call" | custom-call | tf_op jit(solution)/shard_map/fetch_early/pallas_call | solution.py:258
  39.6 4.8 %all-to-all-done.1 = bf16[64,48,128]{2,1,0:T(8,128)(2,1)S(1)} async-done(((bf16[64,48,128]{2,1,0:T(8,128)(2,1)}), bf16[64,48,128]{2,1,0:T(8,128)(2,1)S(1)}, u32[]{:S(2)}, u32[]{:S(2)}) %all-to-all-start.1) | async-done | bytes 786464 | tf_op jit(solution)/shard_map/all_to_all | solution.py:429
  44.4 0.0 copy-start
  44.4 0.0 copy-start.1
  44.4 7.8 %experts.1 = (bf16[64,48,128]{2,1,0:T(8,128)(2,1)}, f32[2,3072]{1,0:T(2,128)S(1)}) custom-call(s32[1]{0:T(128)} %bitcast.2.chip_ref, bf16[3072,128]{1,0:T(8,128)(2,1)S(1)} %bitcast.22, bf16[2,3072]{1,0:T(2,128)(2,1)S(1)} %reshape.40.gain_ref, bf16[3,16,48,512]{3,2,1,0:T(8,128)(2,1)S(1)} %fetch_early.1.early_ref, bf16[64,2,48,512]{3,2,1,0:T(8,128)(2,1)} %bitcast.24, ...), custom_call_target="tpu_custom_call" | custom-call | tf_op jit(solution)/shard_map/experts/pallas_call | solution.py:375
  52.2 11.0 %all-to-all-start.2 = ((bf16[64,48,128]{2,1,0:T(8,128)(2,1)}), bf16[64,48,128]{2,1,0:T(8,128)(2,1)S(1)}, u32[]{:S(2)}, u32[]{:S(2)}) async-start(bf16[64,48,128]{2,1,0:T(8,128)(2,1)} %get-tuple-element.21), calls=%async_computation.2 | async-start | bytes 1572864 | tf_op jit(solution)/shard_map/all_to_all | solution.py:429
  63.2 0.1 reshape.43
  63.3 0.1 copy.17
  63.3 0.1 reshape.44.hidden_ref
  63.5 6.3 %all-to-all-done.2.returned_ref = bf16[64,48,128]{2,1,0:T(8,128)(2,1)S(1)} async-done(((bf16[64,48,128]{2,1,0:T(8,128)(2,1)}), bf16[64,48,128]{2,1,0:T(8,128)(2,1)S(1)}, u32[]{:S(2)}, u32[]{:S(2)}) %all-to-all-start.2) | async-done | bytes 786464 | tf_op jit(solution)/shard_map/all_to_all | solution.py:429
  69.8 0.0 copy-done
  69.8 0.0 copy-done.1
  69.8 0.7 mix.1
  70.5 3.5 %collective-permute-start = (bf16[24,128]{1,0:T(8,128)(2,1)S(1)}, bf16[24,128]{1,0:T(8,128)(2,1)S(1)}, u32[]{:S(2)}, u32[]{:S(2)}) collective-permute-start(bf16[24,128]{1,0:T(8,128)(2,1)S(1)} %get-tuple-element.24), channel_id=1, source_target_pairs={{0,64},{64,0},{1,65},{65,1},{2,66},{66,2},{3,67},{67,3},{4,68},{68... | collective-permute-start | bytes 18440 | tf_op jit(solution)/shard_map/ppermute | solution.py:468
  73.9 0.8 %collective-permute-done = bf16[24,128]{1,0:T(8,128)(2,1)S(1)} collective-permute-done((bf16[24,128]{1,0:T(8,128)(2,1)S(1)}, bf16[24,128]{1,0:T(8,128)(2,1)S(1)}, u32[]{:S(2)}, u32[]{:S(2)}) %collective-permute-start) | collective-permute-done | bytes 6176 | tf_op jit(solution)/shard_map/ppermute | solution.py:468
  74.8 0.6 pad_maximum_fusion
  (3 shorter events, 0.0 us)
Async XLA Ops:
  0.0 37.7 %copy-start.2 = (bf16[6144]{0:T(1024)(128)(2,1)S(1)}, bf16[6144]{0:T(1024)(128)(2,1)}, u32[]{:S(2)}) copy-start(bf16[6144]{0:T(1024)(128)(2,1)} %param.22) | copy-start | bytes 36868
  2.7 22.9 %all-to-all-start = ((bf16[64,25,2,128]{3,2,1,0:T(2,128)(2,1)}), bf16[64,25,2,128]{3,2,1,0:T(2,128)(2,1)S(1)}, u32[]{:S(2)}, u32[]{:S(2)}) async-start(bf16[64,25,2,128]{3,2,1,0:T(2,128)(2,1)} %bitcast.3), calls=%async_computation | async-start | bytes 1638400 | tf_op jit(solution)/shard_map/all_to_all | solution.py:429
  27.3 17.1 %all-to-all-start.1 = ((bf16[64,48,128]{2,1,0:T(8,128)(2,1)}), bf16[64,48,128]{2,1,0:T(8,128)(2,1)S(1)}, u32[]{:S(2)}, u32[]{:S(2)}) async-start(bf16[64,48,128]{2,1,0:T(8,128)(2,1)} %get-tuple-element.18), calls=%async_computation.1 | async-start | bytes 1572864 | tf_op jit(solution)/shard_map/all_to_all | solution.py:429
  44.4 25.3 %copy-start = (s32[2,2]{1,0:T(2,128)S(1)}, s32[2,2]{1,0:T(2,128)}, u32[]{:S(2)}) copy-start(s32[2,2]{1,0:T(2,128)} %ids_ref.1) | copy-start | bytes 52
  44.4 25.3 %copy-start.1 = (f32[2,2]{1,0:T(2,128)S(1)}, f32[2,2]{1,0:T(2,128)}, u32[]{:S(2)}) copy-start(f32[2,2]{1,0:T(2,128)} %gates_ref.1) | copy-start | bytes 52
  52.2 17.6 %all-to-all-start.2 = ((bf16[64,48,128]{2,1,0:T(8,128)(2,1)}), bf16[64,48,128]{2,1,0:T(8,128)(2,1)S(1)}, u32[]{:S(2)}, u32[]{:S(2)}) async-start(bf16[64,48,128]{2,1,0:T(8,128)(2,1)} %get-tuple-element.21), calls=%async_computation.2 | async-start | bytes 1572864 | tf_op jit(solution)/shard_map/all_to_all | solution.py:429
  70.5 4.3 %collective-permute-start = (bf16[24,128]{1,0:T(8,128)(2,1)S(1)}, bf16[24,128]{1,0:T(8,128)(2,1)S(1)}, u32[]{:S(2)}, u32[]{:S(2)}) collective-permute-start(bf16[24,128]{1,0:T(8,128)(2,1)S(1)} %get-tuple-element.24), channel_id=1, source_target_pairs={{0,64},{64,0},{1,65},{65,1},{2,66},{66,2},{3,67},{67,3},{4,68},{68... | collective-permute-start | bytes 18440 | tf_op jit(solution)/shard_map/ppermute | solution.py:468

commit v11 on v10

--- a/solution.py
+++ b/solution.py
@@ -200,15 +200,22 @@
     )(after, *in_hbm(*arrays))
 
 
-def project_kernel(chip_ref, arrived_ref, weight_ref, out_ref, mark_ref, rows, context):
+def project_kernel(chip_ref, arrived_ref, weight_ref, out_ref, mark_ref, rows):
     for source in range(0, DEVS * SENT, 400):
         rows[source : source + 400, :] = arrived_ref[source : source + 400, :].astype(jnp.float32)
-    for head in range(HEADS):
-        context[:, head * 128 : head * 128 + 128] = rows[pl.ds(head, DEVS, stride=SENT), :].astype(
-            jnp.bfloat16
-        )
-    tokens = context[...]
-    projected = last_dims(weight_ref[...], jnp.concatenate([tokens, tokens], axis=0))
+    projected = jnp.zeros((COLS, 128), jnp.float32)
+    for group in range(0, HEADS, 8):
+        tokens = jnp.concatenate(
+            [
+                rows[pl.ds(head, DEVS, stride=SENT), :].astype(jnp.bfloat16)
+                for head in range(group, group + 8)
+            ],
+            axis=1,
+        )
+        projected = projected + last_dims(
+            weight_ref[:, group * 128 : (group + 8) * 128],
+            jnp.concatenate([tokens, tokens], axis=0),
+        )
     flipped = []
     for row in (ROWS, ROWS + 1):
         part = rows[pl.ds(row, DEVS, stride=SENT), :]
@@ -234,7 +241,6 @@
         out_specs=(VMEM_BLOCK, VMEM_BLOCK),
         scratch_shapes=[
             pltpu.VMEM((DEVS * SENT + 56, 128), jnp.float32),
-            pltpu.VMEM((DEVS, D), jnp.bfloat16),
         ],
         compiler_params=pltpu.CompilerParams(vmem_limit_bytes=16 << 20),
         name="project",

time: 75.9 us -> 75.8 us (level)
  no operation moved by 1% of the time
where the time goes in v11:
time: 75.8 us; the launch traced here: 75.4 us
  starting transfers between devices  38.9 us (51%)
  waiting for transfers between devices  19.5 us (26%)
  Pallas kernels  15.6 us (21%)
    all_to_all x3, starting transfers between devices, exchange(): lax.all_to_all(parts, 'dev', split_axis=0, concat_axis=0, tiled=True, axi...  35.5 us
    all_to_all x3, waiting for transfers between devices, exchange(): lax.all_to_all(parts, 'dev', split_axis=0, concat_axis=0, tiled=True, axi...  18.7 us
    pallas_call x1, Pallas kernels, run_experts(): pl.pallas_call(expert_kernel, out_shape=(pltpu.HBM((DEVS, ROWS, 128), jnp...  7.76 us
    ppermute x1, starting transfers between devices, local(): taken = lax.ppermute(given, 'side', [(0, 1), (1, 0)])  3.48 us
    pallas_call x1, Pallas kernels, attend(): pl.pallas_call(attend_kernel, out_shape=(jax.ShapeDtypeStruct((DEVS * SEN...  2.65 us
    pallas_call x1, Pallas kernels, fetch_early(): pl.pallas_call(early_kernel, out_shape=pltpu.VMEM((EARLY, PART, HALF, UNI...  1.64 us
    pallas_call x1, Pallas kernels, project(): pl.pallas_call(project_kernel, out_shape=(jax.ShapeDtypeStruct((DEVS, HAL...  1.62 us
  transfers between devices with their start and end apart: 4, of which 4 were waited for; matrix products, arithmetic and copies ran while one was open for 1% of the time, Pallas kernels for 4%

profile of v11, /device:TPU:1, one launch (start us, length us, event | category | flops | bytes accessed | tf_op | source)
XLA Modules:
  0.0 75.4 jit_solution(8923526432385090663)
XLA Ops:
  0.0 0.0 copy-start.2
  0.0 2.7 %attend.1 = (bf16[3200,128]{1,0:T(8,128)(2,1)}, f32[8,128]{1,0:T(8,128)S(1)}) custom-call(s32[1]{0:T(128)} %bitcast.core_ref, s32[2]{0:T(128)} %cached_ref.1, bf16[2,6144]{1,0:T(2,128)(2,1)} %query_ref.1, bf16[2,1024]{1,0:T(2,128)(2,1)} %new_key_ref.1, bf16[2,1024]{1,0:T(2,128)(2,1)} %new_value_ref.1, bf16[2,6144]{1,0:T(2,128)(2,1)} %residual_ref.1, ...), custom_call_target="tpu_custom_call" | custom-call | tf_op jit(solution)/shard_map/attend/pallas_call | solution.py:147
  2.7 14.1 %all-to-all-start = ((bf16[64,25,2,128]{3,2,1,0:T(2,128)(2,1)}), bf16[64,25,2,128]{3,2,1,0:T(2,128)(2,1)S(1)}, u32[]{:S(2)}, u32[]{:S(2)}) async-start(bf16[64,25,2,128]{3,2,1,0:T(2,128)(2,1)} %bitcast.3), calls=%async_computation | async-start | bytes 1638400 | tf_op jit(solution)/shard_map/all_to_all | solution.py:435
  16.7 1.3 %fetch.1.weight_ref = bf16[96,6144]{1,0:T(8,128)(2,1)S(1)} custom-call(f32[8,128]{1,0:T(8,128)S(1)} %get-tuple-element.17.after_ref, bf16[96,6144]{1,0:T(8,128)(2,1)} %bitcast.26), custom_call_target="tpu_custom_call" | custom-call | bytes 2359296 | tf_op jit(solution)/shard_map/fetch/pallas_call | solution.py:191
  18.0 7.6 %all-to-all-done = bf16[64,25,2,128]{3,2,1,0:T(2,128)(2,1)S(1)} async-done(((bf16[64,25,2,128]{3,2,1,0:T(2,128)(2,1)}), bf16[64,25,2,128]{3,2,1,0:T(2,128)(2,1)S(1)}, u32[]{:S(2)}, u32[]{:S(2)}) %all-to-all-start) | async-done | bytes 819232 | tf_op jit(solution)/shard_map/all_to_all | solution.py:435
  25.6 1.6 %project.1 = (bf16[64,48,128]{2,1,0:T(8,128)(2,1)}, f32[8,128]{1,0:T(8,128)S(1)}) custom-call(s32[1]{0:T(128)} %bitcast.2.chip_ref, bf16[3200,128]{1,0:T(8,128)(2,1)S(1)} %bitcast.21, bf16[96,6144]{1,0:T(8,128)(2,1)S(1)} %fetch.1.weight_ref), custom_call_target="tpu_custom_call" | custom-call | tf_op jit(solution)/shard_map/project/pallas_call | solution.py:234
  27.2 10.4 %all-to-all-start.1 = ((bf16[64,48,128]{2,1,0:T(8,128)(2,1)}), bf16[64,48,128]{2,1,0:T(8,128)(2,1)S(1)}, u32[]{:S(2)}, u32[]{:S(2)}) async-start(bf16[64,48,128]{2,1,0:T(8,128)(2,1)} %get-tuple-element.18), calls=%async_computation.1 | async-start | bytes 1572864 | tf_op jit(solution)/shard_map/all_to_all | solution.py:435
  37.6 0.0 copy-done.2
  37.7 0.1 reshape.39
  37.8 0.1 reshape.40.gain_ref
  37.9 1.6 %fetch_early.1.early_ref = bf16[3,16,48,512]{3,2,1,0:T(8,128)(2,1)S(1)} custom-call(f32[8,128]{1,0:T(8,128)S(1)} %get-tuple-element.20.after_ref, bf16[64,2,48,512]{3,2,1,0:T(8,128)(2,1)} %bitcast.23), custom_call_target="tpu_custom_call" | custom-call | tf_op jit(solution)/shard_map/fetch_early/pallas_call | solution.py:264
  39.5 4.8 %all-to-all-done.1 = bf16[64,48,128]{2,1,0:T(8,128)(2,1)S(1)} async-done(((bf16[64,48,128]{2,1,0:T(8,128)(2,1)}), bf16[64,48,128]{2,1,0:T(8,128)(2,1)S(1)}, u32[]{:S(2)}, u32[]{:S(2)}) %all-to-all-start.1) | async-done | bytes 786464 | tf_op jit(solution)/shard_map/all_to_all | solution.py:435
  44.3 0.0 copy-start
  44.3 0.0 copy-start.1
  44.3 7.8 %experts.1 = (bf16[64,48,128]{2,1,0:T(8,128)(2,1)}, f32[2,3072]{1,0:T(2,128)S(1)}) custom-call(s32[1]{0:T(128)} %bitcast.2.chip_ref, bf16[3072,128]{1,0:T(8,128)(2,1)S(1)} %bitcast.22, bf16[2,3072]{1,0:T(2,128)(2,1)S(1)} %reshape.40.gain_ref, bf16[3,16,48,512]{3,2,1,0:T(8,128)(2,1)S(1)} %fetch_early.1.early_ref, bf16[64,2,48,512]{3,2,1,0:T(8,128)(2,1)} %bitcast.24, ...), custom_call_target="tpu_custom_call" | custom-call | tf_op jit(solution)/shard_map/experts/pallas_call | solution.py:381
  52.1 11.0 %all-to-all-start.2 = ((bf16[64,48,128]{2,1,0:T(8,128)(2,1)}), bf16[64,48,128]{2,1,0:T(8,128)(2,1)S(1)}, u32[]{:S(2)}, u32[]{:S(2)}) async-start(bf16[64,48,128]{2,1,0:T(8,128)(2,1)} %get-tuple-element.21), calls=%async_computation.2 | async-start | bytes 1572864 | tf_op jit(solution)/shard_map/all_to_all | solution.py:435
  63.1 0.1 reshape.43
  63.2 0.1 copy.17
  63.3 0.1 reshape.44.hidden_ref
  63.4 6.3 %all-to-all-done.2.returned_ref = bf16[64,48,128]{2,1,0:T(8,128)(2,1)S(1)} async-done(((bf16[64,48,128]{2,1,0:T(8,128)(2,1)}), bf16[64,48,128]{2,1,0:T(8,128)(2,1)S(1)}, u32[]{:S(2)}, u32[]{:S(2)}) %all-to-all-start.2) | async-done | bytes 786464 | tf_op jit(solution)/shard_map/all_to_all | solution.py:435
  69.7 0.0 copy-done
  69.7 0.0 copy-done.1
  69.7 0.7 mix.1
  70.4 3.5 %collective-permute-start = (bf16[24,128]{1,0:T(8,128)(2,1)S(1)}, bf16[24,128]{1,0:T(8,128)(2,1)S(1)}, u32[]{:S(2)}, u32[]{:S(2)}) collective-permute-start(bf16[24,128]{1,0:T(8,128)(2,1)S(1)} %get-tuple-element.24), channel_id=1, source_target_pairs={{0,64},{64,0},{1,65},{65,1},{2,66},{66,2},{3,67},{67,3},{4,68},{68... | collective-permute-start | bytes 18440 | tf_op jit(solution)/shard_map/ppermute | solution.py:474
  73.9 0.8 %collective-permute-done = bf16[24,128]{1,0:T(8,128)(2,1)S(1)} collective-permute-done((bf16[24,128]{1,0:T(8,128)(2,1)S(1)}, bf16[24,128]{1,0:T(8,128)(2,1)S(1)}, u32[]{:S(2)}, u32[]{:S(2)}) %collective-permute-start) | collective-permute-done | bytes 6176 | tf_op jit(solution)/shard_map/ppermute | solution.py:474
  74.7 0.6 pad_maximum_fusion
  (3 shorter events, 0.0 us)
Async XLA Ops:
  0.0 37.7 %copy-start.2 = (bf16[6144]{0:T(1024)(128)(2,1)S(1)}, bf16[6144]{0:T(1024)(128)(2,1)}, u32[]{:S(2)}) copy-start(bf16[6144]{0:T(1024)(128)(2,1)} %param.22) | copy-start | bytes 36868
  2.7 22.9 %all-to-all-start = ((bf16[64,25,2,128]{3,2,1,0:T(2,128)(2,1)}), bf16[64,25,2,128]{3,2,1,0:T(2,128)(2,1)S(1)}, u32[]{:S(2)}, u32[]{:S(2)}) async-start(bf16[64,25,2,128]{3,2,1,0:T(2,128)(2,1)} %bitcast.3), calls=%async_computation | async-start | bytes 1638400 | tf_op jit(solution)/shard_map/all_to_all | solution.py:435
  27.2 17.1 %all-to-all-start.1 = ((bf16[64,48,128]{2,1,0:T(8,128)(2,1)}), bf16[64,48,128]{2,1,0:T(8,128)(2,1)S(1)}, u32[]{:S(2)}, u32[]{:S(2)}) async-start(bf16[64,48,128]{2,1,0:T(8,128)(2,1)} %get-tuple-element.18), calls=%async_computation.1 | async-start | bytes 1572864 | tf_op jit(solution)/shard_map/all_to_all | solution.py:435
  44.3 25.4 %copy-start = (s32[2,2]{1,0:T(2,128)S(1)}, s32[2,2]{1,0:T(2,128)}, u32[]{:S(2)}) copy-start(s32[2,2]{1,0:T(2,128)} %ids_ref.1) | copy-start | bytes 52
  44.3 25.4 %copy-start.1 = (f32[2,2]{1,0:T(2,128)S(1)}, f32[2,2]{1,0:T(2,128)}, u32[]{:S(2)}) copy-start(f32[2,2]{1,0:T(2,128)} %gates_ref.1) | copy-start | bytes 52
  52.1 17.6 %all-to-all-start.2 = ((bf16[64,48,128]{2,1,0:T(8,128)(2,1)}), bf16[64,48,128]{2,1,0:T(8,128)(2,1)S(1)}, u32[]{:S(2)}, u32[]{:S(2)}) async-start(bf16[64,48,128]{2,1,0:T(8,128)(2,1)} %get-tuple-element.21), calls=%async_computation.2 | async-start | bytes 1572864 | tf_op jit(solution)/shard_map/all_to_all | solution.py:435
  70.4 4.3 %collective-permute-start = (bf16[24,128]{1,0:T(8,128)(2,1)S(1)}, bf16[24,128]{1,0:T(8,128)(2,1)S(1)}, u32[]{:S(2)}, u32[]{:S(2)}) collective-permute-start(bf16[24,128]{1,0:T(8,128)(2,1)S(1)} %get-tuple-element.24), channel_id=1, source_target_pairs={{0,64},{64,0},{1,65},{65,1},{2,66},{66,2},{3,67},{67,3},{4,68},{68... | collective-permute-start | bytes 18440 | tf_op jit(solution)/shard_map/ppermute | solution.py:474
